TPU v7x, 512 devices: a whole 4x4x16 slice. The times are simulated.
512 devices in a mesh: sect: 2 (over core), exp: 64 (over y, z), lat: 4 (over x).
Axes of the slice: x: 4, y: 4, z: 16, core: 2. Of those that a mesh axis runs over, the one named last changes fastest.
Arguments:
- residuals: bfloat16 [16384, 4608], P(('sect', 'exp'), 'lat'), may hold values from -6 to 6
- routes: int32 [16384], P(('sect', 'exp')), may hold values from 0 to 3, as said below
- blocks: int32 [16384, 4], P(('sect', 'exp')), may hold values from 0 to 63, as said below
- enc_weight: bfloat16 [256, 128, 4608], P(('sect', 'exp'), None, 'lat'), may hold values from -0.09375 to 0.09375
- enc_bias: float32 [256, 128], P(('sect', 'exp')), may hold values from -3 to 3
- dec_weight: bfloat16 [256, 128, 4608], P(('sect', 'exp'), None, 'lat'), may hold values from -0.25 to 0.25
- dec_bias: float32 [4608], P('lat'), may hold values from -3 to 3
Outputs:
- reconstruction: bfloat16 [16384, 4608], P(('sect', 'exp'), 'lat')
- enc_grad: bfloat16 [256, 128, 4608], P(('sect', 'exp'), None, 'lat')
- enc_bias_grad: float32 [256, 128], P(('sect', 'exp'))
- dec_grad: bfloat16 [256, 128, 4608], P(('sect', 'exp'), None, 'lat')
Inputs may be any that keep to these rules, and one draw needn't show every extreme that they name: `routes`: half of the tokens of each index of sect and exp route to one expert of that index; the rest route to the other experts. A token's 4 blocks are distinct. Among the 128 tokens of one index of sect and exp, no global block is named by more than 4 of them, and every block of that index's busiest expert is named by exactly 4.
All inputs are finite; a program needn't handle non-finite values.
Results may differ from a plain program's by a relative error of at most 0.023.
Values may be sent and summed in bfloat16 or wider, within the bound.
No kernel may reach another device: no remote copies, remote signals or barrier semaphores. Data moves between devices by JAX's collectives and lax.ppermute only.
A program may use at most 64 MiB of HBM per device.

v0:
```python
import jax
import jax.numpy as jnp
from jax import lax
from jax.sharding import PartitionSpec as P

BLOCKS = 64


L1_COEF = 0.2


def send_rows(outgoing, filled):
    return (
        lax.all_to_all(outgoing, ("sect", "exp"), split_axis=0, concat_axis=0, tiled=True),
        lax.all_to_all(filled, ("sect", "exp"), split_axis=0, concat_axis=0, tiled=True),
    )


def send_partials(partial_value):
    return lax.all_to_all(partial_value, ("sect", "exp"), split_axis=0, concat_axis=0, tiled=True)


def send_errors(errors):
    return lax.all_to_all(errors, ("sect", "exp"), split_axis=0, concat_axis=0, tiled=True)


def shards(residuals, routes, blocks, enc_weight, enc_bias, dec_weight, dec_bias):
    tok_count, feature_width = residuals.shape
    active_count = blocks.shape[1]
    owned_blocks = enc_weight.shape[0]
    owners = lax.axis_size(("sect", "exp"))
    all_blocks = owners * owned_blocks
    capacity = tok_count * active_count // (2 * BLOCKS)
    entries = tok_count * active_count
    global_block = (routes[:, None] * BLOCKS + blocks).reshape(entries)
    onehot = (global_block[:, None] == jnp.arange(all_blocks, dtype=jnp.int32)[None, :]).astype(
        jnp.int32
    )
    ranking = jnp.sum((jnp.cumsum(onehot, 0) - 1) * onehot, 1)
    slot_index = global_block * capacity + ranking
    repeated = jnp.repeat(residuals, active_count, axis=0)
    outgoing = (
        jnp.zeros((all_blocks * capacity, feature_width), jnp.bfloat16).at[slot_index].set(repeated)
    )
    filled = (
        jnp.zeros((all_blocks * capacity,), jnp.bfloat16)
        .at[slot_index]
        .set(jnp.ones((entries,), jnp.bfloat16))
    )
    outgoing = outgoing.reshape(owners, owned_blocks, capacity, feature_width)
    filled = filled.reshape(owners, owned_blocks, capacity)
    incoming, present = send_rows(outgoing, filled)
    present_float = present.astype(jnp.float32)[..., None]
    pre_part = jnp.einsum(
        "sbcd,bld->sbcl", incoming, enc_weight, preferred_element_type=jnp.float32
    )
    pre_total = (
        lax.psum(pre_part.astype(jnp.bfloat16), "lat").astype(jnp.float32)
        + enc_bias[None, :, None, :]
    )
    act_full = jax.nn.softplus(pre_total).astype(jnp.bfloat16)
    partial_value = jnp.einsum(
        "sbcl,bld->sbcd", act_full, dec_weight, preferred_element_type=jnp.float32
    ).astype(jnp.bfloat16)
    returned = send_partials(partial_value).reshape(all_blocks * capacity, feature_width)
    gathered = (
        returned[slot_index].astype(jnp.float32).reshape(tok_count, active_count, feature_width)
    )
    recon = jnp.sum(gathered, 1) + dec_bias[None, :]
    reconstruction = recon.astype(jnp.bfloat16)
    error_rows = (recon - residuals.astype(jnp.float32)).astype(jnp.bfloat16)
    error_out = (
        jnp.zeros((all_blocks * capacity, feature_width), jnp.bfloat16)
        .at[slot_index]
        .set(jnp.repeat(error_rows, active_count, axis=0))
    )
    error_in = send_errors(error_out.reshape(owners, owned_blocks, capacity, feature_width))
    dec_grad = jnp.einsum(
        "sbcl,sbcd->bld", act_full, error_in, preferred_element_type=jnp.float32
    ).astype(jnp.bfloat16)
    dact_part = jnp.einsum(
        "sbcd,bld->sbcl", error_in, dec_weight, preferred_element_type=jnp.float32
    )
    dact = lax.psum(dact_part.astype(jnp.bfloat16), "lat").astype(jnp.float32)
    slope = (dact + L1_COEF * present_float) * jax.nn.sigmoid(pre_total)
    enc_bias_grad = jnp.sum(slope, (0, 2))
    slope_rows = slope.astype(jnp.bfloat16)
    enc_grad = jnp.einsum(
        "sbcl,sbcd->bld", slope_rows, incoming, preferred_element_type=jnp.float32
    ).astype(jnp.bfloat16)
    return (reconstruction, enc_grad, enc_bias_grad, dec_grad)


def solution(mesh):
    return jax.shard_map(
        shards,
        mesh=mesh,
        in_specs=(
            P(("sect", "exp"), "lat"),
            P(("sect", "exp")),
            P(("sect", "exp"), None),
            P(("sect", "exp"), None, "lat"),
            P(("sect", "exp"), None),
            P(("sect", "exp"), None, "lat"),
            P("lat"),
        ),
        out_specs=(
            P(("sect", "exp"), "lat"),
            P(("sect", "exp"), None, "lat"),
            P(("sect", "exp"), None),
            P(("sect", "exp"), None, "lat"),
        ),
        check_vma=False,
    )
```

profile of v0, /device:TPU:1, one launch (start us, length us, event | category | flops | bytes accessed | tf_op | source)
XLA Modules:
  0.0 551.1 jit_solution(17777547251550865532)
XLA Ops:
  7.2 0.8 broadcast_multiply_fusion.1
  10.2 1.2 reshape.104
  11.6 4.3 scatter_custom_fusion
  15.8 2.2 reshape.86
  18.0 127.4 %all_to_all.20 = bf16[128,2,4,1152]{3,2,1,0:T(4,128)(2,1)S(1)} all-to-all(bf16[128,2,4,1152]{3,2,1,0:T(4,128)(2,1)} %reshape.86), channel_id=1, replica_groups=mesh['sect'=2,'exp'=64,'lat'=4] {'sect','exp'}, dimensions={0} | all-to-all | bytes 4718592 | tf_op jit(solution)/shard_map/all_to_all | solution.py:14
  145.4 1.4 copy-done.2
  146.8 1.5 fusion.22
  148.3 52.1 %all-reduce.3.cloned.1.call-done = bf16[128,2,4,128]{3,0,2,1:T(8,128)(2,1)} async-done(((bf16[128,2,4,128]{3,0,2,1:T(8,128)(2,1)}), bf16[128,2,4,128]{3,0,2,1:T(8,128)(2,1)}) %all-reduce.3.cloned.1.call-update) | async-done | bytes 262160 | tf_op jit(solution)/shard_map/psum | solution.py:58
  200.4 1.8 fusion
  202.2 3.2 copy.56
  205.4 19.1 %all-to-all-start.1 = ((bf16[128,2,4,1152]{3,2,1,0:T(4,128)(2,1)}), bf16[128,2,4,1152]{3,2,1,0:T(4,128)(2,1)S(1)}, u32[]{:S(2)}, u32[]{:S(2)}) async-start(bf16[128,2,4,1152]{3,2,1,0:T(4,128)(2,1)} %copy.56), calls=%async_computation.1 | async-start | bytes 4718592 | tf_op jit(solution)/shard_map/all_to_all | solution.py:20
  224.6 3.8 scatter_custom_fusion.2
  228.3 0.8 reshape.90
  229.1 101.8 %all-to-all-done.1 = bf16[128,2,4,1152]{3,2,1,0:T(4,128)(2,1)S(1)} async-done(((bf16[128,2,4,1152]{3,2,1,0:T(4,128)(2,1)}), bf16[128,2,4,1152]{3,2,1,0:T(4,128)(2,1)S(1)}, u32[]{:S(2)}, u32[]{:S(2)}) %all-to-all-start.1) | async-done | bytes 2359328 | tf_op jit(solution)/shard_map/all_to_all | solution.py:20
  330.9 1.4 copy-done.1
  332.3 13.1 %all-to-all-start.3 = ((bf16[128,2,4]{2,1,0:T(2,128)(2,1)}), bf16[128,2,4]{2,1,0:T(2,128)(2,1)}, u32[]{:S(2)}, u32[]{:S(2)}) async-start(bf16[128,2,4]{2,1,0:T(2,128)(2,1)} %reshape.90), calls=%async_computation.3 | async-start | bytes 131072 | tf_op jit(solution)/shard_map/all_to_all | solution.py:15
  345.4 3.9 reshape.87
  349.3 2.8 gather_fusion
  352.1 2.5 reshape.91
  354.6 1.4 reduce_sum.31
  356.0 1.8 subtract_convert_fusion
  358.1 1.2 reshape.112
  359.2 4.3 scatter_custom_fusion.1
  363.5 2.1 reshape.89
  365.7 16.1 %all-to-all-start.2 = ((bf16[128,2,4,1152]{3,2,1,0:T(4,128)(2,1)}), bf16[128,2,4,1152]{3,2,1,0:T(4,128)(2,1)S(1)}, u32[]{:S(2)}, u32[]{:S(2)}) async-start(bf16[128,2,4,1152]{3,2,1,0:T(4,128)(2,1)} %reshape.89), calls=%async_computation.2 | async-start | bytes 4718592 | tf_op jit(solution)/shard_map/all_to_all | solution.py:24
  381.8 1.0 copy.58
  382.8 105.4 %all-to-all-done.2 = bf16[128,2,4,1152]{3,2,1,0:T(4,128)(2,1)S(1)} async-done(((bf16[128,2,4,1152]{3,2,1,0:T(4,128)(2,1)}), bf16[128,2,4,1152]{3,2,1,0:T(4,128)(2,1)S(1)}, u32[]{:S(2)}, u32[]{:S(2)}) %all-to-all-start.2) | async-done | bytes 2359328 | tf_op jit(solution)/shard_map/all_to_all | solution.py:24
  488.1 1.5 fusion.19
  489.6 3.5 fusion.2
  493.1 47.8 %all-reduce.5.cloned.1.call-done = bf16[128,2,4,128]{3,0,2,1:T(8,128)(2,1)} async-done(((bf16[128,2,4,128]{3,0,2,1:T(8,128)(2,1)}), bf16[128,2,4,128]{3,0,2,1:T(8,128)(2,1)}) %all-reduce.5.cloned.1.call-update) | async-done | bytes 262160 | tf_op jit(solution)/shard_map/psum | solution.py:84
  540.9 2.5 fusion.1
  543.5 0.8 fusion.34
  (45 shorter events, 2.8 us)
Async XLA Ops:
  7.2 193.3 %copy-start = (bf16[2,128,1152]{2,1,0:T(8,128)(2,1)S(1)}, bf16[2,128,1152]{2,1,0:T(8,128)(2,1)}, u32[]{:S(2)}) copy-start(bf16[2,128,1152]{2,1,0:T(8,128)(2,1)} %param.12) | copy-start | bytes 1769476
  7.2 2.7 copy-start.5
  7.2 193.3 %all-reduce.3.cloned.1.call-start = ((), (), s32[]{:S(2)}) async-start(), calls=%async_computation.4 | async-start | bytes 524288 | tf_op jit(solution)/shard_map/psum | solution.py:58
  18.0 128.8 %copy-start.10 = (bf16[2,128,1152]{2,1,0:T(8,128)(2,1)S(1)}, bf16[2,128,1152]{2,1,0:T(8,128)(2,1)}, u32[]{:S(2)}) copy-start(bf16[2,128,1152]{2,1,0:T(8,128)(2,1)} %param.10) | copy-start | bytes 1769476
  145.4 1.4 copy-start.2
  146.8 53.6 %copy-start.8 = (f32[2,128]{1,0:T(2,128)S(1)}, f32[2,128]{1,0:T(2,128)}, u32[]{:S(2)}) copy-start(f32[2,128]{1,0:T(2,128)} %param.11) | copy-start | bytes 3076
  205.4 125.5 %all-to-all-start.1 = ((bf16[128,2,4,1152]{3,2,1,0:T(4,128)(2,1)}), bf16[128,2,4,1152]{3,2,1,0:T(4,128)(2,1)S(1)}, u32[]{:S(2)}, u32[]{:S(2)}) async-start(bf16[128,2,4,1152]{3,2,1,0:T(4,128)(2,1)} %copy.56), calls=%async_computation.1 | async-start | bytes 4718592 | tf_op jit(solution)/shard_map/all_to_all | solution.py:20
  330.9 1.4 copy-start.1
  332.3 33.3 %all-to-all-start.3 = ((bf16[128,2,4]{2,1,0:T(2,128)(2,1)}), bf16[128,2,4]{2,1,0:T(2,128)(2,1)}, u32[]{:S(2)}, u32[]{:S(2)}) async-start(bf16[128,2,4]{2,1,0:T(2,128)(2,1)} %reshape.90), calls=%async_computation.3 | async-start | bytes 131072 | tf_op jit(solution)/shard_map/all_to_all | solution.py:15
  354.6 1.4 copy-start.9
  365.7 122.5 %all-to-all-start.2 = ((bf16[128,2,4,1152]{3,2,1,0:T(4,128)(2,1)}), bf16[128,2,4,1152]{3,2,1,0:T(4,128)(2,1)S(1)}, u32[]{:S(2)}, u32[]{:S(2)}) async-start(bf16[128,2,4,1152]{3,2,1,0:T(4,128)(2,1)} %reshape.89), calls=%async_computation.2 | async-start | bytes 4718592 | tf_op jit(solution)/shard_map/all_to_all | solution.py:24
  381.7 107.9 %copy-start.6 = (bf16[128,2,4,128]{3,0,2,1:T(8,128)(2,1)S(1)}, bf16[128,2,4,128]{3,0,2,1:T(8,128)(2,1)}, u32[]{:S(2)}) copy-start(bf16[128,2,4,128]{3,0,2,1:T(8,128)(2,1)} %all-reduce.3.cloned.1.call-done) | copy-start | bytes 786436
  381.7 159.2 %all-reduce.5.cloned.1.call-start = ((), (), s32[]{:S(2)}) async-start(), calls=%async_computation.5 | async-start | bytes 524288 | tf_op jit(solution)/shard_map/psum | solution.py:84
  488.1 1.5 copy-start.4
  489.6 51.3 %copy-start.3 = (bf16[128,2,4,1152]{3,2,1,0:T(4,128)(2,1)S(1)}, bf16[128,2,4,1152]{3,2,1,0:T(4,128)(2,1)}, u32[]{:S(2)}) copy-start(bf16[128,2,4,1152]{3,2,1,0:T(4,128)(2,1)} %copy-done.2) | copy-start | bytes 7077892
  540.9 2.6 copy-start.7
Sparse Core Ops, SparseCore 0:
  148.5 51.9 all-reduce.2
  489.8 51.0 all-reduce.4
where the time goes:
time: 553 us; the launch traced here: 551 us
  waiting for transfers between devices  307 us (56%)
  blocking collectives  127 us (23%)
  starting transfers between devices  48.3 us (9%)
  local copies, waits for them, and re-layouts  37.3 us (7%)
  between operations  14.2 us (3%)
  matrix products  10.8 us (2%)
  other arithmetic  6.01 us (1%)
    all_to_all x1, blocking collectives, send_rows(): lax.all_to_all(outgoing, ('sect', 'exp'), split_axis=0, concat_axis=0, ti...  127 us
    all_to_all x1, waiting for transfers between devices, send_errors(): lax.all_to_all(errors, ('sect', 'exp'), split_axis=0, concat_axis=0, tile...  105 us
    all_to_all x1, waiting for transfers between devices, send_partials(): lax.all_to_all(partial_value, ('sect', 'exp'), split_axis=0, concat_axis=...  102 us
    psum x1, waiting for transfers between devices, shards(): lax.psum(pre_part.astype(jnp.bfloat16), 'lat').astype(jnp.float32)  52.1 us
    psum x1, waiting for transfers between devices, shards(): dact = lax.psum(dact_part.astype(jnp.bfloat16), 'lat').astype(jnp.float32)  47.8 us
    all_to_all x1, starting transfers between devices, send_partials(): lax.all_to_all(partial_value, ('sect', 'exp'), split_axis=0, concat_axis=...  19.1 us
    all_to_all x1, starting transfers between devices, send_errors(): lax.all_to_all(errors, ('sect', 'exp'), split_axis=0, concat_axis=0, tile...  16.1 us
    all_to_all x1, starting transfers between devices, send_rows(): lax.all_to_all(filled, ('sect', 'exp'), split_axis=0, concat_axis=0, tile...  13.1 us
  transfers between devices with their start and end apart: 5, of which 4 were waited for; matrix products, arithmetic and copies ran while one was open for 5% of the time, Pallas kernels for 0%

commit v1 on v0

v1 whole, which is shorter than its diff:
```python
import jax
import jax.numpy as jnp
from jax import lax
from jax.sharding import Mesh, PartitionSpec as P

BLOCKS = 64
L1_COEF = 0.2
CAP = 4
NY = 4
NZ = 16

F32 = jnp.float32
BF16 = jnp.bfloat16


def swap_cores(v):
    return lax.ppermute(v, "sect", [(0, 1), (1, 0)])


def y_ring(v, step):
    perm = [(y, (y + step) % NY) for y in range(NY)]
    perm += [(NY + y, NY + (y - step) % NY) for y in range(NY)]
    return lax.ppermute(v, ("sect", "y"), perm)


def gather_blocks(own):
    chip = jnp.stack([own, swap_cores(own)])
    near = y_ring(chip, 1)
    far = y_ring(near[0], 1)
    half = jnp.concatenate([own[None], near, far[None]])
    return jnp.concatenate([half, swap_cores(half)])


def scatter_blocks(part):
    half = part[:4].astype(F32) + swap_cores(part[4:]).astype(F32)
    half = half.astype(part.dtype)
    far = y_ring(half[3], -1)
    first = (half[1].astype(F32) + far.astype(F32)).astype(part.dtype)
    near = y_ring(jnp.stack([first, half[2]]), -1)
    return half[0].astype(F32) + near[0].astype(F32) + swap_cores(near[1]).astype(F32)


def peer_place(owner_sect, owner_y):
    sect, y = lax.axis_index("sect"), lax.axis_index("y")
    other = owner_sect ^ sect
    delta = owner_y - y
    delta = jnp.where(sect == 0, delta, -delta) & 3
    code = delta * 2 + other
    place = jnp.zeros_like(code)
    for at, value in enumerate((0, 4, 6, 5, 3, 7, 1, 2)):
        place = jnp.where(code == at, value, place)
    return place


def sum_lat(part):
    part = part.astype(BF16)
    turned = [
        lax.ppermute(part, "lat", [(i, (i + k) % 4) for i in range(4)]).astype(F32)
        for k in (1, 2, 3)
    ]
    return (part.astype(F32) + turned[1]) + (turned[0] + turned[2])


def shards(residuals, routes, blocks, enc_weight, enc_bias, dec_weight, dec_bias):
    tok_count, width = residuals.shape
    owned, latents, _ = enc_weight.shape
    local = 8 * owned
    pairs = NZ // 2
    z = lax.axis_index("z")

    rows = lax.all_gather(residuals, "z", axis=0, tiled=True).reshape(pairs, 2 * tok_count, width)

    weights = gather_blocks(jnp.stack([enc_weight, dec_weight]))
    enc_local = weights[:, 0].reshape(local, latents, width)
    dec_local = weights[:, 1].reshape(local, latents, width)
    bias_local = gather_blocks(enc_bias).reshape(local, latents)

    global_block = routes[:, None] * BLOCKS + blocks
    ids = lax.all_to_all(
        jnp.broadcast_to(global_block.reshape(1, -1), (NZ, tok_count * 4)), "z", 0, 0, tiled=True
    ).reshape(pairs, 2, tok_count, 4)
    place = peer_place(ids >> 7, (ids >> 5) & 3) * owned + (ids & 1)
    place = jnp.where(((ids >> 1) & 15) == z, place, -1)
    named = jnp.sum(
        (place[..., None] == jnp.arange(local, dtype=jnp.int32)).astype(F32), axis=3
    )
    lower = (
        jnp.arange(tok_count)[:, None] > jnp.arange(tok_count)[None, :]
    ).astype(BF16)
    rank = jnp.einsum("ut,pstk->psuk", lower, named.astype(BF16), preferred_element_type=F32)
    slot = rank + CAP * jnp.arange(2, dtype=F32)[None, :, None, None]
    slot = jnp.where(named > 0, slot, -1.0).reshape(pairs, 2 * tok_count, local)
    slot = slot.transpose(0, 2, 1)
    pick = (
        slot[:, :, None, :] == jnp.arange(2 * CAP, dtype=F32)[None, None, :, None]
    ).astype(BF16)
    present = jnp.sum(pick.astype(F32), axis=3).transpose(1, 0, 2).reshape(local, -1)

    def to_slots(v):
        taken = jnp.einsum("pkrt,ptd->kprd", pick, v, preferred_element_type=F32).astype(BF16)
        return taken.reshape(local, pairs * 2 * CAP, width)

    incoming = to_slots(rows)
    pre_part = jnp.einsum("krd,kld->krl", incoming, enc_local, preferred_element_type=F32)
    pre = sum_lat(pre_part) + bias_local[:, None, :]
    act = jax.nn.softplus(pre).astype(BF16)
    part = jnp.einsum("krl,kld->krd", act, dec_local, preferred_element_type=F32).astype(BF16)
    part = part.reshape(local, pairs, 2 * CAP, width)
    home = jnp.einsum("pkrt,kprd->ptd", pick, part, preferred_element_type=F32).astype(BF16)
    total = lax.psum_scatter(
        home.reshape(NZ * tok_count, width), "z", scatter_dimension=0, tiled=True
    )
    recon = total.astype(F32) + dec_bias[None, :]
    reconstruction = recon.astype(BF16)
    error = (recon - residuals.astype(F32)).astype(BF16)
    errors = lax.all_gather(error, "z", axis=0, tiled=True).reshape(pairs, 2 * tok_count, width)
    error_in = to_slots(errors)
    dact_part = jnp.einsum("krd,kld->krl", error_in, dec_local, preferred_element_type=F32)
    dact = sum_lat(dact_part)
    dec_part = jnp.einsum("krl,krd->kld", act, error_in, preferred_element_type=F32).astype(BF16)
    dec_grad = scatter_blocks(dec_part.reshape(8, owned, latents, width)).astype(BF16)
    slope = (dact + L1_COEF * present[..., None]) * jax.nn.sigmoid(pre)
    enc_part = jnp.einsum(
        "krl,krd->kld", slope.astype(BF16), incoming, preferred_element_type=F32
    ).astype(BF16)
    enc_grad = scatter_blocks(enc_part.reshape(8, owned, latents, width)).astype(BF16)
    enc_bias_grad = scatter_blocks(jnp.sum(slope, 1).reshape(8, owned, latents))
    return reconstruction, enc_grad, enc_bias_grad, dec_grad


def solution(mesh):
    fine = Mesh(mesh.devices.reshape(2, NY, NZ, 4), ("sect", "y", "z", "lat"))
    own = ("sect", "y", "z")
    return jax.shard_map(
        shards,
        mesh=fine,
        in_specs=(
            P(own, "lat"),
            P(own),
            P(own, None),
            P(own, None, "lat"),
            P(own, None),
            P(own, None, "lat"),
            P("lat"),
        ),
        out_specs=(
            P(own, "lat"),
            P(own, None, "lat"),
            P(own, None),
            P(own, None, "lat"),
        ),
        check_vma=False,
    )
```

time: 553 us -> 412 us (0.75)
  blocking collectives: 127 us -> 0 us
  waiting for transfers between devices: 307 us -> 227 us
  starting transfers between devices: 48.3 us -> 108 us
  local copies, waits for them, and re-layouts: 37.3 us -> 16.8 us
  other arithmetic: 6.01 us -> 22.9 us
  matrix products: 10.8 us -> 22.3 us
    all_to_all x3 -> x1, waiting for transfers between devices: 207 us -> 8.26 us  [shards(): lax.all_to_all(jnp.broadcast_to(global_block.reshape(1, -1), (NZ, tok_cou...]
    all_to_all x1 -> x0, blocking collectives: 127 us -> none  [send_rows(): lax.all_to_all(outgoing, ('sect', 'exp'), split_axis=0, concat_axis=0, ti...]
    psum x2 -> x0, waiting for transfers between devices: 99.9 us -> none  [the longest x1 52.1 us: shards(): lax.psum(pre_part.astype(jnp.bfloat16), 'lat').astype(jnp.float32)]
    ppermute x0 -> x26, starting transfers between devices: none -> 98 us  [the longest x10 49.8 us: swap_cores(): return lax.ppermute(v, 'sect', [(0, 1), (1, 0)])]
    ppermute x0 -> x26, waiting for transfers between devices: none -> 79.9 us  [the longest x10 74.6 us: y_ring(): return lax.ppermute(v, ('sect', 'y'), perm)]
    all_gather x0 -> x2, waiting for transfers between devices: none -> 79.2 us  [the longest x1 79.2 us: shards(): lax.all_gather(error, 'z', axis=0, tiled=True)]
    reduce_scatter x0 -> x1, waiting for transfers between devices: none -> 59.5 us  [shards(): lax.psum_scatter(home.reshape(NZ * tok_count, width), 'z', scatter_dimens...]
    all_to_all x3 -> x1, starting transfers between devices: 48.2 us -> 9.54 us  [shards(): lax.all_to_all(jnp.broadcast_to(global_block.reshape(1, -1), (NZ, tok_cou...]
  transfers between devices with their start and end apart: 5 -> 30, of which waited for: 4 -> 13; matrix products, arithmetic and copies ran while one was open for 5% -> 11% of each run, Pallas kernels for 0% -> 0%
where the time goes in v1:
time: 412 us; the launch traced here: 411 us
  waiting for transfers between devices  227 us (55%)
  starting transfers between devices  108 us (26%)
  other arithmetic  22.9 us (6%)
  matrix products  22.3 us (5%)
  local copies, waits for them, and re-layouts  16.8 us (4%)
  between operations  14.6 us (4%)
    all_gather x1, waiting for transfers between devices, shards(): lax.all_gather(error, 'z', axis=0, tiled=True)  79.2 us
    ppermute x10, waiting for transfers between devices, y_ring(): return lax.ppermute(v, ('sect', 'y'), perm)  74.6 us
    reduce_scatter x1, waiting for transfers between devices, shards(): lax.psum_scatter(home.reshape(NZ * tok_count, width), 'z', scatter_dimens...  59.5 us
    ppermute x10, starting transfers between devices, swap_cores(): return lax.ppermute(v, 'sect', [(0, 1), (1, 0)])  49.8 us
    ppermute x10, starting transfers between devices, y_ring(): return lax.ppermute(v, ('sect', 'y'), perm)  28.4 us
    ppermute x6, starting transfers between devices, sum_lat(): lax.ppermute(part, 'lat', [(i, (i + k) % 4) for i in range(4)]).astype(F32)  19.7 us
    all_to_all x1, starting transfers between devices, shards(): lax.all_to_all(jnp.broadcast_to(global_block.reshape(1, -1), (NZ, tok_cou...  9.54 us
    all_to_all x1, waiting for transfers between devices, shards(): lax.all_to_all(jnp.broadcast_to(global_block.reshape(1, -1), (NZ, tok_cou...  8.26 us
  transfers between devices with their start and end apart: 30, of which 13 were waited for; matrix products, arithmetic and copies ran while one was open for 11% of the time, Pallas kernels for 0%

profile of v1, /device:TPU:1, one launch (start us, length us, event | category | flops | bytes accessed | tf_op | source)
XLA Modules:
  0.0 411.1 jit_solution(15345866038706372155)
XLA Ops:
  8.6 8.8 %collective-permute-start = (bf16[2,2,128,1152]{3,2,1,0:T(8,128)(2,1)S(1)}, bf16[2,2,128,1152]{3,2,1,0:T(8,128)(2,1)S(1)}, u32[]{:S(2)}, u32[]{:S(2)}) collective-permute-start(bf16[2,2,128,1152]{3,2,1,0:T(8,128)(2,1)S(1)} %get-tuple-element.20), channel_id=1, source_target_pairs={{0,256},{256,0},{1,257},{257,1},{2,258},{258,2},{3,259},{259,3},{4... | collective-permute-start | bytes 3538952 | tf_op jit(solution)/shard_map/ppermute | solution.py:17
  23.5 28.2 %collective-permute-done.1 = bf16[2,2,2,128,1152]{4,3,2,1,0:T(8,128)(2,1)S(1)} collective-permute-done((bf16[2,2,2,128,1152]{4,3,2,1,0:T(8,128)(2,1)}, bf16[2,2,2,128,1152]{4,3,2,1,0:T(8,128)(2,1)S(1)}, u32[]{:S(2)}, u32[]{:S(2)}) %collective-permute-start.1) | collective-permute-done | bytes 2359328 | tf_op jit(solution)/shard_map/ppermute | solution.py:23
  51.8 3.1 collective-permute-start.2
  55.0 14.2 %collective-permute-done.2 = bf16[2,2,128,1152]{3,2,1,0:T(8,128)(2,1)S(1)} collective-permute-done((bf16[2,2,128,1152]{3,2,1,0:T(8,128)(2,1)S(1)}, bf16[2,2,128,1152]{3,2,1,0:T(8,128)(2,1)S(1)}, u32[]{:S(2)}, u32[]{:S(2)}) %collective-permute-start.2) | collective-permute-done | bytes 1179680 | tf_op jit(solution)/shard_map/ppermute | solution.py:23
  71.8 6.2 %collective-permute-start.3 = (bf16[4,2,2,128,1152]{4,3,2,1,0:T(8,128)(2,1)}, bf16[4,2,2,128,1152]{4,3,2,1,0:T(8,128)(2,1)}, u32[]{:S(2)}, u32[]{:S(2)}) collective-permute-start(bf16[4,2,2,128,1152]{4,3,2,1,0:T(8,128)(2,1)} %pad_maximum_fusion.1), channel_id=1, source_target_pairs={{0,256},{256,0},{1,257},{257,1},{2,258},{258,2},{3,259},{259,3},{4... | collective-permute-start | bytes 14155784 | tf_op jit(solution)/shard_map/ppermute | solution.py:17
  80.8 9.5 %all-to-all-start = ((s32[16,1,512]{2,1,0:T(1,128)}), s32[16,1,512]{2,1,0:T(1,128)S(1)}, u32[]{:S(2)}, u32[]{:S(2)}) async-start(s32[16,1,512]{2,1,0:T(1,128)} %broadcast_in_dim.46), calls=%async_computation | async-start | bytes 65536 | tf_op jit(solution)/shard_map/all_to_all | solution.py:79
  90.5 3.3 collective-permute-start.8
  93.8 8.3 %all-to-all-done = s32[16,1,512]{2,1,0:T(1,128)S(1)} async-done(((s32[16,1,512]{2,1,0:T(1,128)}), s32[16,1,512]{2,1,0:T(1,128)S(1)}, u32[]{:S(2)}, u32[]{:S(2)}) %all-to-all-start) | async-done | bytes 32800 | tf_op jit(solution)/shard_map/all_to_all | solution.py:79
  110.6 3.4 fusion.2
  114.4 6.7 %pad_maximum_fusion = bf16[8,2,2,128,1152]{4,3,2,1,0:T(8,128)(2,1)} fusion(bf16[4,2,2,128,1152]{4,3,2,1,0:T(8,128)(2,1)} %collective-permute-done.3, bf16[1,2,2,128,1152]{4,3,2,1,0:T(8,128)(2,1)S(1)} %bitcast.140, bf16[2,2,2,128,1152]{4,3,2,1,0:T(8,128)(2,1)S(1)} %copy-done.4, bf16[1,2,2,128,1152]{4,3,2,1,0:T(8,128)(2,1)S(1)} %copy-done.2), kind=kLoop, calls=%fused_computation | loop fusion | flops 14155776 | bytes 18874368 | tf_op jit(solution)/shard_map/concatenate | solution.py:31
  121.1 7.1 %fusion.47 = (bf16[8,1,2,128,1152]{4,3,2,1,0:T(8,128)(2,1)S(1)}, bf16[8,1,2,128,1152]{4,3,2,1,0:T(8,128)(2,1)}) fusion(bf16[8,2,2,128,1152]{4,3,2,1,0:T(8,128)(2,1)} %pad_maximum_fusion), kind=kLoop, calls=%fused_computation.98 | loop fusion | bytes 18874368 | tf_op jit(solution)/shard_map/slice | solution.py:75
  128.2 5.9 %fusion.16 = bf16[16,64,128]{2,1,0:T(8,128)(2,1)S(1)} fusion(bf16[16,128,1152]{2,1,0:T(8,128)(2,1)} %bitcast.133, bf16[16,8,8,1152]{3,2,0,1:T(8,128)(2,1)S(1)} %fusion.2), kind=kOutput, calls=%fused_computation.27 | convolution fusion | flops 302120960 | bytes 7340032 | tf_op jit(solution)/shard_map/krd,kld->krl/dot_general | solution.py:104
  134.1 4.4 %collective-permute-start.6 = (bf16[16,64,128]{2,1,0:T(8,128)(2,1)S(1)}, bf16[16,64,128]{2,1,0:T(8,128)(2,1)S(1)}, u32[]{:S(2)}, u32[]{:S(2)}) collective-permute-start(bf16[16,64,128]{2,1,0:T(8,128)(2,1)S(1)} %fusion.16), channel_id=1, source_target_pairs={{0,3},{1,0},{2,1},{3,2},{4,7},{5,4},{6,5},{7,6},{8,11},{9,8},{10,9... | collective-permute-start | bytes 786440 | tf_op jit(solution)/shard_map/ppermute | solution.py:58
  140.4 3.4 collective-permute-start.4
  143.9 3.5 collective-permute-start.9
  148.5 7.1 %collective-permute-start.10 = (f32[4,2,128]{2,1,0:T(2,128)S(1)}, f32[4,2,128]{2,1,0:T(2,128)S(1)}, u32[]{:S(2)}, u32[]{:S(2)}) collective-permute-start(f32[4,2,128]{2,1,0:T(2,128)S(1)} %pad_maximum_fusion.7), channel_id=1, source_target_pairs={{0,256},{256,0},{1,257},{257,1},{2,258},{258,2},{3,259},{259,3},{4... | collective-permute-start | bytes 12296 | tf_op jit(solution)/shard_map/ppermute | solution.py:17
  157.6 4.0 bitcast_convert_fusion
  161.7 59.5 %reduce-scatter.2.cloned.1.call-done = bf16[128,1152]{1,0:T(8,128)(2,1)} async-done(((bf16[2048,1152]{1,0:T(8,128)(2,1)}), bf16[128,1152]{1,0:T(8,128)(2,1)}) %reduce-scatter.2.cloned.1.call-update) | async-done | bytes 294928 | tf_op jit(solution)/shard_map/reduce_scatter | solution.py:110
  224.8 79.2 %all-gather.5.cloned.1.call-done = bf16[2048,1152]{1,0:T(8,128)(2,1)} async-done(((bf16[128,1152]{1,0:T(8,128)(2,1)}), bf16[2048,1152]{1,0:T(8,128)(2,1)}) %all-gather.5.cloned.1.call-update) | async-done | bytes 4718608 | tf_op jit(solution)/shard_map/all_gather | solution.py:116
  304.0 3.4 convolution_convert_fusion.4
  309.4 4.4 %collective-permute-start.13 = (bf16[16,64,128]{2,1,0:T(8,128)(2,1)S(1)}, bf16[16,64,128]{2,1,0:T(8,128)(2,1)S(1)}, u32[]{:S(2)}, u32[]{:S(2)}) collective-permute-start(bf16[16,64,128]{2,1,0:T(8,128)(2,1)S(1)} %fusion.13), channel_id=1, source_target_pairs={{0,3},{1,0},{2,1},{3,2},{4,7},{5,4},{6,5},{7,6},{8,11},{9,8},{10,9... | collective-permute-start | bytes 786440 | tf_op jit(solution)/shard_map/ppermute | solution.py:58
  315.8 3.7 collective-permute-start.11
  321.4 11.0 %collective-permute-start.22 = (bf16[4,2,128,1152]{3,2,1,0:T(8,128)(2,1)S(1)}, bf16[4,2,128,1152]{3,2,1,0:T(8,128)(2,1)S(1)}, u32[]{:S(2)}, u32[]{:S(2)}) collective-permute-start(bf16[4,2,128,1152]{3,2,1,0:T(8,128)(2,1)S(1)} %bitcast.142), channel_id=1, source_target_pairs={{0,256},{256,0},{1,257},{257,1},{2,258},{258,2},{3,259},{259,3},{4... | collective-permute-start | bytes 7077896 | tf_op jit(solution)/shard_map/ppermute | solution.py:17
  335.0 4.2 %collective-permute-start.14 = (bf16[4,2,128,1152]{3,2,1,0:T(8,128)(2,1)S(1)}, bf16[4,2,128,1152]{3,2,1,0:T(8,128)(2,1)S(1)}, u32[]{:S(2)}, u32[]{:S(2)}) collective-permute-start(bf16[4,2,128,1152]{3,2,1,0:T(8,128)(2,1)S(1)} %bitcast.143), channel_id=1, source_target_pairs={{0,256},{256,0},{1,257},{257,1},{2,258},{258,2},{3,259},{259,3},{4... | collective-permute-start | bytes 7077896 | tf_op jit(solution)/shard_map/ppermute | solution.py:17
  344.1 3.5 collective-permute-start.23
  348.4 2.9 collective-permute-start.15
  351.3 4.6 %collective-permute-done.23 = bf16[2,128,1152]{2,1,0:T(8,128)(2,1)S(1)} collective-permute-done((bf16[2,128,1152]{2,1,0:T(8,128)(2,1)S(1)}, bf16[2,128,1152]{2,1,0:T(8,128)(2,1)S(1)}, u32[]{:S(2)}, u32[]{:S(2)}) %collective-permute-start.23) | collective-permute-done | bytes 589856 | tf_op jit(solution)/shard_map/ppermute | solution.py:23
  358.6 3.6 collective-permute-done.15
  364.9 2.9 collective-permute-start.19
  367.9 19.7 %collective-permute-done.19 = f32[2,128]{1,0:T(2,128)S(1)} collective-permute-done((f32[2,128]{1,0:T(2,128)S(1)}, f32[2,128]{1,0:T(2,128)S(1)}, u32[]{:S(2)}, u32[]{:S(2)}) %collective-permute-start.19) | collective-permute-done | bytes 1056 | tf_op jit(solution)/shard_map/ppermute | solution.py:23
  389.9 3.2 collective-permute-done.20
  393.1 4.4 %collective-permute-start.21 = (f32[2,128]{1,0:T(2,128)S(1)}, f32[2,128]{1,0:T(2,128)S(1)}, u32[]{:S(2)}, u32[]{:S(2)}) collective-permute-start(f32[2,128]{1,0:T(2,128)S(1)} %slice_bitcast_fusion.7), channel_id=1, source_target_pairs={{0,256},{256,0},{1,257},{257,1},{2,258},{258,2},{3,259},{259,3},{4... | collective-permute-start | bytes 3080 | tf_op jit(solution)/shard_map/ppermute | solution.py:17
  (135 shorter events, 59.2 us)
Async XLA Ops:
  7.2 103.4 %all-gather.3.cloned.1.call-start = ((), (), s32[]{:S(2)}) async-start(), calls=%async_computation.2 | async-start | bytes 5013504 | tf_op jit(solution)/shard_map/all_gather | solution.py:71
  8.6 60.6 %copy-start.1 = (bf16[1,2,2,128,1152]{4,3,2,1,0:T(8,128)(2,1)}, bf16[1,2,2,128,1152]{4,3,2,1,0:T(8,128)(2,1)S(1)}, u32[]{:S(2)}) copy-start(bf16[1,2,2,128,1152]{4,3,2,1,0:T(8,128)(2,1)S(1)} %get-tuple-element.19) | copy-start | bytes 3538948
  8.6 11.2 %collective-permute-start = (bf16[2,2,128,1152]{3,2,1,0:T(8,128)(2,1)S(1)}, bf16[2,2,128,1152]{3,2,1,0:T(8,128)(2,1)S(1)}, u32[]{:S(2)}, u32[]{:S(2)}) collective-permute-start(bf16[2,2,128,1152]{3,2,1,0:T(8,128)(2,1)S(1)} %get-tuple-element.20), channel_id=1, source_target_pairs={{0,256},{256,0},{1,257},{257,1},{2,258},{258,2},{3,259},{259,3},{4... | collective-permute-start | bytes 3538952 | tf_op jit(solution)/shard_map/ppermute | solution.py:17
  21.5 30.2 %collective-permute-start.1 = (bf16[2,2,2,128,1152]{4,3,2,1,0:T(8,128)(2,1)}, bf16[2,2,2,128,1152]{4,3,2,1,0:T(8,128)(2,1)S(1)}, u32[]{:S(2)}, u32[]{:S(2)}) collective-permute-start(bf16[2,2,2,128,1152]{4,3,2,1,0:T(8,128)(2,1)} %pad_maximum_fusion.2), channel_id=1, source_target_pairs={{0,64},{64,128},{128,192},{192,0},{256,448},{320,256},{384,320},{4... | collective-permute-start | bytes 7077896 | tf_op jit(solution)/shard_map/ppermute | solution.py:23
  51.8 17.3 %collective-permute-start.2 = (bf16[2,2,128,1152]{3,2,1,0:T(8,128)(2,1)S(1)}, bf16[2,2,128,1152]{3,2,1,0:T(8,128)(2,1)S(1)}, u32[]{:S(2)}, u32[]{:S(2)}) collective-permute-start(bf16[2,2,128,1152]{3,2,1,0:T(8,128)(2,1)S(1)} %slice_bitcast_fusion), channel_id=1, source_target_pairs={{0,64},{64,128},{128,192},{192,0},{256,448},{320,256},{384,320},{4... | collective-permute-start | bytes 3538952 | tf_op jit(solution)/shard_map/ppermute | solution.py:23
  71.8 42.2 %collective-permute-start.3 = (bf16[4,2,2,128,1152]{4,3,2,1,0:T(8,128)(2,1)}, bf16[4,2,2,128,1152]{4,3,2,1,0:T(8,128)(2,1)}, u32[]{:S(2)}, u32[]{:S(2)}) collective-permute-start(bf16[4,2,2,128,1152]{4,3,2,1,0:T(8,128)(2,1)} %pad_maximum_fusion.1), channel_id=1, source_target_pairs={{0,256},{256,0},{1,257},{257,1},{2,258},{258,2},{3,259},{259,3},{4... | collective-permute-start | bytes 14155784 | tf_op jit(solution)/shard_map/ppermute | solution.py:17
  78.0 12.5 %collective-permute-start.7 = (f32[2,128]{1,0:T(2,128)S(1)}, f32[2,128]{1,0:T(2,128)S(1)}, u32[]{:S(2)}, u32[]{:S(2)}) collective-permute-start(f32[2,128]{1,0:T(2,128)S(1)} %copy-done.14), channel_id=1, source_target_pairs={{0,256},{256,0},{1,257},{257,1},{2,258},{258,2},{3,259},{259,3},{4... | collective-permute-start | bytes 3080 | tf_op jit(solution)/shard_map/ppermute | solution.py:17
  80.8 21.2 %all-to-all-start = ((s32[16,1,512]{2,1,0:T(1,128)}), s32[16,1,512]{2,1,0:T(1,128)S(1)}, u32[]{:S(2)}, u32[]{:S(2)}) async-start(s32[16,1,512]{2,1,0:T(1,128)} %broadcast_in_dim.46), calls=%async_computation | async-start | bytes 65536 | tf_op jit(solution)/shard_map/all_to_all | solution.py:79
  90.4 130.8 %reduce-scatter.2.cloned.1.call-start = ((), (), s32[]{:S(2)}) async-start(), calls=%async_computation.3 | async-start | bytes 5013504 | tf_op jit(solution)/shard_map/reduce_scatter | solution.py:110
  90.5 53.4 %collective-permute-start.8 = (f32[2,2,128]{2,1,0:T(2,128)S(1)}, f32[2,2,128]{2,1,0:T(2,128)S(1)}, u32[]{:S(2)}, u32[]{:S(2)}) collective-permute-start(f32[2,2,128]{2,1,0:T(2,128)S(1)} %pad_maximum_fusion.8), channel_id=1, source_target_pairs={{0,64},{64,128},{128,192},{192,0},{256,448},{320,256},{384,320},{4... | collective-permute-start | bytes 6152 | tf_op jit(solution)/shard_map/ppermute | solution.py:23
  134.1 22.1 %collective-permute-start.6 = (bf16[16,64,128]{2,1,0:T(8,128)(2,1)S(1)}, bf16[16,64,128]{2,1,0:T(8,128)(2,1)S(1)}, u32[]{:S(2)}, u32[]{:S(2)}) collective-permute-start(bf16[16,64,128]{2,1,0:T(8,128)(2,1)S(1)} %fusion.16), channel_id=1, source_target_pairs={{0,3},{1,0},{2,1},{3,2},{4,7},{5,4},{6,5},{7,6},{8,11},{9,8},{10,9... | collective-permute-start | bytes 786440 | tf_op jit(solution)/shard_map/ppermute | solution.py:58
  138.5 17.8 %collective-permute-start.5 = (bf16[16,64,128]{2,1,0:T(8,128)(2,1)S(1)}, bf16[16,64,128]{2,1,0:T(8,128)(2,1)S(1)}, u32[]{:S(2)}, u32[]{:S(2)}) collective-permute-start(bf16[16,64,128]{2,1,0:T(8,128)(2,1)S(1)} %fusion.16), channel_id=1, source_target_pairs={{0,1},{1,2},{2,3},{3,0},{4,5},{5,6},{6,7},{7,4},{8,9},{9,10},{10,1... | collective-permute-start | bytes 786440 | tf_op jit(solution)/shard_map/ppermute | solution.py:58
  140.4 15.9 %collective-permute-start.4 = (bf16[16,64,128]{2,1,0:T(8,128)(2,1)S(1)}, bf16[16,64,128]{2,1,0:T(8,128)(2,1)S(1)}, u32[]{:S(2)}, u32[]{:S(2)}) collective-permute-start(bf16[16,64,128]{2,1,0:T(8,128)(2,1)S(1)} %fusion.16), channel_id=1, source_target_pairs={{0,2},{1,3},{2,0},{3,1},{4,6},{5,7},{6,4},{7,5},{8,10},{9,11},{10,... | collective-permute-start | bytes 786440 | tf_op jit(solution)/shard_map/ppermute | solution.py:58
  143.9 4.6 %collective-permute-start.9 = (f32[2,128]{1,0:T(2,128)S(1)}, f32[2,128]{1,0:T(2,128)S(1)}, u32[]{:S(2)}, u32[]{:S(2)}) collective-permute-start(f32[2,128]{1,0:T(2,128)S(1)} %slice_bitcast_fusion.10), channel_id=1, source_target_pairs={{0,64},{64,128},{128,192},{192,0},{256,448},{320,256},{384,320},{4... | collective-permute-start | bytes 3080 | tf_op jit(solution)/shard_map/ppermute | solution.py:23
  148.5 7.7 %collective-permute-start.10 = (f32[4,2,128]{2,1,0:T(2,128)S(1)}, f32[4,2,128]{2,1,0:T(2,128)S(1)}, u32[]{:S(2)}, u32[]{:S(2)}) collective-permute-start(f32[4,2,128]{2,1,0:T(2,128)S(1)} %pad_maximum_fusion.7), channel_id=1, source_target_pairs={{0,256},{256,0},{1,257},{257,1},{2,258},{258,2},{3,259},{259,3},{4... | collective-permute-start | bytes 12296 | tf_op jit(solution)/shard_map/ppermute | solution.py:17
  161.7 142.3 %all-gather.5.cloned.1.call-start = ((), (), s32[]{:S(2)}) async-start(), calls=%async_computation.4 | async-start | bytes 5013504 | tf_op jit(solution)/shard_map/all_gather | solution.py:116
  223.1 84.2 %slice-start = ((s8[4718592]{0:T(1024)(128)(4,1)}), s8[524288]{0:T(1024)(128)(4,1)S(1)}, s32[]{:S(2)}) async-start(s8[4718592]{0:T(1024)(128)(4,1)} %bitcast.130), calls=%async_computation.5 | async-start | bytes 1048576
  309.4 23.0 %collective-permute-start.13 = (bf16[16,64,128]{2,1,0:T(8,128)(2,1)S(1)}, bf16[16,64,128]{2,1,0:T(8,128)(2,1)S(1)}, u32[]{:S(2)}, u32[]{:S(2)}) collective-permute-start(bf16[16,64,128]{2,1,0:T(8,128)(2,1)S(1)} %fusion.13), channel_id=1, source_target_pairs={{0,3},{1,0},{2,1},{3,2},{4,7},{5,4},{6,5},{7,6},{8,11},{9,8},{10,9... | collective-permute-start | bytes 786440 | tf_op jit(solution)/shard_map/ppermute | solution.py:58
  313.9 18.6 %collective-permute-start.12 = (bf16[16,64,128]{2,1,0:T(8,128)(2,1)S(1)}, bf16[16,64,128]{2,1,0:T(8,128)(2,1)S(1)}, u32[]{:S(2)}, u32[]{:S(2)}) collective-permute-start(bf16[16,64,128]{2,1,0:T(8,128)(2,1)S(1)} %fusion.13), channel_id=1, source_target_pairs={{0,1},{1,2},{2,3},{3,0},{4,5},{5,6},{6,7},{7,4},{8,9},{9,10},{10,1... | collective-permute-start | bytes 786440 | tf_op jit(solution)/shard_map/ppermute | solution.py:58
  315.8 16.7 %collective-permute-start.11 = (bf16[16,64,128]{2,1,0:T(8,128)(2,1)S(1)}, bf16[16,64,128]{2,1,0:T(8,128)(2,1)S(1)}, u32[]{:S(2)}, u32[]{:S(2)}) collective-permute-start(bf16[16,64,128]{2,1,0:T(8,128)(2,1)S(1)} %fusion.13), channel_id=1, source_target_pairs={{0,2},{1,3},{2,0},{3,1},{4,6},{5,7},{6,4},{7,5},{8,10},{9,11},{10,... | collective-permute-start | bytes 786440 | tf_op jit(solution)/shard_map/ppermute | solution.py:58
  321.4 21.9 %collective-permute-start.22 = (bf16[4,2,128,1152]{3,2,1,0:T(8,128)(2,1)S(1)}, bf16[4,2,128,1152]{3,2,1,0:T(8,128)(2,1)S(1)}, u32[]{:S(2)}, u32[]{:S(2)}) collective-permute-start(bf16[4,2,128,1152]{3,2,1,0:T(8,128)(2,1)S(1)} %bitcast.142), channel_id=1, source_target_pairs={{0,256},{256,0},{1,257},{257,1},{2,258},{258,2},{3,259},{259,3},{4... | collective-permute-start | bytes 7077896 | tf_op jit(solution)/shard_map/ppermute | solution.py:17
  335.0 12.6 %collective-permute-start.14 = (bf16[4,2,128,1152]{3,2,1,0:T(8,128)(2,1)S(1)}, bf16[4,2,128,1152]{3,2,1,0:T(8,128)(2,1)S(1)}, u32[]{:S(2)}, u32[]{:S(2)}) collective-permute-start(bf16[4,2,128,1152]{3,2,1,0:T(8,128)(2,1)S(1)} %bitcast.143), channel_id=1, source_target_pairs={{0,256},{256,0},{1,257},{257,1},{2,258},{258,2},{3,259},{259,3},{4... | collective-permute-start | bytes 7077896 | tf_op jit(solution)/shard_map/ppermute | solution.py:17
  339.2 4.1 %collective-permute-start.18 = (f32[4,2,128]{2,1,0:T(2,128)S(1)}, f32[4,2,128]{2,1,0:T(2,128)S(1)}, u32[]{:S(2)}, u32[]{:S(2)}) collective-permute-start(f32[4,2,128]{2,1,0:T(2,128)S(1)} %bitcast.157), channel_id=1, source_target_pairs={{0,256},{256,0},{1,257},{257,1},{2,258},{258,2},{3,259},{259,3},{4... | collective-permute-start | bytes 12296 | tf_op jit(solution)/shard_map/ppermute | solution.py:17
  344.1 11.8 %collective-permute-start.23 = (bf16[2,128,1152]{2,1,0:T(8,128)(2,1)S(1)}, bf16[2,128,1152]{2,1,0:T(8,128)(2,1)S(1)}, u32[]{:S(2)}, u32[]{:S(2)}) collective-permute-start(bf16[2,128,1152]{2,1,0:T(8,128)(2,1)S(1)} %get-tuple-element.15), channel_id=1, source_target_pairs={{0,192},{64,0},{128,64},{192,128},{256,320},{320,384},{384,448},{4... | collective-permute-start | bytes 1769480 | tf_op jit(solution)/shard_map/ppermute | solution.py:23
  348.4 13.9 %collective-permute-start.15 = (bf16[2,128,1152]{2,1,0:T(8,128)(2,1)S(1)}, bf16[2,128,1152]{2,1,0:T(8,128)(2,1)S(1)}, u32[]{:S(2)}, u32[]{:S(2)}) collective-permute-start(bf16[2,128,1152]{2,1,0:T(8,128)(2,1)S(1)} %get-tuple-element.17), channel_id=1, source_target_pairs={{0,192},{64,0},{128,64},{192,128},{256,320},{320,384},{384,448},{4... | collective-permute-start | bytes 1769480 | tf_op jit(solution)/shard_map/ppermute | solution.py:23
  356.2 41.3 %collective-permute-start.24 = (bf16[2,2,128,1152]{3,2,1,0:T(8,128)(2,1)S(1)}, bf16[2,2,128,1152]{3,2,1,0:T(8,128)(2,1)S(1)}, u32[]{:S(2)}, u32[]{:S(2)}) collective-permute-start(bf16[2,2,128,1152]{3,2,1,0:T(8,128)(2,1)S(1)} %pad_maximum_fusion.5), channel_id=1, source_target_pairs={{0,192},{64,0},{128,64},{192,128},{256,320},{320,384},{384,448},{4... | collective-permute-start | bytes 3538952 | tf_op jit(solution)/shard_map/ppermute | solution.py:23
  362.5 37.0 %collective-permute-start.16 = (bf16[2,2,128,1152]{3,2,1,0:T(8,128)(2,1)S(1)}, bf16[2,2,128,1152]{3,2,1,0:T(8,128)(2,1)S(1)}, u32[]{:S(2)}, u32[]{:S(2)}) collective-permute-start(bf16[2,2,128,1152]{3,2,1,0:T(8,128)(2,1)S(1)} %pad_maximum_fusion.4), channel_id=1, source_target_pairs={{0,192},{64,0},{128,64},{192,128},{256,320},{320,384},{384,448},{4... | collective-permute-start | bytes 3538952 | tf_op jit(solution)/shard_map/ppermute | solution.py:23
  364.9 22.6 %collective-permute-start.19 = (f32[2,128]{1,0:T(2,128)S(1)}, f32[2,128]{1,0:T(2,128)S(1)}, u32[]{:S(2)}, u32[]{:S(2)}) collective-permute-start(f32[2,128]{1,0:T(2,128)S(1)} %get-tuple-element.25), channel_id=1, source_target_pairs={{0,192},{64,0},{128,64},{192,128},{256,320},{320,384},{384,448},{4... | collective-permute-start | bytes 3080 | tf_op jit(solution)/shard_map/ppermute | solution.py:23
  387.6 5.5 %collective-permute-start.20 = (f32[2,2,128]{2,1,0:T(2,128)S(1)}, f32[2,2,128]{2,1,0:T(2,128)S(1)}, u32[]{:S(2)}, u32[]{:S(2)}) collective-permute-start(f32[2,2,128]{2,1,0:T(2,128)S(1)} %pad_maximum_fusion.9), channel_id=1, source_target_pairs={{0,192},{64,0},{128,64},{192,128},{256,320},{320,384},{384,448},{4... | collective-permute-start | bytes 6152 | tf_op jit(solution)/shard_map/ppermute | solution.py:23
  393.1 8.9 %collective-permute-start.21 = (f32[2,128]{1,0:T(2,128)S(1)}, f32[2,128]{1,0:T(2,128)S(1)}, u32[]{:S(2)}, u32[]{:S(2)}) collective-permute-start(f32[2,128]{1,0:T(2,128)S(1)} %slice_bitcast_fusion.7), channel_id=1, source_target_pairs={{0,256},{256,0},{1,257},{257,1},{2,258},{258,2},{3,259},{259,3},{4... | collective-permute-start | bytes 3080 | tf_op jit(solution)/shard_map/ppermute | solution.py:17
  397.6 5.0 %collective-permute-start.25 = (bf16[2,128,1152]{2,1,0:T(8,128)(2,1)S(1)}, bf16[2,128,1152]{2,1,0:T(8,128)(2,1)S(1)}, u32[]{:S(2)}, u32[]{:S(2)}) collective-permute-start(bf16[2,128,1152]{2,1,0:T(8,128)(2,1)S(1)} %slice_bitcast_fusion.1), channel_id=1, source_target_pairs={{0,256},{256,0},{1,257},{257,1},{2,258},{258,2},{3,259},{259,3},{4... | collective-permute-start | bytes 1769480 | tf_op jit(solution)/shard_map/ppermute | solution.py:17
  399.6 4.0 collective-permute-start.17
  (18 other events, 253.5 us)
Sparse Core Ops, SparseCore 0:
  23.6 72.6 all-gather.2
  161.8 59.3 reduce-scatter.1
  223.9 80.0 all-gather.4

commit v2 on v1

v2 whole, which is shorter than its diff:
```python
import jax
import jax.numpy as jnp
from jax import lax
from jax.sharding import Mesh, PartitionSpec as P

BLOCKS = 64
L1_COEF = 0.2
CAP = 4
NY = 4
NZ = 16

F32 = jnp.float32
BF16 = jnp.bfloat16


def swap_cores(v):
    return lax.ppermute(v, "sect", [(0, 1), (1, 0)])


def y_ring(v, step):
    perm = [(y, (y + step) % NY) for y in range(NY)]
    perm += [(NY + y, NY + (y - step) % NY) for y in range(NY)]
    return lax.ppermute(v, ("sect", "y"), perm)


def gather_blocks(own):
    chip = jnp.stack([own, swap_cores(own)])
    near = y_ring(chip, 1)
    far = y_ring(near[0], 1)
    half = jnp.concatenate([own[None], near, far[None]])
    return half, swap_cores(half)


def scatter_blocks(half, other):
    other = swap_cores(other)
    away = y_ring((half[2:].astype(F32) + other[2:].astype(F32)).astype(half.dtype), -1)
    near = half[1].astype(F32) + other[1].astype(F32) + away[1].astype(F32)
    near = y_ring(near.astype(half.dtype), -1)
    own = half[0].astype(F32) + other[0].astype(F32) + swap_cores(away[0]).astype(F32)
    return own + near.astype(F32)


def peer_place(owner_sect, owner_y):
    sect, y = lax.axis_index("sect"), lax.axis_index("y")
    other = owner_sect ^ sect
    delta = owner_y - y
    delta = jnp.where(sect == 0, delta, -delta) & 3
    code = delta * 2 + other
    place = jnp.zeros_like(code)
    for at, value in enumerate((0, 4, 6, 5, 3, 7, 1, 2)):
        place = jnp.where(code == at, value, place)
    return place


def sum_lat(part):
    part = part.astype(BF16)
    copies = lax.all_to_all(jnp.broadcast_to(part[None], (4,) + part.shape), "lat", 0, 0)
    return jnp.sum(copies.astype(F32), 0)


def routing(place, local):
    sources, _, toks = place.shape
    named = jnp.sum(
        (place[:, :, None, :] == jnp.arange(local, dtype=jnp.int32)[None, None, :, None]).astype(F32), 1
    )
    before = (jnp.arange(toks)[:, None] < jnp.arange(toks)[None, :]).astype(BF16)
    rank = jnp.einsum("skt,tu->sku", named.astype(BF16), before, preferred_element_type=F32)
    slot = rank + CAP * (jnp.arange(sources, dtype=jnp.int32) % 2).astype(F32)[:, None, None]
    slot = jnp.where(named > 0, slot, -1.0)
    slot = slot.reshape(sources // 2, 2, local, toks).transpose(0, 2, 1, 3)
    slot = slot.reshape(sources // 2, local, 2 * toks)
    return (
        slot[:, :, None, :] == jnp.arange(2 * CAP, dtype=F32)[None, None, :, None]
    ).astype(BF16)


def to_slots(pick, v):
    taken = jnp.einsum("pkrt,ptd->kprd", pick, v, preferred_element_type=F32).astype(BF16)
    return taken.reshape(taken.shape[0], -1, taken.shape[3])


def shards(residuals, routes, blocks, enc_weight, enc_bias, dec_weight, dec_bias):
    tok_count, width = residuals.shape
    owned, latents, _ = enc_weight.shape
    local = 8 * owned
    half = local // 2
    pairs = NZ // 2
    sect, y, z = lax.axis_index("sect"), lax.axis_index("y"), lax.axis_index("z")

    def local_blocks(w):
        return [h.reshape(half, *w.shape[1:]) for h in gather_blocks(w)]

    rows = lax.all_gather(residuals, "z", axis=0, tiled=True).reshape(pairs, 2 * tok_count, width)

    global_block = (routes[:, None] * BLOCKS + blocks).T.reshape(1, 4, tok_count)
    ids = lax.all_to_all(
        jnp.broadcast_to(global_block, (NZ, 4, tok_count)), "z", 0, 0, tiled=True
    )
    bias_local = jnp.concatenate(local_blocks(enc_bias))
    ids, bias_local = lax.optimization_barrier((ids, bias_local))
    here = ((ids >> 1) & 15) == z
    place = jnp.where(here, peer_place(ids >> 7, (ids >> 5) & 3) * owned + (ids & 1), -1)
    pick = routing(place, local)
    present = jnp.sum(pick.astype(F32), axis=3).transpose(1, 0, 2).reshape(local, -1)

    enc_local = local_blocks(enc_weight)
    dec_local = local_blocks(dec_weight)

    def halves(v):
        return [to_slots(pick[:, :half], v), to_slots(pick[:, half:], v)]

    def into_latents(v, w):
        return jnp.concatenate(
            [
                jnp.einsum("krd,kld->krl", a, b, preferred_element_type=F32).astype(BF16)
                for a, b in zip(v, w)
            ]
        )

    pre = sum_lat(into_latents(halves(rows), enc_local)) + bias_local[:, None, :]
    act = jax.nn.softplus(pre).astype(BF16)
    act_halves = [act[:half], act[half:]]
    part = [
        jnp.einsum("krl,kld->krd", a, b, preferred_element_type=F32).astype(BF16)
        for a, b in zip(act_halves, dec_local)
    ]
    part = jnp.concatenate(part).reshape(local, pairs, 2 * CAP, width)
    home = jnp.einsum("pkrt,kprd->ptd", pick, part, preferred_element_type=F32).astype(BF16)
    home, rows, ids = lax.optimization_barrier((home, rows, ids))
    total = lax.psum_scatter(
        home.reshape(NZ * tok_count, width), "z", scatter_dimension=0, tiled=True
    )

    here = ((ids >> 1) & 15) == z
    straight = routing(jnp.where(here, (ids >> 5) * owned + (ids & 1), -1), local)
    owner_rows = lax.all_to_all(
        to_slots(straight, rows).reshape(8, owned, -1, width), ("sect", "y"), 0, 0, tiled=True
    )
    owner_rows = owner_rows.transpose(1, 0, 2, 3).reshape(owned, -1, width)

    total, owner_rows = lax.optimization_barrier((total, owner_rows))
    recon = total.astype(F32) + dec_bias[None, :]
    reconstruction = recon.astype(BF16)
    error = (recon - residuals.astype(F32)).astype(BF16)
    errors = lax.all_gather(error, "z", axis=0, tiled=True).reshape(pairs, 2 * tok_count, width)
    error_in = halves(errors)
    dact = into_latents(error_in, dec_local)
    error_in, dact = lax.optimization_barrier((error_in, dact))
    dact = sum_lat(dact)
    dec_part = [
        jnp.einsum("krl,krd->kld", a, b, preferred_element_type=F32)
        .astype(BF16)
        .reshape(4, owned, latents, width)
        for a, b in zip(act_halves, error_in)
    ]
    dec_grad = scatter_blocks(*dec_part).astype(BF16)
    slope = ((dact + L1_COEF * present[..., None]) * jax.nn.sigmoid(pre)).astype(BF16)
    peers = jnp.arange(8, dtype=jnp.int32)
    order = (peer_place(peers >> 2, peers & 3)[:, None] == peers[None, :]).astype(BF16)
    slope = jnp.einsum(
        "ap,pm->am", order, slope.reshape(8, -1), preferred_element_type=F32
    ).astype(BF16)
    owner_slope = lax.all_to_all(
        slope.reshape(8, owned, -1, latents), ("sect", "y"), 0, 0, tiled=True
    )
    owner_slope = owner_slope.transpose(1, 0, 2, 3).reshape(owned, -1, latents)
    enc_bias_grad = jnp.sum(owner_slope.astype(F32), 1)
    enc_grad = jnp.einsum(
        "brl,brd->bld", owner_slope, owner_rows, preferred_element_type=F32
    ).astype(BF16)
    return reconstruction, enc_grad, enc_bias_grad, dec_grad


def solution(mesh):
    fine = Mesh(mesh.devices.reshape(2, NY, NZ, 4), ("sect", "y", "z", "lat"))
    own = ("sect", "y", "z")
    return jax.shard_map(
        shards,
        mesh=fine,
        in_specs=(
            P(own, "lat"),
            P(own),
            P(own, None),
            P(own, None, "lat"),
            P(own, None),
            P(own, None, "lat"),
            P("lat"),
        ),
        out_specs=(
            P(own, "lat"),
            P(own, None, "lat"),
            P(own, None),
            P(own, None, "lat"),
        ),
        check_vma=False,
    )
```

time: 412 us -> 361 us (0.88)
  waiting for transfers between devices: 227 us -> 140 us
  blocking collectives: 0 us -> 52.5 us
  starting transfers between devices: 108 us -> 82.3 us
  matrix products: 22.3 us -> 34.8 us
  other arithmetic: 22.9 us -> 18.6 us
    all_to_all x0 -> x2, blocking collectives: none -> 52.5 us  [the longest x1 36.1 us: shards(): lax.all_to_all(to_slots(straight, rows).reshape(8, owned, -1, width), ('s...]
    ppermute x10 -> x8, waiting for transfers between devices: 74.6 us -> 25.7 us  [y_ring(): return lax.ppermute(v, ('sect', 'y'), perm)]
    reduce_scatter x1, waiting for transfers between devices: 59.5 us -> 24.1 us  [shards(): lax.psum_scatter(home.reshape(NZ * tok_count, width), 'z', scatter_dimens...]
    ppermute x6 -> x0, starting transfers between devices: 19.7 us -> none  [sum_lat(): lax.ppermute(part, 'lat', [(i, (i + k) % 4) for i in range(4)]).astype(F32)]
    all_to_all x1 -> x3, starting transfers between devices: 9.54 us -> 18.8 us  [the longest x1 9.54 us: shards(): lax.all_to_all(jnp.broadcast_to(global_block, (NZ, 4, tok_count)), 'z', 0...]
    ppermute x10 -> x8, starting transfers between devices: 28.4 us -> 19.4 us  [y_ring(): return lax.ppermute(v, ('sect', 'y'), perm)]
    slice x4 -> x1, local copies, waits for them, and re-layouts: 8.1 us -> 0.09 us  [scatter_blocks(): half[2:].astype(F32) + other[2:].astype(F32)]
    dot_general x6 -> x12, matrix products: 11.6 us -> 18.4 us  [the longest x4 9.02 us: into_latents(): jnp.einsum('krd,kld->krl', a, b, preferred_element_type=F32).astype(BF16)]
  transfers between devices with their start and end apart: 30 -> 22, of which waited for: 13 -> 10; matrix products, arithmetic and copies ran while one was open for 11% -> 12% of each run, Pallas kernels for 0% -> 0%
where the time goes in v2:
time: 361 us; the launch traced here: 356 us
  waiting for transfers between devices  140 us (39%)
  starting transfers between devices  82.3 us (23%)
  blocking collectives  52.5 us (15%)
  matrix products  34.8 us (10%)
  other arithmetic  18.6 us (5%)
  between operations  14.4 us (4%)
  local copies, waits for them, and re-layouts  13.9 us (4%)
    all_gather x1, waiting for transfers between devices, shards(): lax.all_gather(error, 'z', axis=0, tiled=True)  80.1 us
    ppermute x8, starting transfers between devices, swap_cores(): return lax.ppermute(v, 'sect', [(0, 1), (1, 0)])  43.8 us
    all_to_all x1, blocking collectives, shards(): lax.all_to_all(to_slots(straight, rows).reshape(8, owned, -1, width), ('s...  36.1 us
    ppermute x8, waiting for transfers between devices, y_ring(): return lax.ppermute(v, ('sect', 'y'), perm)  25.7 us
    reduce_scatter x1, waiting for transfers between devices, shards(): lax.psum_scatter(home.reshape(NZ * tok_count, width), 'z', scatter_dimens...  24.1 us
    ppermute x8, starting transfers between devices, y_ring(): return lax.ppermute(v, ('sect', 'y'), perm)  19.4 us
    all_to_all x1, blocking collectives, sum_lat(): lax.all_to_all(jnp.broadcast_to(part[None], (4,) + part.shape), 'lat', 0, 0)  16.4 us
    dot_general x5, matrix products, to_slots(): jnp.einsum('pkrt,ptd->kprd', pick, v, preferred_element_type=F32)  12.8 us
  transfers between devices with their start and end apart: 22, of which 10 were waited for; matrix products, arithmetic and copies ran while one was open for 12% of the time, Pallas kernels for 0%

profile of v2, /device:TPU:1, one launch (start us, length us, event | category | flops | bytes accessed | tf_op | source)
XLA Modules:
  0.0 356.3 jit_solution(8212707684187134037)
XLA Ops:
  7.9 8.8 %collective-permute-start.4 = (bf16[2,128,1152]{2,1,0:T(8,128)(2,1)}, bf16[2,128,1152]{2,1,0:T(8,128)(2,1)S(1)}, u32[]{:S(2)}, u32[]{:S(2)}) collective-permute-start(bf16[2,128,1152]{2,1,0:T(8,128)(2,1)} %param.10), channel_id=1, source_target_pairs={{0,256},{256,0},{1,257},{257,1},{2,258},{258,2},{3,259},{259,3},{4... | collective-permute-start | bytes 1769480 | tf_op jit(solution)/shard_map/ppermute | solution.py:17
  26.2 11.1 %collective-permute-done.5 = bf16[2,2,128,1152]{3,2,1,0:T(8,128)(2,1)S(1)} collective-permute-done((bf16[2,2,128,1152]{3,2,1,0:T(8,128)(2,1)S(1)}, bf16[2,2,128,1152]{3,2,1,0:T(8,128)(2,1)S(1)}, u32[]{:S(2)}, u32[]{:S(2)}) %collective-permute-start.5) | collective-permute-done | bytes 1179680 | tf_op jit(solution)/shard_map/ppermute | solution.py:23
  37.3 2.7 collective-permute-start.6
  45.5 2.8 collective-permute-done.6
  48.6 6.2 %collective-permute-start.7 = (bf16[4,2,128,1152]{3,2,1,0:T(8,128)(2,1)S(1)}, bf16[4,2,128,1152]{3,2,1,0:T(8,128)(2,1)}, u32[]{:S(2)}, u32[]{:S(2)}) collective-permute-start(bf16[4,2,128,1152]{3,2,1,0:T(8,128)(2,1)S(1)} %pad_maximum_fusion), channel_id=1, source_target_pairs={{0,256},{256,0},{1,257},{257,1},{2,258},{258,2},{3,259},{259,3},{4... | collective-permute-start | bytes 7077896 | tf_op jit(solution)/shard_map/ppermute | solution.py:17
  55.5 9.5 %all-to-all-start = ((s32[16,4,128]{2,1,0:T(4,128)}), s32[16,4,128]{2,1,0:T(4,128)S(1)}, u32[]{:S(2)}, u32[]{:S(2)}) async-start(s32[16,4,128]{2,1,0:T(4,128)} %broadcast_in_dim.82), calls=%async_computation | async-start | bytes 65536 | tf_op jit(solution)/shard_map/all_to_all | solution.py:96
  65.1 2.8 collective-permute-start.2
  69.8 4.1 %collective-permute-start.3 = (f32[4,2,128]{2,1,0:T(2,128)S(1)}, f32[4,2,128]{2,1,0:T(2,128)S(1)}, u32[]{:S(2)}, u32[]{:S(2)}) collective-permute-start(f32[4,2,128]{2,1,0:T(2,128)S(1)} %pad_maximum_fusion.7), channel_id=1, source_target_pairs={{0,256},{256,0},{1,257},{257,1},{2,258},{258,2},{3,259},{259,3},{4... | collective-permute-start | bytes 12296 | tf_op jit(solution)/shard_map/ppermute | solution.py:17
  78.5 8.6 %collective-permute-done.10 = bf16[2,128,1152]{2,1,0:T(8,128)(2,1)} collective-permute-done((bf16[2,128,1152]{2,1,0:T(8,128)(2,1)}, bf16[2,128,1152]{2,1,0:T(8,128)(2,1)}, u32[]{:S(2)}, u32[]{:S(2)}) %collective-permute-start.10) | collective-permute-done | bytes 589856 | tf_op jit(solution)/shard_map/ppermute | solution.py:23
  87.2 3.2 pad_maximum_fusion.1
  90.4 4.0 %collective-permute-start.11 = (bf16[4,2,128,1152]{3,2,1,0:T(8,128)(2,1)}, bf16[4,2,128,1152]{3,2,1,0:T(8,128)(2,1)}, u32[]{:S(2)}, u32[]{:S(2)}) collective-permute-start(bf16[4,2,128,1152]{3,2,1,0:T(8,128)(2,1)} %pad_maximum_fusion.1), channel_id=1, source_target_pairs={{0,256},{256,0},{1,257},{257,1},{2,258},{258,2},{3,259},{259,3},{4... | collective-permute-start | bytes 7077896 | tf_op jit(solution)/shard_map/ppermute | solution.py:17
  94.5 3.3 fusion.9
  97.8 2.7 fusion.28
  102.6 16.4 %all_to_all.25 = bf16[4,16,64,128]{3,2,1,0:T(8,128)(2,1)S(1)} all-to-all(bf16[4,16,64,128]{3,2,1,0:T(8,128)(2,1)S(1)} %broadcast_in_dim.89), channel_id=1, replica_groups=mesh['sect'=2,'y'=4,'z'=16,'lat'=4] {'lat'}, dimensions={0} | all-to-all | bytes 2097152 | tf_op jit(solution)/shard_map/all_to_all | solution.py:57
  123.9 3.6 %bitcast_convert_fusion = bf16[8,256,1152]{2,1,0:T(8,128)(2,1)} fusion(f32[8,16,256]{2,1,0:T(8,128)S(1)} %eq.179, bf16[8,64,1152]{2,1,0:T(8,128)(2,1)S(1)} %convolution_convert_fusion.5, bf16[8,64,1152]{2,1,0:T(8,128)(2,1)S(1)} %convolution_convert_fusion.6), kind=kOutput, calls=%fused_computation.1 | convolution fusion | flops 607780864 | bytes 7208960 | tf_op jit(solution)/shard_map/pkrt,kprd->ptd/dot_general | solution.py:128
  128.2 4.6 %fusion.5 = bf16[16,8,8,1152]{3,0,2,1:T(8,128)(2,1)} fusion(bf16[8,256,1152]{2,1,0:T(8,128)(2,1)} %bitcast.142, f32[8,16,256]{2,1,0:T(8,128)S(1)} %eq.187), kind=kOutput, calls=%fused_computation.7 | convolution fusion | flops 605421568 | bytes 7208960 | tf_op jit(solution)/shard_map/pkrt,ptd->kprd/dot_general | solution.py:78
  132.8 4.8 %reshape_reshape.3 = bf16[8,2,64,1152]{3,1,0,2:T(2,128)(2,1)S(1)} reshape(bf16[16,8,8,1152]{3,0,2,1:T(8,128)(2,1)} %fusion.5) | data formatting | bytes 4718592 | tf_op jit(solution)/shard_map/reshape;reshape | solution.py:137
  139.3 36.1 %all_to_all.26 = bf16[8,2,64,1152]{3,1,2,0:T(2,128)(2,1)} all-to-all(bf16[8,2,64,1152]{3,1,2,0:T(2,128)(2,1)S(1)} %copy.46), channel_id=1, replica_groups=mesh['sect'=2,'y'=4,'z'=16,'lat'=4] {'sect','y'}, dimensions={0} | all-to-all | bytes 4718592 | tf_op jit(solution)/shard_map/all_to_all | solution.py:136
  175.4 24.1 %reduce-scatter.2.cloned.1.call-done = bf16[128,1152]{1,0:T(8,128)(2,1)} async-done(((bf16[2048,1152]{1,0:T(8,128)(2,1)}), bf16[128,1152]{1,0:T(8,128)(2,1)}) %reduce-scatter.2.cloned.1.call-update) | async-done | bytes 294928 | tf_op jit(solution)/shard_map/reduce_scatter | solution.py:130
  201.6 80.1 %all-gather.5.cloned.1.call-done = bf16[2048,1152]{1,0:T(8,128)(2,1)} async-done(((bf16[128,1152]{1,0:T(8,128)(2,1)}), bf16[2048,1152]{1,0:T(8,128)(2,1)}) %all-gather.5.cloned.1.call-update) | async-done | bytes 4718608 | tf_op jit(solution)/shard_map/all_gather | solution.py:145
  281.7 3.3 fusion.11
  286.2 2.7 convolution_convert_fusion.10
  289.1 2.7 convolution_convert_fusion.11
  294.1 10.5 %collective-permute-start.12 = (bf16[4,2,128,1152]{3,2,1,0:T(8,128)(2,1)}, bf16[4,2,128,1152]{3,2,1,0:T(8,128)(2,1)}, u32[]{:S(2)}, u32[]{:S(2)}) collective-permute-start(bf16[4,2,128,1152]{3,2,1,0:T(8,128)(2,1)} %bitcast.56), channel_id=1, source_target_pairs={{0,256},{256,0},{1,257},{257,1},{2,258},{258,2},{3,259},{259,3},{4... | collective-permute-start | bytes 7077896 | tf_op jit(solution)/shard_map/ppermute | solution.py:17
  305.9 3.7 %all-to-all-start.3 = ((bf16[4,16,64,128]{3,2,1,0:T(8,128)(2,1)}), bf16[4,16,64,128]{3,2,1,0:T(8,128)(2,1)S(1)}, u32[]{:S(2)}, u32[]{:S(2)}) async-start(bf16[4,16,64,128]{3,2,1,0:T(8,128)(2,1)} %broadcast_in_dim.93), calls=%async_computation.4 | async-start | bytes 2097152 | tf_op jit(solution)/shard_map/all_to_all | solution.py:57
  310.6 3.4 fusion.12
  313.9 3.1 collective-permute-start.13
  317.4 7.2 %all-to-all-done.3 = bf16[4,16,64,128]{3,2,1,0:T(8,128)(2,1)S(1)} async-done(((bf16[4,16,64,128]{3,2,1,0:T(8,128)(2,1)}), bf16[4,16,64,128]{3,2,1,0:T(8,128)(2,1)S(1)}, u32[]{:S(2)}, u32[]{:S(2)}) %all-to-all-start.3) | async-done | bytes 1048608 | tf_op jit(solution)/shard_map/all_to_all | solution.py:57
  326.1 5.6 %all-to-all-start.4 = ((bf16[8,2,64,128]{3,2,1,0:T(8,128)(2,1)}), bf16[8,2,64,128]{3,2,1,0:T(8,128)(2,1)S(1)}, u32[]{:S(2)}, u32[]{:S(2)}) async-start(bf16[8,2,64,128]{3,2,1,0:T(8,128)(2,1)} %copy.51), calls=%async_computation.5 | async-start | bytes 524288 | tf_op jit(solution)/shard_map/all_to_all | solution.py:163
  334.9 2.5 collective-permute-start.15
  338.5 5.8 %collective-permute-start.14 = (bf16[2,128,1152]{2,1,0:T(8,128)(2,1)S(1)}, bf16[2,128,1152]{2,1,0:T(8,128)(2,1)}, u32[]{:S(2)}, u32[]{:S(2)}) collective-permute-start(bf16[2,128,1152]{2,1,0:T(8,128)(2,1)S(1)} %slice_bitcast_fusion.2), channel_id=1, source_target_pairs={{0,256},{256,0},{1,257},{257,1},{2,258},{258,2},{3,259},{259,3},{4... | collective-permute-start | bytes 1769480 | tf_op jit(solution)/shard_map/ppermute | solution.py:17
  347.0 2.7 fusion.18
  (109 shorter events, 49.1 us)
Async XLA Ops:
  7.2 14.6 %copy-start.1 = (bf16[2,128,1152]{2,1,0:T(8,128)(2,1)S(1)}, bf16[2,128,1152]{2,1,0:T(8,128)(2,1)}, u32[]{:S(2)}) copy-start(bf16[2,128,1152]{2,1,0:T(8,128)(2,1)} %param.12) | copy-start | bytes 1769476
  7.2 16.9 %copy-start.6 = (f32[2,128]{1,0:T(2,128)S(1)}, f32[2,128]{1,0:T(2,128)}, u32[]{:S(2)}) copy-start(f32[2,128]{1,0:T(2,128)} %param.11) | copy-start | bytes 3076
  7.2 87.2 %all-gather.3.cloned.1.call-start = ((), (), s32[]{:S(2)}) async-start(), calls=%async_computation.6 | async-start | bytes 5013504 | tf_op jit(solution)/shard_map/all_gather | solution.py:93
  7.9 10.6 %collective-permute-start.4 = (bf16[2,128,1152]{2,1,0:T(8,128)(2,1)}, bf16[2,128,1152]{2,1,0:T(8,128)(2,1)S(1)}, u32[]{:S(2)}, u32[]{:S(2)}) collective-permute-start(bf16[2,128,1152]{2,1,0:T(8,128)(2,1)} %param.10), channel_id=1, source_target_pairs={{0,256},{256,0},{1,257},{257,1},{2,258},{258,2},{3,259},{259,3},{4... | collective-permute-start | bytes 1769480 | tf_op jit(solution)/shard_map/ppermute | solution.py:17
  19.7 23.5 %copy-start.9 = (s32[128]{0:T(128)S(1)}, s32[128]{0:T(128)}, u32[]{:S(2)}) copy-start(s32[128]{0:T(128)} %param.8) | copy-start | bytes 1540
  19.7 28.6 %copy-start = (bf16[2,128,1152]{2,1,0:T(8,128)(2,1)S(1)}, bf16[2,128,1152]{2,1,0:T(8,128)(2,1)}, u32[]{:S(2)}) copy-start(bf16[2,128,1152]{2,1,0:T(8,128)(2,1)} %param.10) | copy-start | bytes 1769476
  19.7 17.5 %collective-permute-start.5 = (bf16[2,2,128,1152]{3,2,1,0:T(8,128)(2,1)S(1)}, bf16[2,2,128,1152]{3,2,1,0:T(8,128)(2,1)S(1)}, u32[]{:S(2)}, u32[]{:S(2)}) collective-permute-start(bf16[2,2,128,1152]{3,2,1,0:T(8,128)(2,1)S(1)} %pad_maximum_fusion.2), channel_id=1, source_target_pairs={{0,64},{64,128},{128,192},{192,0},{256,448},{320,256},{384,320},{4... | collective-permute-start | bytes 3538952 | tf_op jit(solution)/shard_map/ppermute | solution.py:23
  21.8 18.2 %collective-permute-start.8 = (bf16[2,128,1152]{2,1,0:T(8,128)(2,1)S(1)}, bf16[2,128,1152]{2,1,0:T(8,128)(2,1)S(1)}, u32[]{:S(2)}, u32[]{:S(2)}) collective-permute-start(bf16[2,128,1152]{2,1,0:T(8,128)(2,1)S(1)} %copy-done.1), channel_id=1, source_target_pairs={{0,256},{256,0},{1,257},{257,1},{2,258},{258,2},{3,259},{259,3},{4... | collective-permute-start | bytes 1769480 | tf_op jit(solution)/shard_map/ppermute | solution.py:17
  24.1 19.1 %collective-permute-start = (f32[2,128]{1,0:T(2,128)S(1)}, f32[2,128]{1,0:T(2,128)S(1)}, u32[]{:S(2)}, u32[]{:S(2)}) collective-permute-start(f32[2,128]{1,0:T(2,128)S(1)} %copy-done.6), channel_id=1, source_target_pairs={{0,256},{256,0},{1,257},{257,1},{2,258},{258,2},{3,259},{259,3},{4... | collective-permute-start | bytes 3080 | tf_op jit(solution)/shard_map/ppermute | solution.py:17
  37.3 11.0 %collective-permute-start.6 = (bf16[2,128,1152]{2,1,0:T(8,128)(2,1)S(1)}, bf16[2,128,1152]{2,1,0:T(8,128)(2,1)S(1)}, u32[]{:S(2)}, u32[]{:S(2)}) collective-permute-start(bf16[2,128,1152]{2,1,0:T(8,128)(2,1)S(1)} %slice_bitcast_fusion.5), channel_id=1, source_target_pairs={{0,64},{64,128},{128,192},{192,0},{256,448},{320,256},{384,320},{4... | collective-permute-start | bytes 1769480 | tf_op jit(solution)/shard_map/ppermute | solution.py:23
  41.3 32.7 %collective-permute-start.9 = (bf16[2,2,128,1152]{3,2,1,0:T(8,128)(2,1)}, bf16[2,2,128,1152]{3,2,1,0:T(8,128)(2,1)}, u32[]{:S(2)}, u32[]{:S(2)}) collective-permute-start(bf16[2,2,128,1152]{3,2,1,0:T(8,128)(2,1)} %pad_maximum_fusion.3), channel_id=1, source_target_pairs={{0,64},{64,128},{128,192},{192,0},{256,448},{320,256},{384,320},{4... | collective-permute-start | bytes 3538952 | tf_op jit(solution)/shard_map/ppermute | solution.py:23
  43.2 21.9 %collective-permute-start.1 = (f32[2,2,128]{2,1,0:T(2,128)S(1)}, f32[2,2,128]{2,1,0:T(2,128)S(1)}, u32[]{:S(2)}, u32[]{:S(2)}) collective-permute-start(f32[2,2,128]{2,1,0:T(2,128)S(1)} %pad_maximum_fusion.8), channel_id=1, source_target_pairs={{0,64},{64,128},{128,192},{192,0},{256,448},{320,256},{384,320},{4... | collective-permute-start | bytes 6152 | tf_op jit(solution)/shard_map/ppermute | solution.py:23
  48.3 6.6 %copy-start.7 = (s32[128,4]{0,1:T(4,128)S(1)}, s32[128,4]{0,1:T(4,128)}, u32[]{:S(2)}) copy-start(s32[128,4]{0,1:T(4,128)} %param.9) | copy-start | bytes 6148
  48.6 49.1 %collective-permute-start.7 = (bf16[4,2,128,1152]{3,2,1,0:T(8,128)(2,1)S(1)}, bf16[4,2,128,1152]{3,2,1,0:T(8,128)(2,1)}, u32[]{:S(2)}, u32[]{:S(2)}) collective-permute-start(bf16[4,2,128,1152]{3,2,1,0:T(8,128)(2,1)S(1)} %pad_maximum_fusion), channel_id=1, source_target_pairs={{0,256},{256,0},{1,257},{257,1},{2,258},{258,2},{3,259},{259,3},{4... | collective-permute-start | bytes 7077896 | tf_op jit(solution)/shard_map/ppermute | solution.py:17
  55.5 22.5 %all-to-all-start = ((s32[16,4,128]{2,1,0:T(4,128)}), s32[16,4,128]{2,1,0:T(4,128)S(1)}, u32[]{:S(2)}, u32[]{:S(2)}) async-start(s32[16,4,128]{2,1,0:T(4,128)} %broadcast_in_dim.82), calls=%async_computation | async-start | bytes 65536 | tf_op jit(solution)/shard_map/all_to_all | solution.py:96
  65.0 134.5 %reduce-scatter.2.cloned.1.call-start = ((), (), s32[]{:S(2)}) async-start(), calls=%async_computation.7 | async-start | bytes 5013504 | tf_op jit(solution)/shard_map/reduce_scatter | solution.py:130
  65.1 4.7 %collective-permute-start.2 = (f32[2,128]{1,0:T(2,128)S(1)}, f32[2,128]{1,0:T(2,128)S(1)}, u32[]{:S(2)}, u32[]{:S(2)}) collective-permute-start(f32[2,128]{1,0:T(2,128)S(1)} %slice_bitcast_fusion.6), channel_id=1, source_target_pairs={{0,64},{64,128},{128,192},{192,0},{256,448},{320,256},{384,320},{4... | collective-permute-start | bytes 3080 | tf_op jit(solution)/shard_map/ppermute | solution.py:23
  69.8 8.2 %collective-permute-start.3 = (f32[4,2,128]{2,1,0:T(2,128)S(1)}, f32[4,2,128]{2,1,0:T(2,128)S(1)}, u32[]{:S(2)}, u32[]{:S(2)}) collective-permute-start(f32[4,2,128]{2,1,0:T(2,128)S(1)} %pad_maximum_fusion.7), channel_id=1, source_target_pairs={{0,256},{256,0},{1,257},{257,1},{2,258},{258,2},{3,259},{259,3},{4... | collective-permute-start | bytes 12296 | tf_op jit(solution)/shard_map/ppermute | solution.py:17
  75.9 11.2 %collective-permute-start.10 = (bf16[2,128,1152]{2,1,0:T(8,128)(2,1)}, bf16[2,128,1152]{2,1,0:T(8,128)(2,1)}, u32[]{:S(2)}, u32[]{:S(2)}) collective-permute-start(bf16[2,128,1152]{2,1,0:T(8,128)(2,1)} %slice_bitcast_fusion.4), channel_id=1, source_target_pairs={{0,64},{64,128},{128,192},{192,0},{256,448},{320,256},{384,320},{4... | collective-permute-start | bytes 1769480 | tf_op jit(solution)/shard_map/ppermute | solution.py:23
  90.4 29.2 %collective-permute-start.11 = (bf16[4,2,128,1152]{3,2,1,0:T(8,128)(2,1)}, bf16[4,2,128,1152]{3,2,1,0:T(8,128)(2,1)}, u32[]{:S(2)}, u32[]{:S(2)}) collective-permute-start(bf16[4,2,128,1152]{3,2,1,0:T(8,128)(2,1)} %pad_maximum_fusion.1), channel_id=1, source_target_pairs={{0,256},{256,0},{1,257},{257,1},{2,258},{258,2},{3,259},{259,3},{4... | collective-permute-start | bytes 7077896 | tf_op jit(solution)/shard_map/ppermute | solution.py:17
  94.4 6.0 %slice-start = ((s8[4718592]{0:T(1024)(128)(4,1)}), s8[4194304]{0:T(1024)(128)(4,1)S(1)}, s32[]{:S(2)}) async-start(s8[4718592]{0:T(1024)(128)(4,1)} %bitcast.143), calls=%async_computation.9 | async-start | bytes 8388608
  94.4 6.0 %slice-start.1 = ((s8[4718592]{0:T(1024)(128)(4,1)}), s8[524288]{0:T(1024)(128)(4,1)S(1)}, s32[]{:S(2)}) async-start(s8[4718592]{0:T(1024)(128)(4,1)} %bitcast.143), calls=%async_computation.10 | async-start | bytes 1048576
  127.6 154.1 %all-gather.5.cloned.1.call-start = ((), (), s32[]{:S(2)}) async-start(), calls=%async_computation.8 | async-start | bytes 5013504 | tf_op jit(solution)/shard_map/all_gather | solution.py:145
  139.3 60.2 %copy-start.4 = (bf16[128,1152]{1,0:T(8,128)(2,1)S(1)}, bf16[128,1152]{1,0:T(8,128)(2,1)}, u32[]{:S(2)}) copy-start(bf16[128,1152]{1,0:T(8,128)(2,1)} %param.7) | copy-start | bytes 884740
  139.3 60.2 %copy-start.5 = (f32[1152]{0:T(1024)S(1)}, f32[1152]{0:T(1024)}, u32[]{:S(2)}) copy-start(f32[1152]{0:T(1024)} %param.13) | copy-start | bytes 13828
  294.1 16.4 %collective-permute-start.12 = (bf16[4,2,128,1152]{3,2,1,0:T(8,128)(2,1)}, bf16[4,2,128,1152]{3,2,1,0:T(8,128)(2,1)}, u32[]{:S(2)}, u32[]{:S(2)}) collective-permute-start(bf16[4,2,128,1152]{3,2,1,0:T(8,128)(2,1)} %bitcast.56), channel_id=1, source_target_pairs={{0,256},{256,0},{1,257},{257,1},{2,258},{258,2},{3,259},{259,3},{4... | collective-permute-start | bytes 7077896 | tf_op jit(solution)/shard_map/ppermute | solution.py:17
  305.9 18.7 %all-to-all-start.3 = ((bf16[4,16,64,128]{3,2,1,0:T(8,128)(2,1)}), bf16[4,16,64,128]{3,2,1,0:T(8,128)(2,1)S(1)}, u32[]{:S(2)}, u32[]{:S(2)}) async-start(bf16[4,16,64,128]{3,2,1,0:T(8,128)(2,1)} %broadcast_in_dim.93), calls=%async_computation.4 | async-start | bytes 2097152 | tf_op jit(solution)/shard_map/all_to_all | solution.py:57
  313.9 18.5 %collective-permute-start.13 = (bf16[2,2,128,1152]{3,2,1,0:T(8,128)(2,1)}, bf16[2,2,128,1152]{3,2,1,0:T(8,128)(2,1)}, u32[]{:S(2)}, u32[]{:S(2)}) collective-permute-start(bf16[2,2,128,1152]{3,2,1,0:T(8,128)(2,1)} %fusion.12), channel_id=1, source_target_pairs={{0,192},{64,0},{128,64},{192,128},{256,320},{320,384},{384,448},{4... | collective-permute-start | bytes 3538952 | tf_op jit(solution)/shard_map/ppermute | solution.py:23
  326.1 18.9 %copy-start.2 = (bf16[8,2,64,1152]{3,1,2,0:T(2,128)(2,1)S(1)}, bf16[8,2,64,1152]{3,1,2,0:T(2,128)(2,1)}, u32[]{:S(2)}) copy-start(bf16[8,2,64,1152]{3,1,2,0:T(2,128)(2,1)} %all_to_all.26) | copy-start | bytes 7077892
  326.1 18.3 %all-to-all-start.4 = ((bf16[8,2,64,128]{3,2,1,0:T(8,128)(2,1)}), bf16[8,2,64,128]{3,2,1,0:T(8,128)(2,1)S(1)}, u32[]{:S(2)}, u32[]{:S(2)}) async-start(bf16[8,2,64,128]{3,2,1,0:T(8,128)(2,1)} %copy.51), calls=%async_computation.5 | async-start | bytes 524288 | tf_op jit(solution)/shard_map/all_to_all | solution.py:163
  334.9 12.1 %collective-permute-start.15 = (bf16[2,128,1152]{2,1,0:T(8,128)(2,1)}, bf16[2,128,1152]{2,1,0:T(8,128)(2,1)}, u32[]{:S(2)}, u32[]{:S(2)}) collective-permute-start(bf16[2,128,1152]{2,1,0:T(8,128)(2,1)} %fusion.15), channel_id=1, source_target_pairs={{0,192},{64,0},{128,64},{192,128},{256,320},{320,384},{384,448},{4... | collective-permute-start | bytes 1769480 | tf_op jit(solution)/shard_map/ppermute | solution.py:23
  338.5 8.5 %collective-permute-start.14 = (bf16[2,128,1152]{2,1,0:T(8,128)(2,1)S(1)}, bf16[2,128,1152]{2,1,0:T(8,128)(2,1)}, u32[]{:S(2)}, u32[]{:S(2)}) collective-permute-start(bf16[2,128,1152]{2,1,0:T(8,128)(2,1)S(1)} %slice_bitcast_fusion.2), channel_id=1, source_target_pairs={{0,256},{256,0},{1,257},{257,1},{2,258},{258,2},{3,259},{259,3},{4... | collective-permute-start | bytes 1769480 | tf_op jit(solution)/shard_map/ppermute | solution.py:17
  (2 other events, 7.2 us)
Sparse Core Ops, SparseCore 0:
  10.1 78.7 all-gather.2
  127.7 71.7 reduce-scatter.1
  202.2 79.4 all-gather.4

commit v3 on v2

v3 whole, which is shorter than its diff:
```python
import jax
import jax.numpy as jnp
from jax import lax
from jax.experimental import pallas as pl
from jax.experimental.pallas import tpu as pltpu
from jax.sharding import Mesh, PartitionSpec as P

BLOCKS = 64
L1_COEF = 0.2
CAP = 4
NY = 4
NZ = 16
GROUP = 4
TILES = 3

F32 = jnp.float32
BF16 = jnp.bfloat16


def swap_cores(v):
    return lax.ppermute(v, "sect", [(0, 1), (1, 0)])


def y_ring(v, step):
    perm = [(y, (y + step) % NY) for y in range(NY)]
    perm += [(NY + y, NY + (y - step) % NY) for y in range(NY)]
    return lax.ppermute(v, ("sect", "y"), perm)


def add_body(*refs):
    *values, out = refs
    total = values[0][...].astype(F32)
    for v in values[1:]:
        total = total + v[...].astype(F32)
    out[...] = total.astype(out.dtype)


def add(*terms, count=1):
    first = terms[0][0]
    shape = (1, 1) + first.shape[2:]
    rest = (0,) * (first.ndim - 2)
    return pl.pallas_call(
        add_body,
        grid=(count, first.shape[1]),
        in_specs=[
            pl.BlockSpec(shape, lambda i, j, at=at: (i + at, j) + rest) for _, at in terms
        ],
        out_specs=pl.BlockSpec(shape, lambda i, j: (i, j) + rest),
        out_shape=jax.ShapeDtypeStruct((count,) + first.shape[1:], first.dtype),
        cost_estimate=pl.CostEstimate(flops=0, bytes_accessed=3_000_000, transcendentals=0),
    )(*[v for v, _ in terms])


def gather_blocks(own):
    chip = jnp.stack([own, swap_cores(own)])
    near = y_ring(chip, 1)
    far = y_ring(near[0], 1)
    half = jnp.concatenate([own[None], near, far[None]])
    return half, swap_cores(half)


def scatter_blocks(half, other):
    other = swap_cores(other)
    away = y_ring(add((half, 2), (other, 2), count=2), -1)
    near = y_ring(add((half, 1), (other, 1), (away, 1)), -1)
    side = swap_cores(away[:1])
    return add((half, 0), (other, 0), (side, 0), (near, 0))[0]


def peer_place(owner_sect, owner_y):
    sect, y = lax.axis_index("sect"), lax.axis_index("y")
    other = owner_sect ^ sect
    delta = owner_y - y
    delta = jnp.where(sect == 0, delta, -delta) & 3
    code = delta * 2 + other
    place = jnp.zeros_like(code)
    for at, value in enumerate((0, 4, 6, 5, 3, 7, 1, 2)):
        place = jnp.where(code == at, value, place)
    return place


def routing(place, local):
    sources, _, toks = place.shape
    groups = sources // GROUP
    named = jnp.sum(
        (place[:, :, None, :] == jnp.arange(local, dtype=jnp.int32)[None, None, :, None]).astype(F32), 1
    )
    before = (jnp.arange(toks)[:, None] < jnp.arange(toks)[None, :]).astype(BF16)
    rank = jnp.einsum("skt,tu->sku", named.astype(BF16), before, preferred_element_type=F32)
    slot = rank + CAP * (jnp.arange(sources, dtype=jnp.int32) % GROUP).astype(F32)[:, None, None]
    slot = jnp.where(named > 0, slot, -1.0)
    slot = slot.reshape(groups, GROUP, local, toks).transpose(0, 2, 1, 3)
    slot = slot.reshape(groups, local, GROUP * toks)
    return (
        slot[:, :, None, :] == jnp.arange(GROUP * CAP, dtype=F32)[None, None, :, None]
    ).astype(BF16)


def to_slots(pick, v):
    taken = jnp.einsum("pkrt,ptd->kprd", pick, v, preferred_element_type=F32).astype(BF16)
    return taken.reshape(taken.shape[0], -1, taken.shape[3])


def whole(*shape):
    return pl.BlockSpec(shape, lambda i: (0,) * len(shape))


def columns(*shape):
    return pl.BlockSpec(shape, lambda i: (0,) * (len(shape) - 1) + (i,))


PARAMS = pltpu.CompilerParams(
    dimension_semantics=("arbitrary",), vmem_limit_bytes=40 * 1024 * 1024
)


def project_body(grads, *refs):
    if grads:
        pick, rows, wa, wb, act, out, ga, gb, slots, total = refs
    else:
        pick, rows, wa, wb, out, slots, total = refs
    step = pl.program_id(0)

    @pl.when(step == 0)
    def _():
        total[...] = jnp.zeros_like(total)

    groups, wide, _ = pick.shape
    local = slots.shape[0]
    each = wide // local
    for q in range(groups):
        taken = jnp.dot(pick[q], rows[q], preferred_element_type=F32).astype(BF16)
        slots[:, q * each : (q + 1) * each, :] = taken.reshape(local, each, taken.shape[1])
    for k in range(local):
        w = wa[k] if k < local // 2 else wb[k - local // 2]
        part = jnp.dot(slots[k], w, preferred_element_type=F32)
        total[k] = total[k] + part
        if grads:
            g = jnp.dot(act[k], slots[k], preferred_element_type=F32).astype(BF16)
            if k < local // 2:
                ga[k] = g
            else:
                gb[k - local // 2] = g

    @pl.when(step == TILES - 1)
    def _():
        value = total[...].astype(BF16)
        for c in range(out.shape[0]):
            out[c] = value


def project(pick, rows, wa, wb, act=None):
    groups, wide, toks = pick.shape
    half, width, latents = wa.shape
    local, tile = 2 * half, width // TILES
    count = groups * wide // local
    depth = pl.BlockSpec((half, tile, latents), lambda i: (0, i, 0))
    ins = [pick, rows, wa, wb]
    in_specs = [
        whole(groups, wide, toks),
        columns(groups, toks, tile),
        depth,
        depth,
    ]
    outs = [jax.ShapeDtypeStruct((4, local, count, latents), BF16)]
    out_specs = [whole(4, local, count, latents)]
    if act is not None:
        ins.append(act)
        in_specs.append(whole(local, latents, count))
        outs += [jax.ShapeDtypeStruct((half, latents, width), BF16)] * 2
        out_specs += [columns(half, latents, tile)] * 2
    return pl.pallas_call(
        lambda *refs: project_body(act is not None, *refs),
        grid=(TILES,),
        in_specs=in_specs,
        out_specs=out_specs,
        out_shape=outs,
        scratch_shapes=[
            pltpu.VMEM((local, count, tile), BF16),
            pltpu.VMEM((local, count, latents), F32),
        ],
        compiler_params=PARAMS,
        cost_estimate=pl.CostEstimate(
            flops=2 * groups * wide * toks * width, bytes_accessed=12_000_000, transcendentals=0
        ),
    )(*ins)


def decode_body(copies, bias, turned, wa, wb, pre, act, home, part):
    step = pl.program_id(0)
    groups, _, wide = turned.shape
    local = part.shape[0]
    each = wide // local

    @pl.when(step == 0)
    def _():
        value = copies[0].astype(F32)
        for c in range(1, copies.shape[0]):
            value = value + copies[c].astype(F32)
        value = value + bias[...][:, None, :]
        pre[...] = value
        soft = jnp.maximum(value, 0.0) + jnp.log1p(jnp.exp(-jnp.abs(value)))
        act[...] = soft.astype(BF16)

    for k in range(local):
        w = wa[k] if k < local // 2 else wb[k - local // 2]
        part[k] = jnp.dot(act[k], w, preferred_element_type=F32).astype(BF16)
    for q in range(groups):
        rows = part[:, q * each : (q + 1) * each, :].reshape(wide, part.shape[2])
        home[q] = jnp.dot(turned[q], rows, preferred_element_type=F32).astype(BF16)


def decode(copies, bias, turned, wa, wb):
    groups, toks, wide = turned.shape
    half, latents, width = wa.shape
    local, tile = 2 * half, width // TILES
    count = groups * wide // local
    return pl.pallas_call(
        decode_body,
        grid=(TILES,),
        in_specs=[
            whole(4, local, count, latents),
            whole(local, latents),
            whole(groups, toks, wide),
            columns(half, latents, tile),
            columns(half, latents, tile),
        ],
        out_specs=[
            whole(local, count, latents),
            whole(local, count, latents),
            columns(groups, toks, tile),
        ],
        out_shape=[
            jax.ShapeDtypeStruct((local, count, latents), F32),
            jax.ShapeDtypeStruct((local, count, latents), BF16),
            jax.ShapeDtypeStruct((groups, toks, width), BF16),
        ],
        scratch_shapes=[pltpu.VMEM((local, count, tile), BF16)],
        compiler_params=PARAMS,
        cost_estimate=pl.CostEstimate(
            flops=2 * groups * wide * toks * width, bytes_accessed=12_000_000, transcendentals=0
        ),
    )(copies, bias, turned, wa, wb)


def slope_body(order, copies, flat, sig, out):
    owned = out.shape[1]
    for a in range(out.shape[0]):
        for i in range(owned):
            k = order[a] * owned + i
            value = copies[0, k].astype(F32)
            for c in range(1, copies.shape[0]):
                value = value + copies[c, k].astype(F32)
            out[a, i] = ((value + flat[k]) * sig[k]).astype(BF16)


def slopes(order, copies, flat, sig):
    _, local, count, latents = copies.shape
    return pl.pallas_call(
        slope_body,
        in_specs=[pl.BlockSpec(memory_space=pltpu.SMEM)]
        + [pl.BlockSpec(memory_space=pltpu.VMEM)] * 3,
        out_specs=pl.BlockSpec(memory_space=pltpu.VMEM),
        out_shape=jax.ShapeDtypeStruct((8, local // 8, count, latents), BF16),
        cost_estimate=pl.CostEstimate(flops=0, bytes_accessed=2_500_000, transcendentals=0),
    )(order, copies, flat, sig)


def over_lat(copies):
    return lax.all_to_all(copies, "lat", 0, 0, tiled=True)


def shards(residuals, routes, blocks, enc_weight, enc_bias, dec_weight, dec_bias):
    tok_count, width = residuals.shape
    owned, latents, _ = enc_weight.shape
    local = 8 * owned
    half = local // 2
    groups = NZ // GROUP
    sect, y, z = lax.axis_index("sect"), lax.axis_index("y"), lax.axis_index("z")

    def local_blocks(w):
        return [h.reshape(half, *w.shape[1:]) for h in gather_blocks(w)]

    rows = lax.all_gather(residuals, "z", axis=0, tiled=True).reshape(groups, GROUP * tok_count, width)

    global_block = (routes[:, None] * BLOCKS + blocks).T.reshape(1, 4, tok_count)
    ids = lax.all_to_all(
        jnp.broadcast_to(global_block, (NZ, 4, tok_count)), "z", 0, 0, tiled=True
    )
    bias_local = jnp.concatenate(local_blocks(enc_bias))
    ids, bias_local = lax.optimization_barrier((ids, bias_local))
    here = ((ids >> 1) & 15) == z
    place = jnp.where(here, peer_place(ids >> 7, (ids >> 5) & 3) * owned + (ids & 1), -1)
    pick = routing(place, local)
    present = jnp.sum(pick.astype(F32), axis=3).transpose(1, 0, 2).reshape(local, -1)
    pick = pick.reshape(groups, -1, GROUP * tok_count)
    turned = pick.transpose(0, 2, 1)

    enc_local = local_blocks(enc_weight)
    dec_local = local_blocks(dec_weight)

    pre_part, = project(pick, rows, *[w.swapaxes(1, 2) for w in enc_local])
    pre, act, home = decode(over_lat(pre_part), bias_local, turned, *dec_local)
    home, rows, ids = lax.optimization_barrier((home, rows, ids))
    total = lax.psum_scatter(
        home.reshape(NZ * tok_count, width), "z", scatter_dimension=0, tiled=True
    )

    here = ((ids >> 1) & 15) == z
    straight = routing(jnp.where(here, (ids >> 5) * owned + (ids & 1), -1), local)
    owner_rows = lax.all_to_all(
        to_slots(straight, rows).reshape(8, owned, -1, width), ("sect", "y"), 0, 0, tiled=True
    )
    owner_rows = owner_rows.transpose(1, 0, 2, 3).reshape(owned, -1, width)

    turned_dec = [w.swapaxes(1, 2) for w in dec_local]
    turned_act = act.swapaxes(1, 2)
    flat = jnp.broadcast_to(L1_COEF * present[..., None], pre.shape)
    sig = jax.nn.sigmoid(pre)
    peers = jnp.arange(8, dtype=jnp.int32)
    order = peer_place(peers >> 2, peers & 3)
    total, owner_rows, turned_dec, turned_act, flat, sig, order = lax.optimization_barrier(
        (total, owner_rows, turned_dec, turned_act, flat, sig, order)
    )
    recon = total.astype(F32) + dec_bias[None, :]
    reconstruction = recon.astype(BF16)
    error = (recon - residuals.astype(F32)).astype(BF16)
    errors = lax.all_gather(error, "z", axis=0, tiled=True).reshape(groups, GROUP * tok_count, width)
    dact, *dec_part = project(pick, errors, *turned_dec, turned_act)
    owner_slope = lax.all_to_all(
        slopes(order, over_lat(dact), flat, sig), ("sect", "y"), 0, 0, tiled=True
    )
    dec_grad = scatter_blocks(*[g.reshape(4, owned, latents, width) for g in dec_part])
    owner_slope = owner_slope.transpose(1, 0, 2, 3).reshape(owned, -1, latents)
    enc_bias_grad = jnp.sum(owner_slope.astype(F32), 1)
    enc_grad = jnp.einsum(
        "brl,brd->bld", owner_slope, owner_rows, preferred_element_type=F32
    ).astype(BF16)
    return reconstruction, enc_grad, enc_bias_grad, dec_grad


def solution(mesh):
    fine = Mesh(mesh.devices.reshape(2, NY, NZ, 4), ("sect", "y", "z", "lat"))
    own = ("sect", "y", "z")
    return jax.shard_map(
        shards,
        mesh=fine,
        in_specs=(
            P(own, "lat"),
            P(own),
            P(own, None),
            P(own, None, "lat"),
            P(own, None),
            P(own, None, "lat"),
            P("lat"),
        ),
        out_specs=(
            P(own, "lat"),
            P(own, None, "lat"),
            P(own, None),
            P(own, None, "lat"),
        ),
        check_vma=False,
    )
```

time: 361 us -> 384 us (1.064)
  waiting for transfers between devices: 140 us -> 178 us
  blocking collectives: 52.5 us -> 16.4 us
  local copies, waits for them, and re-layouts: 13.9 us -> 48.1 us
  matrix products: 34.8 us -> 5.55 us
  Pallas kernels: 0 us -> 27.1 us
  other arithmetic: 18.6 us -> 9.05 us
    all_to_all x2 -> x1, blocking collectives: 52.5 us -> 16.4 us  [over_lat(): return lax.all_to_all(copies, 'lat', 0, 0, tiled=True)]
    pallas_call x0 -> x7, Pallas kernels: none -> 27.1 us  [the longest x2 10.3 us: project(): pl.pallas_call(lambda *refs: project_body(act is not None, *refs), grid=(...]
    all_to_all x2 -> x3, waiting for transfers between devices: 7.16 us -> 32.2 us  [the longest x1 19.6 us: shards(): lax.all_to_all(to_slots(straight, rows).reshape(8, owned, -1, width), ('s...]
    dot_general x10 -> x0, matrix products: 20.3 us -> none  [the longest x4 9.02 us: into_latents(): jnp.einsum('krd,kld->krl', a, b, preferred_element_type=F32).astype(BF16)]
    unnamed x24 -> x54, local copies, waits for them, and re-layouts: 0.51 us -> 19.8 us
    ppermute x8, starting transfers between devices: 43.8 us -> 33.7 us  [swap_cores(): return lax.ppermute(v, 'sect', [(0, 1), (1, 0)])]
    all_to_all x2 -> x3, starting transfers between devices: 9.3 us -> 18.3 us  [the longest x1 7.67 us: shards(): lax.all_to_all(slopes(order, over_lat(dact), flat, sig), ('sect', 'y'), 0...]
    dot_general x5 -> x1, matrix products: 12.8 us -> 3.87 us  [to_slots(): jnp.einsum('pkrt,ptd->kprd', pick, v, preferred_element_type=F32)]
  transfers between devices with their start and end apart: 22 -> 23, of which waited for: 10 -> 13; matrix products, arithmetic and copies ran while one was open for 12% -> 10% of each run, Pallas kernels for 0% -> 2%
where the time goes in v3:
time: 384 us; the launch traced here: 382 us
  waiting for transfers between devices  178 us (46%)
  starting transfers between devices  84.3 us (22%)
  local copies, waits for them, and re-layouts  48.1 us (13%)
  Pallas kernels  27.1 us (7%)
  blocking collectives  16.4 us (4%)
  between operations  14.2 us (4%)
  other arithmetic  9.05 us (2%)
  matrix products  5.55 us (1%)
    all_gather x1, waiting for transfers between devices, shards(): lax.all_gather(error, 'z', axis=0, tiled=True)  79.3 us
    ppermute x8, starting transfers between devices, swap_cores(): return lax.ppermute(v, 'sect', [(0, 1), (1, 0)])  33.7 us
    ppermute x8, waiting for transfers between devices, y_ring(): return lax.ppermute(v, ('sect', 'y'), perm)  33.4 us
    ppermute x8, starting transfers between devices, y_ring(): return lax.ppermute(v, ('sect', 'y'), perm)  22.7 us
    unnamed x54, local copies, waits for them, and re-layouts  19.8 us
    all_to_all x1, waiting for transfers between devices, shards(): lax.all_to_all(to_slots(straight, rows).reshape(8, owned, -1, width), ('s...  19.6 us
    all_to_all x1, blocking collectives, over_lat(): return lax.all_to_all(copies, 'lat', 0, 0, tiled=True)  16.4 us
    reduce_scatter x1, waiting for transfers between devices, shards(): lax.psum_scatter(home.reshape(NZ * tok_count, width), 'z', scatter_dimens...  16.4 us
  transfers between devices with their start and end apart: 23, of which 13 were waited for; matrix products, arithmetic and copies ran while one was open for 10% of the time, Pallas kernels for 2%

profile of v3, /device:TPU:1, one launch (start us, length us, event | category | flops | bytes accessed | tf_op | source)
XLA Modules:
  0.0 382.4 jit_solution(2662792214932654769)
XLA Ops:
  7.9 8.8 %collective-permute-start.4 = (bf16[2,128,1152]{2,1,0:T(8,128)(2,1)}, bf16[2,128,1152]{2,1,0:T(8,128)(2,1)S(1)}, u32[]{:S(2)}, u32[]{:S(2)}) collective-permute-start(bf16[2,128,1152]{2,1,0:T(8,128)(2,1)} %param.10), channel_id=1, source_target_pairs={{0,256},{256,0},{1,257},{257,1},{2,258},{258,2},{3,259},{259,3},{4... | collective-permute-start | bytes 1769480 | tf_op jit(solution)/shard_map/ppermute | solution.py:21
  24.0 13.2 %collective-permute-done.5 = bf16[2,2,128,1152]{3,2,1,0:T(8,128)(2,1)S(1)} collective-permute-done((bf16[2,2,128,1152]{3,2,1,0:T(8,128)(2,1)S(1)}, bf16[2,2,128,1152]{3,2,1,0:T(8,128)(2,1)S(1)}, u32[]{:S(2)}, u32[]{:S(2)}) %collective-permute-start.5) | collective-permute-done | bytes 1179680 | tf_op jit(solution)/shard_map/ppermute | solution.py:27
  37.2 2.7 collective-permute-start.6
  40.0 9.9 %collective-permute-done.9 = bf16[2,2,128,1152]{3,2,1,0:T(8,128)(2,1)S(1)} collective-permute-done((bf16[2,2,128,1152]{3,2,1,0:T(8,128)(2,1)S(1)}, bf16[2,2,128,1152]{3,2,1,0:T(8,128)(2,1)S(1)}, u32[]{:S(2)}, u32[]{:S(2)}) %collective-permute-start.9) | collective-permute-done | bytes 1179680 | tf_op jit(solution)/shard_map/ppermute | solution.py:27
  49.9 2.7 collective-permute-start.10
  52.6 3.5 collective-permute-done.6
  57.9 4.4 %collective-permute-start.7 = (bf16[4,2,128,1152]{3,2,1,0:T(8,128)(2,1)}, bf16[4,2,128,1152]{3,2,1,0:T(8,128)(2,1)}, u32[]{:S(2)}, u32[]{:S(2)}) collective-permute-start(bf16[4,2,128,1152]{3,2,1,0:T(8,128)(2,1)} %pad_maximum_fusion), channel_id=1, source_target_pairs={{0,256},{256,0},{1,257},{257,1},{2,258},{258,2},{3,259},{259,3},{4... | collective-permute-start | bytes 7077896 | tf_op jit(solution)/shard_map/ppermute | solution.py:21
  71.2 4.7 %collective-permute-start.2 = (f32[2,128]{1,0:T(2,128)S(1)}, f32[2,128]{1,0:T(2,128)S(1)}, u32[]{:S(2)}, u32[]{:S(2)}) collective-permute-start(f32[2,128]{1,0:T(2,128)S(1)} %slice_bitcast_fusion.2), channel_id=1, source_target_pairs={{0,64},{64,128},{128,192},{192,0},{256,448},{320,256},{384,320},{4... | collective-permute-start | bytes 3080 | tf_op jit(solution)/shard_map/ppermute | solution.py:27
  76.6 9.5 %all-to-all-start = ((s32[16,4,128]{2,1,0:T(4,128)}), s32[16,4,128]{2,1,0:T(4,128)S(1)}, u32[]{:S(2)}, u32[]{:S(2)}) async-start(s32[16,4,128]{2,1,0:T(4,128)} %broadcast_in_dim.72), calls=%async_computation | async-start | bytes 65536 | tf_op jit(solution)/shard_map/all_to_all | solution.py:287
  89.2 8.3 %all-to-all-done = s32[16,4,128]{2,1,0:T(4,128)S(1)} async-done(((s32[16,4,128]{2,1,0:T(4,128)}), s32[16,4,128]{2,1,0:T(4,128)S(1)}, u32[]{:S(2)}, u32[]{:S(2)}) %all-to-all-start) | async-done | bytes 32800 | tf_op jit(solution)/shard_map/all_to_all | solution.py:287
  98.8 4.3 %copy.76 = bf16[4,2,128,1152]{2,3,1,0:T(8,128)(2,1)} copy(bf16[4,2,128,1152]{3,2,1,0:T(8,128)(2,1)} %pad_maximum_fusion) | data formatting | bytes 4718592 | tf_op jit(solution)/shard_map/concatenate | solution.py:58
  103.1 4.3 %copy.77 = bf16[4,2,128,1152]{2,3,1,0:T(8,128)(2,1)} copy(bf16[4,2,128,1152]{3,2,1,0:T(8,128)(2,1)} %collective-permute-done.7) | data formatting | bytes 4718592 | tf_op jit(solution)/shard_map/ppermute | solution.py:21
  113.1 4.0 %shard_map.102 = bf16[4,16,64,128]{3,2,1,0:T(8,128)(2,1)S(1)} custom-call(bf16[4,256,512]{2,1,0:T(8,128)(2,1)S(1)} %fusion.9.refs_0_, bf16[4,512,1152]{2,1,0:T(8,128)(2,1)S(1)} %bitcast.88, bf16[8,1152,128]{2,1,0:T(8,128)(2,1)S(1)} %bitcast.85, bf16[8,1152,128]{2,1,0:T(8,128)(2,1)S(1)} %bitcast.86), custom_call_target="tpu_custom_call" | custom-call | flops 1207959552 | bytes 12000000 | tf_op jit(solution)/shard_map/pallas_call | solution.py:172
  118.1 4.3 %all-to-all-start.1 = ((bf16[4,16,64,128]{3,2,1,0:T(8,128)(2,1)}), bf16[4,16,64,128]{3,2,1,0:T(8,128)(2,1)}, u32[]{:S(2)}, u32[]{:S(2)}) async-start(bf16[4,16,64,128]{3,2,1,0:T(8,128)(2,1)} %copy-done.8), calls=%async_computation.1 | async-start | bytes 2097152 | tf_op jit(solution)/shard_map/all_to_all | solution.py:270
  123.8 12.6 %all-to-all-done.1.copies = bf16[4,16,64,128]{3,2,1,0:T(8,128)(2,1)} async-done(((bf16[4,16,64,128]{3,2,1,0:T(8,128)(2,1)}), bf16[4,16,64,128]{3,2,1,0:T(8,128)(2,1)}, u32[]{:S(2)}, u32[]{:S(2)}) %all-to-all-start.1) | async-done | bytes 1048608 | tf_op jit(solution)/shard_map/all_to_all | solution.py:270
  137.6 5.8 %shard_map.103 = (f32[16,64,128]{2,1,0:T(8,128)S(1)}, bf16[16,64,128]{2,1,0:T(8,128)(2,1)S(1)}, bf16[4,512,1152]{2,1,0:T(8,128)(2,1)S(1)}) custom-call(bf16[4,16,64,128]{3,2,1,0:T(8,128)(2,1)} %all-to-all-done.1.copies, f32[16,128]{1,0:T(8,128)S(1)} %pad_maximum_fusion.4.bias, bf16[4,512,256]{2,1,0:T(8,128)(2,1)S(1)} %copy-done.7, ...), custom_call_target="tpu_custom_call" | custom-call | flops 1207959552 | bytes 12000000 | tf_op jit(solution)/shard_map/pallas_call | solution.py:218
  150.4 3.9 %fusion.5 = bf16[16,4,16,1152]{3,2,0,1:T(8,128)(2,1)S(1)} fusion(bf16[4,512,1152]{2,1,0:T(8,128)(2,1)} %bitcast.87, f32[4,16,512]{2,1,0:T(8,128)} %eq.160), kind=kOutput, calls=%fused_computation.3 | convolution fusion | flops 1209663488 | bytes 7208960 | tf_op jit(solution)/shard_map/pkrt,ptd->kprd/dot_general | solution.py:100
  156.1 6.4 %all-to-all-start.2 = ((bf16[8,2,64,1152]{3,2,1,0:T(8,128)(2,1)}), bf16[8,2,64,1152]{3,2,1,0:T(8,128)(2,1)}, u32[]{:S(2)}, u32[]{:S(2)}) async-start(bf16[8,2,64,1152]{3,2,1,0:T(8,128)(2,1)} %bitcast.93), calls=%async_computation.3 | async-start | bytes 4718592 | tf_op jit(solution)/shard_map/all_to_all | solution.py:311
  165.9 4.4 %copy.79 = bf16[4,2,128,1152]{2,3,1,0:T(8,128)(2,1)} copy(bf16[4,2,128,1152]{3,2,1,0:T(8,128)(2,1)} %collective-permute-done.11) | data formatting | bytes 4718592 | tf_op jit(solution)/shard_map/ppermute | solution.py:21
  172.3 19.6 %all-to-all-done.2 = bf16[8,2,64,1152]{3,2,1,0:T(8,128)(2,1)} async-done(((bf16[8,2,64,1152]{3,2,1,0:T(8,128)(2,1)}), bf16[8,2,64,1152]{3,2,1,0:T(8,128)(2,1)}, u32[]{:S(2)}, u32[]{:S(2)}) %all-to-all-start.2) | async-done | bytes 2359328 | tf_op jit(solution)/shard_map/all_to_all | solution.py:311
  191.9 3.4 copy.85
  195.3 16.4 %reduce-scatter.2.cloned.1.call-done = bf16[128,1152]{1,0:T(8,128)(2,1)} async-done(((bf16[2048,1152]{1,0:T(8,128)(2,1)}), bf16[128,1152]{1,0:T(8,128)(2,1)}) %reduce-scatter.2.cloned.1.call-update) | async-done | bytes 294928 | tf_op jit(solution)/shard_map/reduce_scatter | solution.py:305
  214.7 79.3 %all-gather.5.cloned.1.call-done = bf16[2048,1152]{1,0:T(8,128)(2,1)} async-done(((bf16[128,1152]{1,0:T(8,128)(2,1)}), bf16[2048,1152]{1,0:T(8,128)(2,1)}) %all-gather.5.cloned.1.call-update) | async-done | bytes 4718608 | tf_op jit(solution)/shard_map/all_gather | solution.py:328
  296.7 6.3 %shard_map.104 = (bf16[4,16,64,128]{3,2,1,0:T(8,128)(2,1)S(1)}, bf16[8,128,1152]{2,1,0:T(8,128)(2,1)S(1)}, bf16[8,128,1152]{2,1,0:T(8,128)(2,1)S(1)}) custom-call(bf16[4,256,512]{2,1,0:T(8,128)(2,1)S(1)} %fusion.9.refs_0_, bf16[4,512,1152]{2,1,0:T(8,128)(2,1)} %bitcast.94, bf16[8,1152,128]{2,1,0:T(8,128)(2,1)S(1)} %bitcast.83, ...), custom_call_target="tpu_custom_call" | custom-call | flops 1207959552 | bytes 12000000 | tf_op jit(solution)/shard_map/pallas_call | solution.py:172
  305.5 10.5 %collective-permute-start.12 = (bf16[4,2,128,1152]{3,2,1,0:T(8,128)(2,1)S(1)}, bf16[4,2,128,1152]{3,2,1,0:T(8,128)(2,1)S(1)}, u32[]{:S(2)}, u32[]{:S(2)}) collective-permute-start(bf16[4,2,128,1152]{3,2,1,0:T(8,128)(2,1)S(1)} %bitcast.91), channel_id=1, source_target_pairs={{0,256},{256,0},{1,257},{257,1},{2,258},{258,2},{3,259},{259,3},{4... | collective-permute-start | bytes 7077896 | tf_op jit(solution)/shard_map/ppermute | solution.py:21
  316.0 4.1 %collective-permute-done.12.refs_1_ = bf16[4,2,128,1152]{3,2,1,0:T(8,128)(2,1)S(1)} collective-permute-done((bf16[4,2,128,1152]{3,2,1,0:T(8,128)(2,1)S(1)}, bf16[4,2,128,1152]{3,2,1,0:T(8,128)(2,1)S(1)}, u32[]{:S(2)}, u32[]{:S(2)}) %collective-permute-start.12) | collective-permute-done | bytes 2359328 | tf_op jit(solution)/shard_map/ppermute | solution.py:21
  321.5 3.8 %shard_map.106 = bf16[2,2,128,1152]{3,2,1,0:T(8,128)(2,1)} custom-call(bf16[4,2,128,1152]{3,2,1,0:T(8,128)(2,1)} %bitcast.78, bf16[4,2,128,1152]{3,2,1,0:T(8,128)(2,1)} %copy-done.16), custom_call_target="tpu_custom_call" | custom-call | bytes 3000000 | tf_op jit(solution)/shard_map/pallas_call | solution.py:42
  325.4 2.9 collective-permute-start.13
  328.3 16.4 %all_to_all.25.copies = bf16[4,16,64,128]{3,2,1,0:T(8,128)(2,1)} all-to-all(bf16[4,16,64,128]{3,2,1,0:T(8,128)(2,1)S(1)} %copy-done.11), channel_id=1, replica_groups=mesh['sect'=2,'y'=4,'z'=16,'lat'=4] {'lat'}, dimensions={0} | all-to-all | bytes 2097152 | tf_op jit(solution)/shard_map/all_to_all | solution.py:270
  347.1 7.7 %all-to-all-start.4 = ((bf16[8,2,64,128]{3,2,1,0:T(8,128)(2,1)}), bf16[8,2,64,128]{3,2,1,0:T(8,128)(2,1)S(1)}, u32[]{:S(2)}, u32[]{:S(2)}) async-start(bf16[8,2,64,128]{3,2,1,0:T(8,128)(2,1)} %shard_map.105), calls=%async_computation.5 | async-start | bytes 524288 | tf_op jit(solution)/shard_map/all_to_all | solution.py:330
  361.0 3.6 collective-permute-start.15
  366.7 6.7 %collective-permute-done.15.refs_3_ = bf16[1,2,128,1152]{3,2,1,0:T(8,128)(2,1)} collective-permute-done((bf16[1,2,128,1152]{3,2,1,0:T(8,128)(2,1)}, bf16[1,2,128,1152]{3,2,1,0:T(8,128)(2,1)}, u32[]{:S(2)}, u32[]{:S(2)}) %collective-permute-start.15) | collective-permute-done | bytes 589856 | tf_op jit(solution)/shard_map/ppermute | solution.py:27
  (127 shorter events, 69.6 us)
Async XLA Ops:
  7.2 14.6 %copy-start.20 = (bf16[2,128,1152]{2,1,0:T(8,128)(2,1)S(1)}, bf16[2,128,1152]{2,1,0:T(8,128)(2,1)}, u32[]{:S(2)}) copy-start(bf16[2,128,1152]{2,1,0:T(8,128)(2,1)} %param.12) | copy-start | bytes 1769476
  7.2 100.2 %all-gather.3.cloned.1.call-start = ((), (), s32[]{:S(2)}) async-start(), calls=%async_computation.6 | async-start | bytes 5013504 | tf_op jit(solution)/shard_map/all_gather | solution.py:284
  7.9 10.7 %collective-permute-start.4 = (bf16[2,128,1152]{2,1,0:T(8,128)(2,1)}, bf16[2,128,1152]{2,1,0:T(8,128)(2,1)S(1)}, u32[]{:S(2)}, u32[]{:S(2)}) collective-permute-start(bf16[2,128,1152]{2,1,0:T(8,128)(2,1)} %param.10), channel_id=1, source_target_pairs={{0,256},{256,0},{1,257},{257,1},{2,258},{258,2},{3,259},{259,3},{4... | collective-permute-start | bytes 1769480 | tf_op jit(solution)/shard_map/ppermute | solution.py:21
  16.7 5.1 %collective-permute-start.8 = (bf16[2,128,1152]{2,1,0:T(8,128)(2,1)}, bf16[2,128,1152]{2,1,0:T(8,128)(2,1)S(1)}, u32[]{:S(2)}, u32[]{:S(2)}) collective-permute-start(bf16[2,128,1152]{2,1,0:T(8,128)(2,1)} %param.12), channel_id=1, source_target_pairs={{0,256},{256,0},{1,257},{257,1},{2,258},{258,2},{3,259},{259,3},{4... | collective-permute-start | bytes 1769480 | tf_op jit(solution)/shard_map/ppermute | solution.py:21
  19.8 17.3 %collective-permute-start.5 = (bf16[2,2,128,1152]{3,2,1,0:T(8,128)(2,1)S(1)}, bf16[2,2,128,1152]{3,2,1,0:T(8,128)(2,1)S(1)}, u32[]{:S(2)}, u32[]{:S(2)}) collective-permute-start(bf16[2,2,128,1152]{3,2,1,0:T(8,128)(2,1)S(1)} %pad_maximum_fusion.2), channel_id=1, source_target_pairs={{0,64},{64,128},{128,192},{192,0},{256,448},{320,256},{384,320},{4... | collective-permute-start | bytes 3538952 | tf_op jit(solution)/shard_map/ppermute | solution.py:27
  21.8 34.4 %copy-start.19 = (bf16[2,128,1152]{2,1,0:T(8,128)(2,1)S(1)}, bf16[2,128,1152]{2,1,0:T(8,128)(2,1)}, u32[]{:S(2)}) copy-start(bf16[2,128,1152]{2,1,0:T(8,128)(2,1)} %param.10) | copy-start | bytes 1769476
  21.9 27.9 %collective-permute-start.9 = (bf16[2,2,128,1152]{3,2,1,0:T(8,128)(2,1)S(1)}, bf16[2,2,128,1152]{3,2,1,0:T(8,128)(2,1)S(1)}, u32[]{:S(2)}, u32[]{:S(2)}) collective-permute-start(bf16[2,2,128,1152]{3,2,1,0:T(8,128)(2,1)S(1)} %pad_maximum_fusion.3), channel_id=1, source_target_pairs={{0,64},{64,128},{128,192},{192,0},{256,448},{320,256},{384,320},{4... | collective-permute-start | bytes 3538952 | tf_op jit(solution)/shard_map/ppermute | solution.py:27
  37.2 18.9 %collective-permute-start.6 = (bf16[2,128,1152]{2,1,0:T(8,128)(2,1)S(1)}, bf16[2,128,1152]{2,1,0:T(8,128)(2,1)S(1)}, u32[]{:S(2)}, u32[]{:S(2)}) collective-permute-start(bf16[2,128,1152]{2,1,0:T(8,128)(2,1)S(1)} %slice_bitcast_fusion.1), channel_id=1, source_target_pairs={{0,64},{64,128},{128,192},{192,0},{256,448},{320,256},{384,320},{4... | collective-permute-start | bytes 1769480 | tf_op jit(solution)/shard_map/ppermute | solution.py:27
  49.9 18.5 %collective-permute-start.10 = (bf16[2,128,1152]{2,1,0:T(8,128)(2,1)S(1)}, bf16[2,128,1152]{2,1,0:T(8,128)(2,1)S(1)}, u32[]{:S(2)}, u32[]{:S(2)}) collective-permute-start(bf16[2,128,1152]{2,1,0:T(8,128)(2,1)S(1)} %slice_bitcast_fusion), channel_id=1, source_target_pairs={{0,64},{64,128},{128,192},{192,0},{256,448},{320,256},{384,320},{4... | collective-permute-start | bytes 1769480 | tf_op jit(solution)/shard_map/ppermute | solution.py:27
  56.1 6.2 %copy-start.24 = (f32[2,128]{1,0:T(2,128)S(1)}, f32[2,128]{1,0:T(2,128)}, u32[]{:S(2)}) copy-start(f32[2,128]{1,0:T(2,128)} %param.11) | copy-start | bytes 3076
  57.9 45.2 %collective-permute-start.7 = (bf16[4,2,128,1152]{3,2,1,0:T(8,128)(2,1)}, bf16[4,2,128,1152]{3,2,1,0:T(8,128)(2,1)}, u32[]{:S(2)}, u32[]{:S(2)}) collective-permute-start(bf16[4,2,128,1152]{3,2,1,0:T(8,128)(2,1)} %pad_maximum_fusion), channel_id=1, source_target_pairs={{0,256},{256,0},{1,257},{257,1},{2,258},{258,2},{3,259},{259,3},{4... | collective-permute-start | bytes 7077896 | tf_op jit(solution)/shard_map/ppermute | solution.py:21
  62.3 4.1 %collective-permute-start = (f32[2,128]{1,0:T(2,128)S(1)}, f32[2,128]{1,0:T(2,128)S(1)}, u32[]{:S(2)}, u32[]{:S(2)}) collective-permute-start(f32[2,128]{1,0:T(2,128)S(1)} %copy-done.24), channel_id=1, source_target_pairs={{0,256},{256,0},{1,257},{257,1},{2,258},{258,2},{3,259},{259,3},{4... | collective-permute-start | bytes 3080 | tf_op jit(solution)/shard_map/ppermute | solution.py:21
  66.5 4.7 %collective-permute-start.1 = (f32[2,2,128]{2,1,0:T(2,128)S(1)}, f32[2,2,128]{2,1,0:T(2,128)S(1)}, u32[]{:S(2)}, u32[]{:S(2)}) collective-permute-start(f32[2,2,128]{2,1,0:T(2,128)S(1)} %pad_maximum_fusion.6), channel_id=1, source_target_pairs={{0,64},{64,128},{128,192},{192,0},{256,448},{320,256},{384,320},{4... | collective-permute-start | bytes 6152 | tf_op jit(solution)/shard_map/ppermute | solution.py:27
  68.4 7.5 %copy-start.25 = (s32[128,4]{0,1:T(4,128)S(1)}, s32[128,4]{0,1:T(4,128)}, u32[]{:S(2)}) copy-start(s32[128,4]{0,1:T(4,128)} %param.9) | copy-start | bytes 6148
  68.7 55.0 %collective-permute-start.11 = (bf16[4,2,128,1152]{3,2,1,0:T(8,128)(2,1)S(1)}, bf16[4,2,128,1152]{3,2,1,0:T(8,128)(2,1)}, u32[]{:S(2)}, u32[]{:S(2)}) collective-permute-start(bf16[4,2,128,1152]{3,2,1,0:T(8,128)(2,1)S(1)} %pad_maximum_fusion.1), channel_id=1, source_target_pairs={{0,256},{256,0},{1,257},{257,1},{2,258},{258,2},{3,259},{259,3},{4... | collective-permute-start | bytes 7077896 | tf_op jit(solution)/shard_map/ppermute | solution.py:21
  71.2 14.9 %collective-permute-start.2 = (f32[2,128]{1,0:T(2,128)S(1)}, f32[2,128]{1,0:T(2,128)S(1)}, u32[]{:S(2)}, u32[]{:S(2)}) collective-permute-start(f32[2,128]{1,0:T(2,128)S(1)} %slice_bitcast_fusion.2), channel_id=1, source_target_pairs={{0,64},{64,128},{128,192},{192,0},{256,448},{320,256},{384,320},{4... | collective-permute-start | bytes 3080 | tf_op jit(solution)/shard_map/ppermute | solution.py:27
  76.6 21.0 %all-to-all-start = ((s32[16,4,128]{2,1,0:T(4,128)}), s32[16,4,128]{2,1,0:T(4,128)S(1)}, u32[]{:S(2)}, u32[]{:S(2)}) async-start(s32[16,4,128]{2,1,0:T(4,128)} %broadcast_in_dim.72), calls=%async_computation | async-start | bytes 65536 | tf_op jit(solution)/shard_map/all_to_all | solution.py:287
  86.1 3.1 collective-permute-start.3
  118.1 18.3 %all-to-all-start.1 = ((bf16[4,16,64,128]{3,2,1,0:T(8,128)(2,1)}), bf16[4,16,64,128]{3,2,1,0:T(8,128)(2,1)}, u32[]{:S(2)}, u32[]{:S(2)}) async-start(bf16[4,16,64,128]{3,2,1,0:T(8,128)(2,1)} %copy-done.8), calls=%async_computation.1 | async-start | bytes 2097152 | tf_op jit(solution)/shard_map/all_to_all | solution.py:270
  122.4 89.3 %reduce-scatter.2.cloned.1.call-start = ((), (), s32[]{:S(2)}) async-start(), calls=%async_computation.7 | async-start | bytes 5013504 | tf_op jit(solution)/shard_map/reduce_scatter | solution.py:305
  156.1 35.8 %all-to-all-start.2 = ((bf16[8,2,64,1152]{3,2,1,0:T(8,128)(2,1)}), bf16[8,2,64,1152]{3,2,1,0:T(8,128)(2,1)}, u32[]{:S(2)}, u32[]{:S(2)}) async-start(bf16[8,2,64,1152]{3,2,1,0:T(8,128)(2,1)} %bitcast.93), calls=%async_computation.3 | async-start | bytes 4718592 | tf_op jit(solution)/shard_map/all_to_all | solution.py:311
  162.4 131.6 %all-gather.5.cloned.1.call-start = ((), (), s32[]{:S(2)}) async-start(), calls=%async_computation.8 | async-start | bytes 5013504 | tf_op jit(solution)/shard_map/all_gather | solution.py:328
  191.8 20.8 %copy-start.23 = (f32[1152]{0:T(1024)S(1)}, f32[1152]{0:T(1024)}, u32[]{:S(2)}) copy-start(f32[1152]{0:T(1024)} %param.13) | copy-start | bytes 13828
  191.8 102.2 %copy-start.1 = (bf16[4,2,128,1152]{2,3,1,0:T(8,128)(2,1)S(1)}, bf16[4,2,128,1152]{2,3,1,0:T(8,128)(2,1)}, u32[]{:S(2)}) copy-start(bf16[4,2,128,1152]{2,3,1,0:T(8,128)(2,1)} %copy.78) | copy-start | bytes 7077892
  305.5 14.6 %collective-permute-start.12 = (bf16[4,2,128,1152]{3,2,1,0:T(8,128)(2,1)S(1)}, bf16[4,2,128,1152]{3,2,1,0:T(8,128)(2,1)S(1)}, u32[]{:S(2)}, u32[]{:S(2)}) collective-permute-start(bf16[4,2,128,1152]{3,2,1,0:T(8,128)(2,1)S(1)} %bitcast.91), channel_id=1, source_target_pairs={{0,256},{256,0},{1,257},{257,1},{2,258},{258,2},{3,259},{259,3},{4... | collective-permute-start | bytes 7077896 | tf_op jit(solution)/shard_map/ppermute | solution.py:21
  321.5 6.8 %copy-start.11 = (bf16[4,16,64,128]{3,2,1,0:T(8,128)(2,1)S(1)}, bf16[4,16,64,128]{3,2,1,0:T(8,128)(2,1)}, u32[]{:S(2)}) copy-start(bf16[4,16,64,128]{3,2,1,0:T(8,128)(2,1)} %copy-done.10) | copy-start | bytes 3145732
  325.4 29.4 %collective-permute-start.13 = (bf16[2,2,128,1152]{3,2,1,0:T(8,128)(2,1)}, bf16[2,2,128,1152]{3,2,1,0:T(8,128)(2,1)S(1)}, u32[]{:S(2)}, u32[]{:S(2)}) collective-permute-start(bf16[2,2,128,1152]{3,2,1,0:T(8,128)(2,1)} %shard_map.106), channel_id=1, source_target_pairs={{0,192},{64,0},{128,64},{192,128},{256,320},{320,384},{384,448},{4... | collective-permute-start | bytes 3538952 | tf_op jit(solution)/shard_map/ppermute | solution.py:27
  347.1 17.5 %all-to-all-start.4 = ((bf16[8,2,64,128]{3,2,1,0:T(8,128)(2,1)}), bf16[8,2,64,128]{3,2,1,0:T(8,128)(2,1)S(1)}, u32[]{:S(2)}, u32[]{:S(2)}) async-start(bf16[8,2,64,128]{3,2,1,0:T(8,128)(2,1)} %shard_map.105), calls=%async_computation.5 | async-start | bytes 524288 | tf_op jit(solution)/shard_map/all_to_all | solution.py:330
  356.7 8.6 %copy-start.17 = (bf16[2,8,64,1152]{3,2,1,0:T(8,128)(2,1)S(1)}, bf16[2,8,64,1152]{3,2,1,0:T(8,128)(2,1)}, u32[]{:S(2)}) copy-start(bf16[2,8,64,1152]{3,2,1,0:T(8,128)(2,1)} %copy.85) | copy-start | bytes 7077892
  356.7 10.0 %collective-permute-start.14 = (bf16[1,2,128,1152]{3,2,1,0:T(8,128)(2,1)}, bf16[1,2,128,1152]{3,2,1,0:T(8,128)(2,1)S(1)}, u32[]{:S(2)}, u32[]{:S(2)}) collective-permute-start(bf16[1,2,128,1152]{3,2,1,0:T(8,128)(2,1)} %slice.19), channel_id=1, source_target_pairs={{0,256},{256,0},{1,257},{257,1},{2,258},{258,2},{3,259},{259,3},{4... | collective-permute-start | bytes 1769480 | tf_op jit(solution)/shard_map/ppermute | solution.py:21
  361.0 12.4 %collective-permute-start.15 = (bf16[1,2,128,1152]{3,2,1,0:T(8,128)(2,1)}, bf16[1,2,128,1152]{3,2,1,0:T(8,128)(2,1)}, u32[]{:S(2)}, u32[]{:S(2)}) collective-permute-start(bf16[1,2,128,1152]{3,2,1,0:T(8,128)(2,1)} %shard_map.107), channel_id=1, source_target_pairs={{0,192},{64,0},{128,64},{192,128},{256,320},{320,384},{384,448},{4... | collective-permute-start | bytes 1769480 | tf_op jit(solution)/shard_map/ppermute | solution.py:27
  366.7 6.7 %copy-start.21 = (bf16[1,2,128,1152]{3,2,1,0:T(8,128)(2,1)}, bf16[1,2,128,1152]{3,2,1,0:T(8,128)(2,1)S(1)}, u32[]{:S(2)}) copy-start(bf16[1,2,128,1152]{3,2,1,0:T(8,128)(2,1)S(1)} %collective-permute-done.14.refs_2_) | copy-start | bytes 1769476
  (18 other events, 32.2 us)
Sparse Core Ops, SparseCore 0:
  10.1 77.5 all-gather.2
  147.2 64.3 reduce-scatter.1
  214.8 79.1 all-gather.4

commit v4 on v1

v4 whole, which is shorter than its diff:
```python
import jax
import jax.numpy as jnp
from jax import lax
from jax.experimental import pallas as pl
from jax.experimental.pallas import tpu as pltpu
from jax.sharding import Mesh, PartitionSpec as P

BLOCKS = 64
L1_COEF = 0.2
CAP = 4
NY = 4
NZ = 16
GROUP = 4
TILES = 3
LOCAL = 16

F32 = jnp.float32
BF16 = jnp.bfloat16


def swap_cores(v):
    return lax.ppermute(v, "sect", [(0, 1), (1, 0)])


def y_ring(v, step):
    perm = [(y, (y + step) % NY) for y in range(NY)]
    perm += [(NY + y, NY + (y - step) % NY) for y in range(NY)]
    return lax.ppermute(v, ("sect", "y"), perm)


def gather_half(own):
    chip = jnp.stack([own, swap_cores(own)])
    near = y_ring(chip, 1)
    far = y_ring(near[0], 1)
    return jnp.concatenate([own[None], near, far[None]])


def tie(*values):
    return lax.optimization_barrier(values)


def peer_place(owner_sect, owner_y):
    sect, y = lax.axis_index("sect"), lax.axis_index("y")
    other = owner_sect ^ sect
    delta = owner_y - y
    delta = jnp.where(sect == 0, delta, -delta) & 3
    code = delta * 2 + other
    place = jnp.zeros_like(code)
    for at, value in enumerate((0, 4, 6, 5, 3, 7, 1, 2)):
        place = jnp.where(code == at, value, place)
    return place


def routing(place, local):
    sources, _, toks = place.shape
    groups = sources // GROUP
    named = jnp.sum(
        (place[:, :, None, :] == jnp.arange(local, dtype=jnp.int32)[None, None, :, None]).astype(F32), 1
    )
    before = (jnp.arange(toks)[:, None] < jnp.arange(toks)[None, :]).astype(BF16)
    rank = jnp.einsum("skt,tu->sku", named.astype(BF16), before, preferred_element_type=F32)
    slot = rank + CAP * (jnp.arange(sources, dtype=jnp.int32) % GROUP).astype(F32)[:, None, None]
    slot = jnp.where(named > 0, slot, -1.0)
    slot = slot.reshape(groups, GROUP, local, toks).transpose(0, 2, 1, 3)
    slot = slot.reshape(groups, local, GROUP * toks)
    number = jnp.arange(GROUP * CAP, dtype=F32)
    pick = (slot[:, :, None, :] == number[None, None, :, None]).astype(BF16)
    turned = jnp.repeat(slot.transpose(0, 2, 1), GROUP * CAP, axis=2)
    turned = (turned == jnp.tile(number, local)[None, None, :]).astype(BF16)
    return pick.reshape(groups, -1, GROUP * toks), turned


def whole(*shape):
    return pl.BlockSpec(shape, lambda i: (0,) * len(shape))


def columns(*shape):
    return pl.BlockSpec(shape, lambda i: (0,) * (len(shape) - 1) + (i,))


PARAMS = pltpu.CompilerParams(
    dimension_semantics=("arbitrary",), vmem_limit_bytes=58 * 1024 * 1024
)


def take(pick, rows, slots):
    groups, wide, _ = pick.shape
    each = wide // LOCAL
    for q in range(groups):
        taken = jnp.dot(pick[q], rows[q], preferred_element_type=F32).astype(BF16)
        slots[:, q * each : (q + 1) * each, :] = taken.reshape(LOCAL, each, taken.shape[1])


def placed(order, wa, wb, k, owned):
    place = order[k // owned]
    at = (place & 3) * owned + k % owned
    return jnp.where(place < 4, wa[at], wb[at])


ORDER = pl.BlockSpec(memory_space=pltpu.SMEM)


def call(body, ins, in_specs, outs, out_specs, scratch, flops, moved):
    return pl.pallas_call(
        body,
        grid=(TILES,),
        in_specs=in_specs,
        out_specs=out_specs,
        out_shape=[jax.ShapeDtypeStruct(shape, kind) for shape, kind in outs],
        scratch_shapes=scratch,
        compiler_params=PARAMS,
        cost_estimate=pl.CostEstimate(flops=flops, bytes_accessed=moved, transcendentals=0),
    )(*ins)


def select(pick, rows):
    groups, wide, toks = pick.shape
    width = rows.shape[2]
    count = groups * wide // LOCAL
    return call(
        take,
        (pick, rows),
        [whole(groups, wide, toks), columns(groups, toks, width // TILES)],
        [((LOCAL, count, width), BF16)],
        [columns(LOCAL, count, width // TILES)],
        [],
        2 * groups * wide * toks * width,
        8_000_000,
    )[0]


def project_body(order, pick, rows, wa, wb, out, slots, total):
    step = pl.program_id(0)

    @pl.when(step == 0)
    def _():
        total[...] = jnp.zeros_like(total)

    take(pick, rows, slots)
    for k in range(LOCAL):
        w = placed(order, wa, wb, k, LOCAL // 8)
        total[k] = total[k] + jnp.dot(slots[k], w, preferred_element_type=F32)

    @pl.when(step == TILES - 1)
    def _():
        out[...] = total[...].astype(BF16)


def project(order, pick, rows, wa, wb, keep):
    groups, wide, toks = pick.shape
    half, _, latents = wa.shape
    width = rows.shape[2]
    tile = width // TILES
    count = groups * wide // LOCAL
    depth = pl.BlockSpec((half, tile, latents), lambda i: (0, i, 0))
    outs = [((LOCAL, count, latents), BF16)]
    out_specs = [whole(LOCAL, count, latents)]
    scratch = [pltpu.VMEM((LOCAL, count, latents), F32)]
    if keep:
        outs.append(((LOCAL, count, width), BF16))
        out_specs.append(columns(LOCAL, count, tile))
    else:
        scratch.insert(0, pltpu.VMEM((LOCAL, count, tile), BF16))
    return call(
        project_body,
        (order, pick, rows, wa, wb),
        [ORDER, whole(groups, wide, toks), columns(groups, toks, tile), depth, depth],
        outs,
        out_specs,
        scratch,
        2 * groups * wide * toks * width,
        12_000_000,
    )


def over_lat(part):
    return [part] + [
        lax.ppermute(part, "lat", [(i, (i + k) % 4) for i in range(4)]) for k in (1, 2, 3)
    ]


def sum_lat(a, b, c, d):
    return (a.astype(F32) + c.astype(F32)) + (b.astype(F32) + d.astype(F32))


def decode_body(order, a, b, c, d, bias, turned, wa, wb, pre, act, home, part):
    groups, _, wide = turned.shape
    each = wide // LOCAL

    @pl.when(pl.program_id(0) == 0)
    def _():
        for k in range(LOCAL):
            owned = LOCAL // 8
            at = order[k // owned] * owned + k % owned
            value = sum_lat(a[k], b[k], c[k], d[k]) + bias[at]
            pre[k] = value
            soft = jnp.maximum(value, 0.0) + jnp.log1p(jnp.exp(-jnp.abs(value)))
            act[k] = soft.astype(BF16)

    for k in range(LOCAL):
        w = placed(order, wa, wb, k, LOCAL // 8)
        part[k] = jnp.dot(act[k], w, preferred_element_type=F32).astype(BF16)
    for q in range(groups):
        rows = part[:, q * each : (q + 1) * each, :].reshape(wide, part.shape[2])
        home[q] = jnp.dot(turned[q], rows, preferred_element_type=F32).astype(BF16)


def decode(order, part, bias, turned, wa, wb):
    groups, toks, wide = turned.shape
    half, latents, width = wa.shape
    tile = width // TILES
    count = groups * wide // LOCAL
    return call(
        decode_body,
        (order, *over_lat(part), bias, turned, wa, wb),
        [
            ORDER,
            *[whole(LOCAL, count, latents)] * 4,
            whole(LOCAL, 1, latents),
            whole(groups, toks, wide),
            columns(half, latents, tile),
            columns(half, latents, tile),
        ],
        [
            ((LOCAL, count, latents), F32),
            ((LOCAL, count, latents), BF16),
            ((groups, toks, width), BF16),
        ],
        [
            whole(LOCAL, count, latents),
            whole(LOCAL, count, latents),
            columns(groups, toks, tile),
        ],
        [pltpu.VMEM((LOCAL, count, tile), BF16)],
        2 * groups * wide * toks * width,
        12_000_000,
    )


def slope_body(a, b, c, d, sig, out):
    out[...] = ((sum_lat(a[...], b[...], c[...], d[...]) + L1_COEF) * sig[...]).astype(BF16)


def slopes(part, sig):
    return pl.pallas_call(
        slope_body,
        in_specs=[pl.BlockSpec(memory_space=pltpu.VMEM)] * 5,
        out_specs=pl.BlockSpec(memory_space=pltpu.VMEM),
        out_shape=jax.ShapeDtypeStruct(sig.shape, BF16),
        compiler_params=pltpu.CompilerParams(vmem_limit_bytes=16 * 1024 * 1024),
        cost_estimate=pl.CostEstimate(flops=0, bytes_accessed=2_500_000, transcendentals=0),
    )(*over_lat(part), sig)


def outer_body(values, rows, grad, sums, turned):
    peers, owned, count, tile = rows.shape

    @pl.when(pl.program_id(0) == 0)
    def _():
        for i in range(owned):
            value = values[:, i].reshape(peers * count, values.shape[3]).astype(F32)
            sums[i, :] = jnp.sum(value, 0)
            turned[i] = value.T.astype(BF16)

    for i in range(owned):
        grad[i] = jnp.dot(
            turned[i], rows[:, i].reshape(peers * count, tile), preferred_element_type=F32
        ).astype(BF16)


def outer(values, rows):
    peers, owned, count, width = rows.shape
    latents = values.shape[3]
    tile = width // TILES
    return call(
        outer_body,
        (values, rows),
        [whole(peers, owned, count, latents), columns(peers, owned, count, tile)],
        [((owned, latents, width), BF16), ((owned, latents), F32)],
        [columns(owned, latents, tile), whole(owned, latents)],
        [pltpu.VMEM((owned, latents, peers * count), BF16)],
        4 * peers * count * width * latents,
        5_000_000,
    )


def shards(residuals, routes, blocks, enc_weight, enc_bias, dec_weight, dec_bias):
    tok_count, width = residuals.shape
    owned, latents, _ = enc_weight.shape
    half = LOCAL // 2
    groups = NZ // GROUP
    z = lax.axis_index("z")

    def both(part):
        return [h.reshape(half, *h.shape[2:]) for h in (part, swap_cores(part))]

    def to_owners(v):
        return lax.all_to_all(
            v.reshape(8, owned, *v.shape[1:]), ("sect", "y"), 0, 0, tiled=True
        )

    def over_z(v):
        v = lax.all_gather(v, "z", axis=0, tiled=True)
        return v.reshape(groups, GROUP * tok_count, width)

    rows = over_z(residuals)

    global_block = (routes[:, None] * BLOCKS + blocks).T.reshape(1, 4, tok_count)
    ids = lax.all_to_all(
        jnp.broadcast_to(global_block, (NZ, 4, tok_count)), "z", 0, 0, tiled=True
    )
    here = ((ids >> 1) & 15) == z
    pick, turned = routing(jnp.where(here, (ids >> 5) * owned + (ids & 1), -1), LOCAL)
    present = jnp.sum(pick.astype(F32), axis=2).reshape(groups, LOCAL, -1)
    present = present.transpose(1, 0, 2).reshape(LOCAL, -1, 1)
    peers = jnp.arange(8, dtype=jnp.int32)
    order = peer_place(peers >> 2, peers & 3)

    pick, turned, present, order, dec_weight = tie(pick, turned, present, order, dec_weight)

    pieces, left = [], enc_bias
    for _ in range(3):
        piece = lax.reduce_precision(left, 8, 7)
        pieces.append(piece.astype(BF16))
        left = left - piece
    pieces = jnp.stack(pieces, 1)
    turned_enc = jnp.concatenate(
        [enc_weight.swapaxes(1, 2), jnp.pad(pieces, ((0, 0), (0, 13), (0, 0)))], axis=1
    )
    turned_enc = both(gather_half(turned_enc))
    dec_half = gather_half(dec_weight)
    bias_local = jnp.concatenate([w[:, width : width + 3] for w in turned_enc])
    bias_local = jnp.sum(bias_local.astype(F32)[:, ::-1], 1, keepdims=True)

    pick, bias_local = tie(pick, bias_local)
    pre_part, = project(order, pick, rows, *turned_enc, False)
    dec_half, pre_part = tie(dec_half, pre_part)
    dec_local = both(dec_half)
    pre, act, home = decode(order, pre_part, bias_local, turned, *dec_local)
    home, rows = tie(home, rows)
    total = lax.psum_scatter(
        home.reshape(NZ * tok_count, width), "z", scatter_dimension=0, tiled=True
    )

    owner_rows = to_owners(select(pick, rows))
    turned_dec = [w.swapaxes(1, 2) for w in dec_local]
    total, owner_rows, turned_dec = tie(total, owner_rows, turned_dec)
    recon = total.astype(F32) + dec_bias[None, :]
    reconstruction = recon.astype(BF16)
    error = (recon - residuals.astype(F32)).astype(BF16)
    errors = over_z(error)

    owner_act = to_owners(act)
    sig = jax.nn.sigmoid(pre) * present
    errors, owner_act, sig = tie(errors, owner_act, sig)

    dact, error_slots = project(order, pick, errors, *turned_dec, True)
    owner_errors = to_owners(error_slots)
    slope, owner_errors = tie(slopes(dact, sig), owner_errors)
    owner_slope = to_owners(slope)
    enc_grad, enc_bias_grad = outer(owner_slope, owner_rows)
    dec_grad, _ = outer(owner_act, owner_errors)
    return reconstruction, enc_grad, enc_bias_grad, dec_grad


def solution(mesh):
    fine = Mesh(mesh.devices.reshape(2, NY, NZ, 4), ("sect", "y", "z", "lat"))
    own = ("sect", "y", "z")
    return jax.shard_map(
        shards,
        mesh=fine,
        in_specs=(
            P(own, "lat"),
            P(own),
            P(own, None),
            P(own, None, "lat"),
            P(own, None),
            P(own, None, "lat"),
            P("lat"),
        ),
        out_specs=(
            P(own, "lat"),
            P(own, None, "lat"),
            P(own, None),
            P(own, None, "lat"),
        ),
        check_vma=False,
    )
```

time: 412 us -> 357 us (0.87)
  waiting for transfers between devices: 227 us -> 170 us
  Pallas kernels: 0 us -> 37.2 us
  matrix products: 22.3 us -> 0.16 us
  other arithmetic: 22.9 us -> 10.1 us
    ppermute x10 -> x4, waiting for transfers between devices: 74.6 us -> 18.9 us  [y_ring(): return lax.ppermute(v, ('sect', 'y'), perm)]
    all_to_all x1 -> x5, waiting for transfers between devices: 8.26 us -> 45.9 us  [the longest x4 40.9 us: to_owners(): lax.all_to_all(v.reshape(8, owned, *v.shape[1:]), ('sect', 'y'), 0, 0, ti...]
    pallas_call x0 -> x7, Pallas kernels: none -> 37.2 us  [the longest x6 36.3 us: call(): pl.pallas_call(body, grid=(TILES,), in_specs=in_specs, out_specs=out_spec...]
    all_to_all x1 -> x5, starting transfers between devices: 9.54 us -> 45.1 us  [the longest x4 35.6 us: to_owners(): lax.all_to_all(v.reshape(8, owned, *v.shape[1:]), ('sect', 'y'), 0, 0, ti...]
    reduce_scatter x1, waiting for transfers between devices: 59.5 us -> 27.8 us  [shards(): lax.psum_scatter(home.reshape(NZ * tok_count, width), 'z', scatter_dimens...]
    ppermute x10 -> x4, starting transfers between devices: 49.8 us -> 22.3 us  [swap_cores(): return lax.ppermute(v, 'sect', [(0, 1), (1, 0)])]
    dot_general x9 -> x1, matrix products: 22.3 us -> 0.16 us  [routing(): jnp.einsum('skt,tu->sku', named.astype(BF16), before, preferred_element_t...]
    all_gather x2, waiting for transfers between devices: 79.2 us -> 60 us  [over_z(): v = lax.all_gather(v, 'z', axis=0, tiled=True)]
  transfers between devices with their start and end apart: 30 -> 22, of which waited for: 13 -> 16; matrix products, arithmetic and copies ran while one was open for 11% -> 6% of each run, Pallas kernels for 0% -> 3%
where the time goes in v4:
time: 357 us; the launch traced here: 355 us
  waiting for transfers between devices  170 us (48%)
  starting transfers between devices  105 us (29%)
  Pallas kernels  37.2 us (10%)
  local copies, waits for them, and re-layouts  17.8 us (5%)
  between operations  14.1 us (4%)
  other arithmetic  10.1 us (3%)
    all_gather x2, waiting for transfers between devices, over_z(): v = lax.all_gather(v, 'z', axis=0, tiled=True)  60 us
    all_to_all x4, waiting for transfers between devices, to_owners(): lax.all_to_all(v.reshape(8, owned, *v.shape[1:]), ('sect', 'y'), 0, 0, ti...  40.9 us
    pallas_call x6, Pallas kernels, call(): pl.pallas_call(body, grid=(TILES,), in_specs=in_specs, out_specs=out_spec...  36.3 us
    all_to_all x4, starting transfers between devices, to_owners(): lax.all_to_all(v.reshape(8, owned, *v.shape[1:]), ('sect', 'y'), 0, 0, ti...  35.6 us
    reduce_scatter x1, waiting for transfers between devices, shards(): lax.psum_scatter(home.reshape(NZ * tok_count, width), 'z', scatter_dimens...  27.8 us
    ppermute x4, starting transfers between devices, swap_cores(): return lax.ppermute(v, 'sect', [(0, 1), (1, 0)])  22.3 us
    ppermute x6, starting transfers between devices, over_lat(): lax.ppermute(part, 'lat', [(i, (i + k) % 4) for i in range(4)])  20.8 us
    ppermute x4, waiting for transfers between devices, y_ring(): return lax.ppermute(v, ('sect', 'y'), perm)  18.9 us
  transfers between devices with their start and end apart: 22, of which 16 were waited for; matrix products, arithmetic and copies ran while one was open for 6% of the time, Pallas kernels for 3%

profile of v4, /device:TPU:1, one launch (start us, length us, event | category | flops | bytes accessed | tf_op | source)
XLA Modules:
  0.0 355.2 jit_solution(4708324922018026010)
XLA Ops:
  10.2 8.8 %collective-permute-start.3 = (bf16[2,1168,128]{2,1,0:T(8,128)(2,1)S(1)}, bf16[2,1168,128]{2,1,0:T(8,128)(2,1)S(1)}, u32[]{:S(2)}, u32[]{:S(2)}) collective-permute-start(bf16[2,1168,128]{2,1,0:T(8,128)(2,1)S(1)} %get-tuple-element.61), channel_id=1, source_target_pairs={{0,256},{256,0},{1,257},{257,1},{2,258},{258,2},{3,259},{259,3},{4... | collective-permute-start | bytes 1794056 | tf_op jit(solution)/shard_map/ppermute | solution.py:22
  19.6 9.5 %all-to-all-start = ((s32[16,4,128]{2,1,0:T(4,128)}), s32[16,4,128]{2,1,0:T(4,128)S(1)}, u32[]{:S(2)}, u32[]{:S(2)}) async-start(s32[16,4,128]{2,1,0:T(4,128)} %broadcast_in_dim.50), calls=%async_computation | async-start | bytes 65536 | tf_op jit(solution)/shard_map/all_to_all | solution.py:309
  30.4 4.6 %collective-permute-start.4 = (bf16[2,2,1168,128]{3,2,1,0:T(8,128)(2,1)}, bf16[2,2,1168,128]{3,2,1,0:T(8,128)(2,1)}, u32[]{:S(2)}, u32[]{:S(2)}) collective-permute-start(bf16[2,2,1168,128]{3,2,1,0:T(8,128)(2,1)} %pad_maximum_fusion.2), channel_id=1, source_target_pairs={{0,64},{64,128},{128,192},{192,0},{256,448},{320,256},{384,320},{4... | collective-permute-start | bytes 3588104 | tf_op jit(solution)/shard_map/ppermute | solution.py:28
  35.6 5.0 %all-to-all-done = s32[16,4,128]{2,1,0:T(4,128)S(1)} async-done(((s32[16,4,128]{2,1,0:T(4,128)}), s32[16,4,128]{2,1,0:T(4,128)S(1)}, u32[]{:S(2)}, u32[]{:S(2)}) %all-to-all-start) | async-done | bytes 32800 | tf_op jit(solution)/shard_map/all_to_all | solution.py:309
  47.5 3.3 collective-permute-start
  51.9 4.8 %collective-permute-start.5 = (bf16[2,1168,128]{2,1,0:T(8,128)(2,1)S(1)}, bf16[2,1168,128]{2,1,0:T(8,128)(2,1)S(1)}, u32[]{:S(2)}, u32[]{:S(2)}) collective-permute-start(bf16[2,1168,128]{2,1,0:T(8,128)(2,1)S(1)} %slice_bitcast_fusion), channel_id=1, source_target_pairs={{0,64},{64,128},{128,192},{192,0},{256,448},{320,256},{384,320},{4... | collective-permute-start | bytes 1794056 | tf_op jit(solution)/shard_map/ppermute | solution.py:28
  59.2 4.4 %collective-permute-done.5 = bf16[2,1168,128]{2,1,0:T(8,128)(2,1)S(1)} collective-permute-done((bf16[2,1168,128]{2,1,0:T(8,128)(2,1)S(1)}, bf16[2,1168,128]{2,1,0:T(8,128)(2,1)S(1)}, u32[]{:S(2)}, u32[]{:S(2)}) %collective-permute-start.5) | collective-permute-done | bytes 598048 | tf_op jit(solution)/shard_map/ppermute | solution.py:28
  65.2 3.3 collective-permute-start.6
  68.4 7.8 %collective-permute-done.1 = bf16[2,2,128,1152]{3,2,1,0:T(8,128)(2,1)S(1)} collective-permute-done((bf16[2,2,128,1152]{3,2,1,0:T(8,128)(2,1)S(1)}, bf16[2,2,128,1152]{3,2,1,0:T(8,128)(2,1)S(1)}, u32[]{:S(2)}, u32[]{:S(2)}) %collective-permute-start.1) | collective-permute-done | bytes 1179680 | tf_op jit(solution)/shard_map/ppermute | solution.py:28
  76.3 5.4 %collective-permute-start.2 = (bf16[2,128,1152]{2,1,0:T(8,128)(2,1)S(1)}, bf16[2,128,1152]{2,1,0:T(8,128)(2,1)S(1)}, u32[]{:S(2)}, u32[]{:S(2)}) collective-permute-start(bf16[2,128,1152]{2,1,0:T(8,128)(2,1)S(1)} %slice_bitcast_fusion.1), channel_id=1, source_target_pairs={{0,64},{64,128},{128,192},{192,0},{256,448},{320,256},{384,320},{4... | collective-permute-start | bytes 1769480 | tf_op jit(solution)/shard_map/ppermute | solution.py:28
  81.7 6.8 %collective-permute-done.2 = bf16[2,128,1152]{2,1,0:T(8,128)(2,1)S(1)} collective-permute-done((bf16[2,128,1152]{2,1,0:T(8,128)(2,1)S(1)}, bf16[2,128,1152]{2,1,0:T(8,128)(2,1)S(1)}, u32[]{:S(2)}, u32[]{:S(2)}) %collective-permute-start.2) | collective-permute-done | bytes 589856 | tf_op jit(solution)/shard_map/ppermute | solution.py:28
  91.1 7.0 %shard_map.102.a = bf16[16,64,128]{2,1,0:T(8,128)(2,1)} custom-call(s32[8]{0:T(128)} %compare_select_fusion.6.order, bf16[4,256,512]{2,1,0:T(8,128)(2,1)} %fusion.1.pick, bf16[4,512,1152]{2,1,0:T(8,128)(2,1)} %bitcast.54, bf16[8,1168,128]{2,1,0:T(8,128)(2,1)} %bitcast.57, bf16[8,1168,128]{2,1,0:T(8,128)(2,1)} %bitcast.66), custom_call_target="tpu_custom_call" | custom-call | flops 1207959552 | bytes 12000000 | tf_op jit(solution)/shard_map/pallas_call | solution.py:104
  98.1 6.9 %collective-permute-start.10 = (bf16[4,2,128,1152]{3,2,1,0:T(8,128)(2,1)S(1)}, bf16[4,2,128,1152]{3,2,1,0:T(8,128)(2,1)S(1)}, u32[]{:S(2)}, u32[]{:S(2)}) collective-permute-start(bf16[4,2,128,1152]{3,2,1,0:T(8,128)(2,1)S(1)} %pad_maximum_fusion.1), channel_id=1, source_target_pairs={{0,256},{256,0},{1,257},{257,1},{2,258},{258,2},{3,259},{259,3},{4... | collective-permute-start | bytes 7077896 | tf_op jit(solution)/shard_map/ppermute | solution.py:22
  107.8 4.9 %collective-permute-start.8 = (bf16[16,64,128]{2,1,0:T(8,128)(2,1)}, bf16[16,64,128]{2,1,0:T(8,128)(2,1)S(1)}, u32[]{:S(2)}, u32[]{:S(2)}) collective-permute-start(bf16[16,64,128]{2,1,0:T(8,128)(2,1)} %shard_map.102.a), channel_id=1, source_target_pairs={{0,2},{1,3},{2,0},{3,1},{4,6},{5,7},{6,4},{7,5},{8,10},{9,11},{10,... | collective-permute-start | bytes 786440 | tf_op jit(solution)/shard_map/ppermute | solution.py:178
  116.3 6.7 %collective-permute-done.8.c = bf16[16,64,128]{2,1,0:T(8,128)(2,1)S(1)} collective-permute-done((bf16[16,64,128]{2,1,0:T(8,128)(2,1)}, bf16[16,64,128]{2,1,0:T(8,128)(2,1)S(1)}, u32[]{:S(2)}, u32[]{:S(2)}) %collective-permute-start.8) | collective-permute-done | bytes 262176 | tf_op jit(solution)/shard_map/ppermute | solution.py:178
  125.6 8.0 %shard_map.103 = (f32[16,64,128]{2,1,0:T(8,128)}, bf16[16,64,128]{2,1,0:T(8,128)(2,1)}, bf16[4,512,1152]{2,1,0:T(8,128)(2,1)}) custom-call(s32[8]{0:T(128)} %compare_select_fusion.6.order, bf16[16,64,128]{2,1,0:T(8,128)(2,1)} %shard_map.102.a, bf16[16,64,128]{2,1,0:T(8,128)(2,1)} %copy-done.12, bf16[16,64,128]{2,1,0:T(8,128)(2,1)} %copy-done.13, ...), custom_call_target="tpu_custom_call" | custom-call | flops 1207959552 | bytes 12000000 | tf_op jit(solution)/shard_map/pallas_call | solution.py:104
  133.6 5.9 %shard_map.104 = bf16[16,64,1152]{2,1,0:T(8,128)(2,1)} custom-call(bf16[4,256,512]{2,1,0:T(8,128)(2,1)} %fusion.1.pick, bf16[4,512,1152]{2,1,0:T(8,128)(2,1)} %bitcast.55), custom_call_target="tpu_custom_call" | custom-call | flops 1207959552 | bytes 8000000 | tf_op jit(solution)/shard_map/pallas_call | solution.py:104
  139.5 5.5 %all-to-all-start.1 = ((bf16[8,2,64,1152]{3,2,1,0:T(8,128)(2,1)}), bf16[8,2,64,1152]{3,2,1,0:T(8,128)(2,1)}, u32[]{:S(2)}, u32[]{:S(2)}) async-start(bf16[8,2,64,1152]{3,2,1,0:T(8,128)(2,1)} %bitcast.61), calls=%async_computation.2 | async-start | bytes 4718592 | tf_op jit(solution)/shard_map/all_to_all | solution.py:298
  147.6 4.3 %copy.52 = bf16[4,2,128,1152]{2,3,1,0:T(8,128)(2,1)} copy(bf16[4,2,128,1152]{3,2,1,0:T(8,128)(2,1)} %copy-done.5) | data formatting | bytes 4718592 | tf_op jit(solution)/shard_map/ppermute | solution.py:22
  151.9 22.5 %all-to-all-done.1.rows = bf16[8,2,64,1152]{3,2,1,0:T(8,128)(2,1)} async-done(((bf16[8,2,64,1152]{3,2,1,0:T(8,128)(2,1)}), bf16[8,2,64,1152]{3,2,1,0:T(8,128)(2,1)}, u32[]{:S(2)}, u32[]{:S(2)}) %all-to-all-start.1) | async-done | bytes 2359328 | tf_op jit(solution)/shard_map/all_to_all | solution.py:298
  174.4 27.8 %reduce-scatter.2.cloned.1.call-done = bf16[128,1152]{1,0:T(8,128)(2,1)} async-done(((bf16[2048,1152]{1,0:T(8,128)(2,1)}), bf16[128,1152]{1,0:T(8,128)(2,1)}) %reduce-scatter.2.cloned.1.call-update) | async-done | bytes 294928 | tf_op jit(solution)/shard_map/reduce_scatter | solution.py:341
  204.1 13.6 %all-to-all-start.2 = ((bf16[8,2,64,128]{3,2,1,0:T(8,128)(2,1)}), bf16[8,2,64,128]{3,2,1,0:T(8,128)(2,1)S(1)}, u32[]{:S(2)}, u32[]{:S(2)}) async-start(bf16[8,2,64,128]{3,2,1,0:T(8,128)(2,1)} %bitcast.33), calls=%async_computation.3 | async-start | bytes 524288 | tf_op jit(solution)/shard_map/all_to_all | solution.py:298
  217.9 6.3 %all-to-all-done.2.values = bf16[8,2,64,128]{3,2,1,0:T(8,128)(2,1)S(1)} async-done(((bf16[8,2,64,128]{3,2,1,0:T(8,128)(2,1)}), bf16[8,2,64,128]{3,2,1,0:T(8,128)(2,1)S(1)}, u32[]{:S(2)}, u32[]{:S(2)}) %all-to-all-start.2) | async-done | bytes 262176 | tf_op jit(solution)/shard_map/all_to_all | solution.py:298
  224.3 60.0 %all-gather.5.cloned.1.call-done = bf16[2048,1152]{1,0:T(8,128)(2,1)} async-done(((bf16[128,1152]{1,0:T(8,128)(2,1)}), bf16[2048,1152]{1,0:T(8,128)(2,1)}) %all-gather.5.cloned.1.call-update) | async-done | bytes 4718608 | tf_op jit(solution)/shard_map/all_gather | solution.py:303
  284.2 7.9 %shard_map.105 = (bf16[16,64,128]{2,1,0:T(8,128)(2,1)}, bf16[16,64,1152]{2,1,0:T(8,128)(2,1)}) custom-call(s32[8]{0:T(128)} %compare_select_fusion.6.order, bf16[4,256,512]{2,1,0:T(8,128)(2,1)} %fusion.1.pick, bf16[4,512,1152]{2,1,0:T(8,128)(2,1)} %bitcast.64, bf16[8,1152,128]{2,1,0:T(8,128)(2,1)} %bitcast.59, bf16[8,1152,128]{2,1,0:T(8,128)(2,1)} %bitcast.60), custom_call_target="tpu_custom_call" | custom-call | flops 1207959552 | bytes 12000000 | tf_op jit(solution)/shard_map/pallas_call | solution.py:104
  292.1 12.8 %all-to-all-start.3 = ((bf16[8,2,64,1152]{3,2,1,0:T(8,128)(2,1)}), bf16[8,2,64,1152]{3,2,1,0:T(8,128)(2,1)S(1)}, u32[]{:S(2)}, u32[]{:S(2)}) async-start(bf16[8,2,64,1152]{3,2,1,0:T(8,128)(2,1)} %bitcast.69), calls=%async_computation.4 | async-start | bytes 4718592 | tf_op jit(solution)/shard_map/all_to_all | solution.py:298
  308.0 4.4 %collective-permute-start.12 = (bf16[16,64,128]{2,1,0:T(8,128)(2,1)S(1)}, bf16[16,64,128]{2,1,0:T(8,128)(2,1)S(1)}, u32[]{:S(2)}, u32[]{:S(2)}) collective-permute-start(bf16[16,64,128]{2,1,0:T(8,128)(2,1)S(1)} %copy-done), channel_id=1, source_target_pairs={{0,2},{1,3},{2,0},{3,1},{4,6},{5,7},{6,4},{7,5},{8,10},{9,11},{10,... | collective-permute-start | bytes 786440 | tf_op jit(solution)/shard_map/ppermute | solution.py:178
  315.9 6.6 %collective-permute-done.12.c = bf16[16,64,128]{2,1,0:T(8,128)(2,1)S(1)} collective-permute-done((bf16[16,64,128]{2,1,0:T(8,128)(2,1)S(1)}, bf16[16,64,128]{2,1,0:T(8,128)(2,1)S(1)}, u32[]{:S(2)}, u32[]{:S(2)}) %collective-permute-start.12) | collective-permute-done | bytes 262176 | tf_op jit(solution)/shard_map/ppermute | solution.py:178
  324.5 9.4 %all-to-all-done.3.rows = bf16[8,2,64,1152]{3,2,1,0:T(8,128)(2,1)S(1)} async-done(((bf16[8,2,64,1152]{3,2,1,0:T(8,128)(2,1)}), bf16[8,2,64,1152]{3,2,1,0:T(8,128)(2,1)S(1)}, u32[]{:S(2)}, u32[]{:S(2)}) %all-to-all-start.3) | async-done | bytes 2359328 | tf_op jit(solution)/shard_map/all_to_all | solution.py:298
  333.9 3.7 %all-to-all-start.4 = ((bf16[8,2,64,128]{3,2,1,0:T(8,128)(2,1)}), bf16[8,2,64,128]{3,2,1,0:T(8,128)(2,1)S(1)}, u32[]{:S(2)}, u32[]{:S(2)}) async-start(bf16[8,2,64,128]{3,2,1,0:T(8,128)(2,1)} %bitcast.36), calls=%async_computation.5 | async-start | bytes 524288 | tf_op jit(solution)/shard_map/all_to_all | solution.py:298
  337.6 3.8 %shard_map.108 = (bf16[2,128,1152]{2,1,0:T(8,128)(2,1)}, f32[2,128]{1,0:T(2,128)}) custom-call(bf16[8,2,64,128]{3,2,1,0:T(8,128)(2,1)} %copy-done.9, bf16[8,2,64,1152]{3,2,1,0:T(8,128)(2,1)} %copy-done.4), custom_call_target="tpu_custom_call" | custom-call | flops 301989888 | bytes 5000000 | tf_op jit(solution)/shard_map/pallas_call | solution.py:104
  344.9 3.8 %shard_map.107 = (bf16[2,128,1152]{2,1,0:T(8,128)(2,1)}, f32[2,128]{1,0:T(2,128)}) custom-call(bf16[8,2,64,128]{3,2,1,0:T(8,128)(2,1)} %copy-done.10, bf16[8,2,64,1152]{3,2,1,0:T(8,128)(2,1)} %all-to-all-done.1.rows), custom_call_target="tpu_custom_call" | custom-call | flops 301989888 | bytes 5000000 | tf_op jit(solution)/shard_map/pallas_call | solution.py:104
  (97 shorter events, 45.7 us)
Async XLA Ops:
  7.2 11.8 %copy-start.17 = (s32[128]{0:T(128)S(1)}, s32[128]{0:T(128)}, u32[]{:S(2)}) copy-start(s32[128]{0:T(128)} %param.8) | copy-start | bytes 1540
  7.2 11.8 %copy-start.16 = (s32[128,4]{0,1:T(4,128)S(1)}, s32[128,4]{0,1:T(4,128)}, u32[]{:S(2)}) copy-start(s32[128,4]{0,1:T(4,128)} %param.9) | copy-start | bytes 6148
  7.2 83.9 %all-gather.3.cloned.1.call-start = ((), (), s32[]{:S(2)}) async-start(), calls=%async_computation.6 | async-start | bytes 5013504 | tf_op jit(solution)/shard_map/all_gather | solution.py:303
  10.2 19.1 %collective-permute-start.3 = (bf16[2,1168,128]{2,1,0:T(8,128)(2,1)S(1)}, bf16[2,1168,128]{2,1,0:T(8,128)(2,1)S(1)}, u32[]{:S(2)}, u32[]{:S(2)}) collective-permute-start(bf16[2,1168,128]{2,1,0:T(8,128)(2,1)S(1)} %get-tuple-element.61), channel_id=1, source_target_pairs={{0,256},{256,0},{1,257},{257,1},{2,258},{258,2},{3,259},{259,3},{4... | collective-permute-start | bytes 1794056 | tf_op jit(solution)/shard_map/ppermute | solution.py:22
  19.6 21.0 %all-to-all-start = ((s32[16,4,128]{2,1,0:T(4,128)}), s32[16,4,128]{2,1,0:T(4,128)S(1)}, u32[]{:S(2)}, u32[]{:S(2)}) async-start(s32[16,4,128]{2,1,0:T(4,128)} %broadcast_in_dim.50), calls=%async_computation | async-start | bytes 65536 | tf_op jit(solution)/shard_map/all_to_all | solution.py:309
  29.2 173.1 %reduce-scatter.2.cloned.1.call-start = ((), (), s32[]{:S(2)}) async-start(), calls=%async_computation.7 | async-start | bytes 5013504 | tf_op jit(solution)/shard_map/reduce_scatter | solution.py:341
  30.4 20.4 %collective-permute-start.4 = (bf16[2,2,1168,128]{3,2,1,0:T(8,128)(2,1)}, bf16[2,2,1168,128]{3,2,1,0:T(8,128)(2,1)}, u32[]{:S(2)}, u32[]{:S(2)}) collective-permute-start(bf16[2,2,1168,128]{3,2,1,0:T(8,128)(2,1)} %pad_maximum_fusion.2), channel_id=1, source_target_pairs={{0,64},{64,128},{128,192},{192,0},{256,448},{320,256},{384,320},{4... | collective-permute-start | bytes 3588104 | tf_op jit(solution)/shard_map/ppermute | solution.py:28
  47.5 9.2 %collective-permute-start = (bf16[2,128,1152]{2,1,0:T(8,128)(2,1)S(1)}, bf16[2,128,1152]{2,1,0:T(8,128)(2,1)S(1)}, u32[]{:S(2)}, u32[]{:S(2)}) collective-permute-start(bf16[2,128,1152]{2,1,0:T(8,128)(2,1)S(1)} %copy-done.7), channel_id=1, source_target_pairs={{0,256},{256,0},{1,257},{257,1},{2,258},{258,2},{3,259},{259,3},{4... | collective-permute-start | bytes 1769480 | tf_op jit(solution)/shard_map/ppermute | solution.py:22
  51.9 11.7 %collective-permute-start.5 = (bf16[2,1168,128]{2,1,0:T(8,128)(2,1)S(1)}, bf16[2,1168,128]{2,1,0:T(8,128)(2,1)S(1)}, u32[]{:S(2)}, u32[]{:S(2)}) collective-permute-start(bf16[2,1168,128]{2,1,0:T(8,128)(2,1)S(1)} %slice_bitcast_fusion), channel_id=1, source_target_pairs={{0,64},{64,128},{128,192},{192,0},{256,448},{320,256},{384,320},{4... | collective-permute-start | bytes 1794056 | tf_op jit(solution)/shard_map/ppermute | solution.py:28
  56.8 19.4 %collective-permute-start.1 = (bf16[2,2,128,1152]{3,2,1,0:T(8,128)(2,1)S(1)}, bf16[2,2,128,1152]{3,2,1,0:T(8,128)(2,1)S(1)}, u32[]{:S(2)}, u32[]{:S(2)}) collective-permute-start(bf16[2,2,128,1152]{3,2,1,0:T(8,128)(2,1)S(1)} %pad_maximum_fusion.3), channel_id=1, source_target_pairs={{0,64},{64,128},{128,192},{192,0},{256,448},{320,256},{384,320},{4... | collective-permute-start | bytes 3538952 | tf_op jit(solution)/shard_map/ppermute | solution.py:28
  65.2 23.7 %copy-start.3 = (bf16[4,2,1168,128]{3,2,1,0:T(8,128)(2,1)}, bf16[4,2,1168,128]{3,2,1,0:T(8,128)(2,1)S(1)}, u32[]{:S(2)}) copy-start(bf16[4,2,1168,128]{3,2,1,0:T(8,128)(2,1)S(1)} %pad_maximum_fusion) | copy-start | bytes 7176196
  65.2 23.7 %collective-permute-start.6 = (bf16[4,2,1168,128]{3,2,1,0:T(8,128)(2,1)S(1)}, bf16[4,2,1168,128]{3,2,1,0:T(8,128)(2,1)S(1)}, u32[]{:S(2)}, u32[]{:S(2)}) collective-permute-start(bf16[4,2,1168,128]{3,2,1,0:T(8,128)(2,1)S(1)} %pad_maximum_fusion), channel_id=1, source_target_pairs={{0,256},{256,0},{1,257},{257,1},{2,258},{258,2},{3,259},{259,3},{4... | collective-permute-start | bytes 7176200 | tf_op jit(solution)/shard_map/ppermute | solution.py:22
  76.3 12.2 %collective-permute-start.2 = (bf16[2,128,1152]{2,1,0:T(8,128)(2,1)S(1)}, bf16[2,128,1152]{2,1,0:T(8,128)(2,1)S(1)}, u32[]{:S(2)}, u32[]{:S(2)}) collective-permute-start(bf16[2,128,1152]{2,1,0:T(8,128)(2,1)S(1)} %slice_bitcast_fusion.1), channel_id=1, source_target_pairs={{0,64},{64,128},{128,192},{192,0},{256,448},{320,256},{384,320},{4... | collective-permute-start | bytes 1769480 | tf_op jit(solution)/shard_map/ppermute | solution.py:28
  88.9 9.3 %copy-start.1 = (bf16[4,2,128,1152]{3,2,1,0:T(8,128)(2,1)}, bf16[4,2,128,1152]{3,2,1,0:T(8,128)(2,1)S(1)}, u32[]{:S(2)}) copy-start(bf16[4,2,128,1152]{3,2,1,0:T(8,128)(2,1)S(1)} %pad_maximum_fusion.1) | copy-start | bytes 7077892
  98.1 26.0 %collective-permute-start.10 = (bf16[4,2,128,1152]{3,2,1,0:T(8,128)(2,1)S(1)}, bf16[4,2,128,1152]{3,2,1,0:T(8,128)(2,1)S(1)}, u32[]{:S(2)}, u32[]{:S(2)}) collective-permute-start(bf16[4,2,128,1152]{3,2,1,0:T(8,128)(2,1)S(1)} %pad_maximum_fusion.1), channel_id=1, source_target_pairs={{0,256},{256,0},{1,257},{257,1},{2,258},{258,2},{3,259},{259,3},{4... | collective-permute-start | bytes 7077896 | tf_op jit(solution)/shard_map/ppermute | solution.py:22
  105.1 11.2 %collective-permute-start.7 = (bf16[16,64,128]{2,1,0:T(8,128)(2,1)}, bf16[16,64,128]{2,1,0:T(8,128)(2,1)S(1)}, u32[]{:S(2)}, u32[]{:S(2)}) collective-permute-start(bf16[16,64,128]{2,1,0:T(8,128)(2,1)} %shard_map.102.a), channel_id=1, source_target_pairs={{0,1},{1,2},{2,3},{3,0},{4,5},{5,6},{6,7},{7,4},{8,9},{9,10},{10,1... | collective-permute-start | bytes 786440 | tf_op jit(solution)/shard_map/ppermute | solution.py:178
  107.8 15.2 %collective-permute-start.8 = (bf16[16,64,128]{2,1,0:T(8,128)(2,1)}, bf16[16,64,128]{2,1,0:T(8,128)(2,1)S(1)}, u32[]{:S(2)}, u32[]{:S(2)}) collective-permute-start(bf16[16,64,128]{2,1,0:T(8,128)(2,1)} %shard_map.102.a), channel_id=1, source_target_pairs={{0,2},{1,3},{2,0},{3,1},{4,6},{5,7},{6,4},{7,5},{8,10},{9,11},{10,... | collective-permute-start | bytes 786440 | tf_op jit(solution)/shard_map/ppermute | solution.py:178
  112.7 11.4 %collective-permute-start.9 = (bf16[16,64,128]{2,1,0:T(8,128)(2,1)}, bf16[16,64,128]{2,1,0:T(8,128)(2,1)S(1)}, u32[]{:S(2)}, u32[]{:S(2)}) collective-permute-start(bf16[16,64,128]{2,1,0:T(8,128)(2,1)} %shard_map.102.a), channel_id=1, source_target_pairs={{0,3},{1,0},{2,1},{3,2},{4,7},{5,4},{6,5},{7,6},{8,11},{9,8},{10,9... | collective-permute-start | bytes 786440 | tf_op jit(solution)/shard_map/ppermute | solution.py:178
  116.3 7.8 %copy-start.12 = (bf16[16,64,128]{2,1,0:T(8,128)(2,1)}, bf16[16,64,128]{2,1,0:T(8,128)(2,1)S(1)}, u32[]{:S(2)}) copy-start(bf16[16,64,128]{2,1,0:T(8,128)(2,1)S(1)} %collective-permute-done.7.b) | copy-start | bytes 786436
  139.5 35.0 %all-to-all-start.1 = ((bf16[8,2,64,1152]{3,2,1,0:T(8,128)(2,1)}), bf16[8,2,64,1152]{3,2,1,0:T(8,128)(2,1)}, u32[]{:S(2)}, u32[]{:S(2)}) async-start(bf16[8,2,64,1152]{3,2,1,0:T(8,128)(2,1)} %bitcast.61), calls=%async_computation.2 | async-start | bytes 4718592 | tf_op jit(solution)/shard_map/all_to_all | solution.py:298
  145.0 139.2 %all-gather.5.cloned.1.call-start = ((), (), s32[]{:S(2)}) async-start(), calls=%async_computation.8 | async-start | bytes 5013504 | tf_op jit(solution)/shard_map/all_gather | solution.py:303
  147.6 54.6 %copy-start.8 = (bf16[128,1152]{1,0:T(8,128)(2,1)S(1)}, bf16[128,1152]{1,0:T(8,128)(2,1)}, u32[]{:S(2)}) copy-start(bf16[128,1152]{1,0:T(8,128)(2,1)} %param.7) | copy-start | bytes 884740
  147.6 54.6 %copy-start.15 = (f32[1152]{0:T(1024)S(1)}, f32[1152]{0:T(1024)}, u32[]{:S(2)}) copy-start(f32[1152]{0:T(1024)} %param.13) | copy-start | bytes 13828
  151.9 65.8 %copy-start.11 = (f32[16,64,128]{2,1,0:T(8,128)S(1)}, f32[16,64,128]{2,1,0:T(8,128)}, u32[]{:S(2)}) copy-start(f32[16,64,128]{2,1,0:T(8,128)} %get-tuple-element.45) | copy-start | bytes 1572868
  204.1 20.1 %all-to-all-start.2 = ((bf16[8,2,64,128]{3,2,1,0:T(8,128)(2,1)}), bf16[8,2,64,128]{3,2,1,0:T(8,128)(2,1)S(1)}, u32[]{:S(2)}, u32[]{:S(2)}) async-start(bf16[8,2,64,128]{3,2,1,0:T(8,128)(2,1)} %bitcast.33), calls=%async_computation.3 | async-start | bytes 524288 | tf_op jit(solution)/shard_map/all_to_all | solution.py:298
  224.3 67.8 %copy-start.9 = (bf16[8,2,64,128]{3,2,1,0:T(8,128)(2,1)}, bf16[8,2,64,128]{3,2,1,0:T(8,128)(2,1)S(1)}, u32[]{:S(2)}) copy-start(bf16[8,2,64,128]{3,2,1,0:T(8,128)(2,1)S(1)} %all-to-all-done.2.values) | copy-start | bytes 786436
  292.1 12.8 %copy-start = (bf16[16,64,128]{2,1,0:T(8,128)(2,1)S(1)}, bf16[16,64,128]{2,1,0:T(8,128)(2,1)}, u32[]{:S(2)}) copy-start(bf16[16,64,128]{2,1,0:T(8,128)(2,1)} %get-tuple-element.50.a) | copy-start | bytes 786436
  292.1 41.8 %all-to-all-start.3 = ((bf16[8,2,64,1152]{3,2,1,0:T(8,128)(2,1)}), bf16[8,2,64,1152]{3,2,1,0:T(8,128)(2,1)S(1)}, u32[]{:S(2)}, u32[]{:S(2)}) async-start(bf16[8,2,64,1152]{3,2,1,0:T(8,128)(2,1)} %bitcast.69), calls=%async_computation.4 | async-start | bytes 4718592 | tf_op jit(solution)/shard_map/all_to_all | solution.py:298
  304.9 11.0 %collective-permute-start.11 = (bf16[16,64,128]{2,1,0:T(8,128)(2,1)S(1)}, bf16[16,64,128]{2,1,0:T(8,128)(2,1)S(1)}, u32[]{:S(2)}, u32[]{:S(2)}) collective-permute-start(bf16[16,64,128]{2,1,0:T(8,128)(2,1)S(1)} %copy-done), channel_id=1, source_target_pairs={{0,1},{1,2},{2,3},{3,0},{4,5},{5,6},{6,7},{7,4},{8,9},{9,10},{10,1... | collective-permute-start | bytes 786440 | tf_op jit(solution)/shard_map/ppermute | solution.py:178
  308.0 14.6 %collective-permute-start.12 = (bf16[16,64,128]{2,1,0:T(8,128)(2,1)S(1)}, bf16[16,64,128]{2,1,0:T(8,128)(2,1)S(1)}, u32[]{:S(2)}, u32[]{:S(2)}) collective-permute-start(bf16[16,64,128]{2,1,0:T(8,128)(2,1)S(1)} %copy-done), channel_id=1, source_target_pairs={{0,2},{1,3},{2,0},{3,1},{4,6},{5,7},{6,4},{7,5},{8,10},{9,11},{10,... | collective-permute-start | bytes 786440 | tf_op jit(solution)/shard_map/ppermute | solution.py:178
  312.4 11.3 %collective-permute-start.13 = (bf16[16,64,128]{2,1,0:T(8,128)(2,1)S(1)}, bf16[16,64,128]{2,1,0:T(8,128)(2,1)S(1)}, u32[]{:S(2)}, u32[]{:S(2)}) collective-permute-start(bf16[16,64,128]{2,1,0:T(8,128)(2,1)S(1)} %copy-done), channel_id=1, source_target_pairs={{0,3},{1,0},{2,1},{3,2},{4,7},{5,4},{6,5},{7,6},{8,11},{9,8},{10,9... | collective-permute-start | bytes 786440 | tf_op jit(solution)/shard_map/ppermute | solution.py:178
  333.9 10.3 %all-to-all-start.4 = ((bf16[8,2,64,128]{3,2,1,0:T(8,128)(2,1)}), bf16[8,2,64,128]{3,2,1,0:T(8,128)(2,1)S(1)}, u32[]{:S(2)}, u32[]{:S(2)}) async-start(bf16[8,2,64,128]{3,2,1,0:T(8,128)(2,1)} %bitcast.36), calls=%async_computation.5 | async-start | bytes 524288 | tf_op jit(solution)/shard_map/all_to_all | solution.py:298
  (8 other events, 16.4 us)
Sparse Core Ops, SparseCore 0:
  10.1 77.7 all-gather.2
  133.7 68.4 reduce-scatter.1
  204.9 79.2 all-gather.4

commit v5 on v4

--- a/solution.py
+++ b/solution.py
@@ -28,11 +28,11 @@
     return lax.ppermute(v, ("sect", "y"), perm)
 
 
-def gather_half(own):
+def gather_half(own, early, late):
     chip = jnp.stack([own, swap_cores(own)])
-    near = y_ring(chip, 1)
-    far = y_ring(near[0], 1)
-    return jnp.concatenate([own[None], near, far[None]])
+    near, early = tie(y_ring(chip, 1), early)
+    far, late = tie(y_ring(near[0], 1), late(early))
+    return jnp.concatenate([own[None], near, far[None]]), late
 
 
 def tie(*values):
@@ -143,7 +143,9 @@
 
     @pl.when(step == TILES - 1)
     def _():
-        out[...] = total[...].astype(BF16)
+        value = total[...].astype(BF16)
+        for c in range(out.shape[0]):
+            out[c] = value
 
 
 def project(order, pick, rows, wa, wb, keep):
@@ -153,8 +155,9 @@
     tile = width // TILES
     count = groups * wide // LOCAL
     depth = pl.BlockSpec((half, tile, latents), lambda i: (0, i, 0))
-    outs = [((LOCAL, count, latents), BF16)]
-    out_specs = [whole(LOCAL, count, latents)]
+    copies = 1 if keep else 4
+    outs = [((copies, LOCAL, count, latents), BF16)]
+    out_specs = [whole(copies, LOCAL, count, latents)]
     scratch = [pltpu.VMEM((LOCAL, count, latents), F32)]
     if keep:
         outs.append(((LOCAL, count, width), BF16))
@@ -183,7 +186,7 @@
     return (a.astype(F32) + c.astype(F32)) + (b.astype(F32) + d.astype(F32))
 
 
-def decode_body(order, a, b, c, d, bias, turned, wa, wb, pre, act, home, part):
+def decode_body(order, copies, bias, turned, wa, wb, pre, act, home, part):
     groups, _, wide = turned.shape
     each = wide // LOCAL
 
@@ -192,7 +195,7 @@
         for k in range(LOCAL):
             owned = LOCAL // 8
             at = order[k // owned] * owned + k % owned
-            value = sum_lat(a[k], b[k], c[k], d[k]) + bias[at]
+            value = sum_lat(*[copies[c, k] for c in range(4)]) + bias[at]
             pre[k] = value
             soft = jnp.maximum(value, 0.0) + jnp.log1p(jnp.exp(-jnp.abs(value)))
             act[k] = soft.astype(BF16)
@@ -205,17 +208,17 @@
         home[q] = jnp.dot(turned[q], rows, preferred_element_type=F32).astype(BF16)
 
 
-def decode(order, part, bias, turned, wa, wb):
+def decode(order, copies, bias, turned, wa, wb):
     groups, toks, wide = turned.shape
     half, latents, width = wa.shape
     tile = width // TILES
     count = groups * wide // LOCAL
     return call(
         decode_body,
-        (order, *over_lat(part), bias, turned, wa, wb),
+        (order, copies, bias, turned, wa, wb),
         [
             ORDER,
-            *[whole(LOCAL, count, latents)] * 4,
+            whole(4, LOCAL, count, latents),
             whole(LOCAL, 1, latents),
             whole(groups, toks, wide),
             columns(half, latents, tile),
@@ -309,14 +312,14 @@
     ids = lax.all_to_all(
         jnp.broadcast_to(global_block, (NZ, 4, tok_count)), "z", 0, 0, tiled=True
     )
-    here = ((ids >> 1) & 15) == z
-    pick, turned = routing(jnp.where(here, (ids >> 5) * owned + (ids & 1), -1), LOCAL)
-    present = jnp.sum(pick.astype(F32), axis=2).reshape(groups, LOCAL, -1)
-    present = present.transpose(1, 0, 2).reshape(LOCAL, -1, 1)
-    peers = jnp.arange(8, dtype=jnp.int32)
-    order = peer_place(peers >> 2, peers & 3)
-
-    pick, turned, present, order, dec_weight = tie(pick, turned, present, order, dec_weight)
+
+    def tables(ids):
+        here = ((ids >> 1) & 15) == z
+        pick, turned = routing(jnp.where(here, (ids >> 5) * owned + (ids & 1), -1), LOCAL)
+        present = jnp.sum(pick.astype(F32), axis=2).reshape(groups, LOCAL, -1)
+        present = present.transpose(1, 0, 2).reshape(LOCAL, -1, 1)
+        peers = jnp.arange(8, dtype=jnp.int32)
+        return pick, turned, present, peer_place(peers >> 2, peers & 3)
 
     pieces, left = [], enc_bias
     for _ in range(3):
@@ -327,16 +330,16 @@
     turned_enc = jnp.concatenate(
         [enc_weight.swapaxes(1, 2), jnp.pad(pieces, ((0, 0), (0, 13), (0, 0)))], axis=1
     )
-    turned_enc = both(gather_half(turned_enc))
-    dec_half = gather_half(dec_weight)
+    turned_enc = both(gather_half(turned_enc, (), lambda v: v)[0])
+    dec_half, (pick, turned, present, order) = gather_half(dec_weight, ids, tables)
     bias_local = jnp.concatenate([w[:, width : width + 3] for w in turned_enc])
     bias_local = jnp.sum(bias_local.astype(F32)[:, ::-1], 1, keepdims=True)
 
     pick, bias_local = tie(pick, bias_local)
     pre_part, = project(order, pick, rows, *turned_enc, False)
-    dec_half, pre_part = tie(dec_half, pre_part)
     dec_local = both(dec_half)
-    pre, act, home = decode(order, pre_part, bias_local, turned, *dec_local)
+    copies = lax.all_to_all(pre_part, "lat", 0, 0, tiled=True)
+    pre, act, home = decode(order, copies, bias_local, turned, *dec_local)
     home, rows = tie(home, rows)
     total = lax.psum_scatter(
         home.reshape(NZ * tok_count, width), "z", scatter_dimension=0, tiled=True
@@ -356,7 +359,7 @@
 
     dact, error_slots = project(order, pick, errors, *turned_dec, True)
     owner_errors = to_owners(error_slots)
-    slope, owner_errors = tie(slopes(dact, sig), owner_errors)
+    slope, owner_errors = tie(slopes(dact[0], sig), owner_errors)
     owner_slope = to_owners(slope)
     enc_grad, enc_bias_grad = outer(owner_slope, owner_rows)
     dec_grad, _ = outer(owner_act, owner_errors)

time: 357 us -> 349 us (0.978)
  starting transfers between devices: 105 us -> 99.5 us
    ppermute x4, waiting for transfers between devices: 18.9 us -> 5.33 us  [y_ring(): return lax.ppermute(v, ('sect', 'y'), perm)]
    ppermute x6 -> x3, starting transfers between devices: 20.8 us -> 10.5 us  [over_lat(): lax.ppermute(part, 'lat', [(i, (i + k) % 4) for i in range(4)])]
    all_to_all x0 -> x1, waiting for transfers between devices: none -> 9.73 us  [shards(): copies = lax.all_to_all(pre_part, 'lat', 0, 0, tiled=True)]
    all_to_all x4, starting transfers between devices: 35.6 us -> 44.5 us  [to_owners(): lax.all_to_all(v.reshape(8, owned, *v.shape[1:]), ('sect', 'y'), 0, 0, ti...]
    ppermute x6 -> x3, waiting for transfers between devices: 17 us -> 8.25 us  [over_lat(): lax.ppermute(part, 'lat', [(i, (i + k) % 4) for i in range(4)])]
    ppermute x4, starting transfers between devices: 17.3 us -> 8.86 us  [y_ring(): return lax.ppermute(v, ('sect', 'y'), perm)]
    all_to_all x1, waiting for transfers between devices: 5.03 us -> 11.1 us  [shards(): lax.all_to_all(jnp.broadcast_to(global_block, (NZ, 4, tok_count)), 'z', 0...]
    all_gather x2, waiting for transfers between devices: 60 us -> 64.9 us  [over_z(): v = lax.all_gather(v, 'z', axis=0, tiled=True)]
  transfers between devices with their start and end apart: 22 -> 20, of which waited for: 16 -> 14; matrix products, arithmetic and copies ran while one was open for 6% -> 7% of each run, Pallas kernels for 3% -> 5%
where the time goes in v5:
time: 349 us; the launch traced here: 347 us
  waiting for transfers between devices  167 us (48%)
  starting transfers between devices  99.5 us (29%)
  Pallas kernels  37.5 us (11%)
  local copies, waits for them, and re-layouts  16.9 us (5%)
  between operations  14 us (4%)
  other arithmetic  12.4 us (4%)
    all_gather x2, waiting for transfers between devices, over_z(): v = lax.all_gather(v, 'z', axis=0, tiled=True)  64.9 us
    all_to_all x4, starting transfers between devices, to_owners(): lax.all_to_all(v.reshape(8, owned, *v.shape[1:]), ('sect', 'y'), 0, 0, ti...  44.5 us
    all_to_all x4, waiting for transfers between devices, to_owners(): lax.all_to_all(v.reshape(8, owned, *v.shape[1:]), ('sect', 'y'), 0, 0, ti...  40.9 us
    pallas_call x6, Pallas kernels, call(): pl.pallas_call(body, grid=(TILES,), in_specs=in_specs, out_specs=out_spec...  36.6 us
    reduce_scatter x1, waiting for transfers between devices, shards(): lax.psum_scatter(home.reshape(NZ * tok_count, width), 'z', scatter_dimens...  25.9 us
    ppermute x4, starting transfers between devices, swap_cores(): return lax.ppermute(v, 'sect', [(0, 1), (1, 0)])  18.9 us
    all_to_all x1, starting transfers between devices, shards(): lax.all_to_all(jnp.broadcast_to(global_block, (NZ, 4, tok_count)), 'z', 0...  12.7 us
    all_to_all x1, waiting for transfers between devices, shards(): lax.all_to_all(jnp.broadcast_to(global_block, (NZ, 4, tok_count)), 'z', 0...  11.1 us
  transfers between devices with their start and end apart: 20, of which 14 were waited for; matrix products, arithmetic and copies ran while one was open for 7% of the time, Pallas kernels for 5%

profile of v5, /device:TPU:1, one launch (start us, length us, event | category | flops | bytes accessed | tf_op | source)
XLA Modules:
  0.0 347.3 jit_solution(7307446261405590293)
XLA Ops:
  10.2 8.8 %collective-permute-start.3 = (bf16[2,1168,128]{2,1,0:T(8,128)(2,1)S(1)}, bf16[2,1168,128]{2,1,0:T(8,128)(2,1)S(1)}, u32[]{:S(2)}, u32[]{:S(2)}) collective-permute-start(bf16[2,1168,128]{2,1,0:T(8,128)(2,1)S(1)} %get-tuple-element.61), channel_id=1, source_target_pairs={{0,256},{256,0},{1,257},{257,1},{2,258},{258,2},{3,259},{259,3},{4... | collective-permute-start | bytes 1794056 | tf_op jit(solution)/shard_map/ppermute | solution.py:22
  27.8 12.7 %all-to-all-start = ((s32[16,4,128]{2,1,0:T(4,128)}), s32[16,4,128]{2,1,0:T(4,128)S(1)}, u32[]{:S(2)}, u32[]{:S(2)}) async-start(s32[16,4,128]{2,1,0:T(4,128)} %broadcast_in_dim.48), calls=%async_computation | async-start | bytes 65536 | tf_op jit(solution)/shard_map/all_to_all | solution.py:312
  41.2 11.1 %all-to-all-done = s32[16,4,128]{2,1,0:T(4,128)S(1)} async-done(((s32[16,4,128]{2,1,0:T(4,128)}), s32[16,4,128]{2,1,0:T(4,128)S(1)}, u32[]{:S(2)}, u32[]{:S(2)}) %all-to-all-start) | async-done | bytes 32800 | tf_op jit(solution)/shard_map/all_to_all | solution.py:312
  52.5 3.1 collective-permute-start.5
  58.4 5.2 %collective-permute-done.5 = bf16[2,1168,128]{2,1,0:T(8,128)(2,1)S(1)} collective-permute-done((bf16[2,1168,128]{2,1,0:T(8,128)(2,1)S(1)}, bf16[2,1168,128]{2,1,0:T(8,128)(2,1)S(1)}, u32[]{:S(2)}, u32[]{:S(2)}) %collective-permute-start.5) | collective-permute-done | bytes 598048 | tf_op jit(solution)/shard_map/ppermute | solution.py:28
  65.4 6.3 %collective-permute-start.6 = (bf16[4,2,1168,128]{3,2,1,0:T(8,128)(2,1)}, bf16[4,2,1168,128]{3,2,1,0:T(8,128)(2,1)}, u32[]{:S(2)}, u32[]{:S(2)}) collective-permute-start(bf16[4,2,1168,128]{3,2,1,0:T(8,128)(2,1)} %pad_maximum_fusion), channel_id=1, source_target_pairs={{0,256},{256,0},{1,257},{257,1},{2,258},{258,2},{3,259},{259,3},{4... | collective-permute-start | bytes 7176200 | tf_op jit(solution)/shard_map/ppermute | solution.py:22
  74.9 1.9 copy.47
  83.9 5.0 %all-gather.3.cloned.1.call-done = bf16[2048,1152]{1,0:T(8,128)(2,1)} async-done(((bf16[128,1152]{1,0:T(8,128)(2,1)}), bf16[2048,1152]{1,0:T(8,128)(2,1)}) %all-gather.3.cloned.1.call-update) | async-done | bytes 4718608 | tf_op jit(solution)/shard_map/all_gather | solution.py:306
  88.9 7.3 %shard_map.102 = bf16[4,16,64,128]{3,2,1,0:T(8,128)(2,1)} custom-call(s32[8]{0:T(128)} %compare_select_fusion.6.order, bf16[4,256,512]{2,1,0:T(8,128)(2,1)} %fusion.1.pick, bf16[4,512,1152]{2,1,0:T(8,128)(2,1)} %bitcast.59, bf16[8,1168,128]{2,1,0:T(8,128)(2,1)} %bitcast.19.wa, bf16[8,1168,128]{2,1,0:T(8,128)(2,1)} %bitcast.20.wb), custom_call_target="tpu_custom_call" | custom-call | flops 1207959552 | bytes 12000000 | tf_op jit(solution)/shard_map/pallas_call | solution.py:104
  96.2 4.0 %all-to-all-start.1 = ((bf16[4,16,64,128]{3,2,1,0:T(8,128)(2,1)}), bf16[4,16,64,128]{3,2,1,0:T(8,128)(2,1)S(1)}, u32[]{:S(2)}, u32[]{:S(2)}) async-start(bf16[4,16,64,128]{3,2,1,0:T(8,128)(2,1)} %shard_map.102), calls=%async_computation.1 | async-start | bytes 2097152 | tf_op jit(solution)/shard_map/all_to_all | solution.py:341
  100.2 9.7 %all-to-all-done.1.copies = bf16[4,16,64,128]{3,2,1,0:T(8,128)(2,1)S(1)} async-done(((bf16[4,16,64,128]{3,2,1,0:T(8,128)(2,1)}), bf16[4,16,64,128]{3,2,1,0:T(8,128)(2,1)S(1)}, u32[]{:S(2)}, u32[]{:S(2)}) %all-to-all-start.1) | async-done | bytes 1048608 | tf_op jit(solution)/shard_map/all_to_all | solution.py:341
  110.9 7.9 %shard_map.103 = (f32[16,64,128]{2,1,0:T(8,128)}, bf16[16,64,128]{2,1,0:T(8,128)(2,1)}, bf16[4,512,1152]{2,1,0:T(8,128)(2,1)}) custom-call(s32[8]{0:T(128)} %compare_select_fusion.6.order, bf16[4,16,64,128]{3,2,1,0:T(8,128)(2,1)} %copy-done.4, f32[16,1,128]{2,1,0:T(1,128)} %bitcast.79, bf16[4,512,256]{2,1,0:T(8,128)(2,1)} %compare_convert_fusion.turned, ...), custom_call_target="tpu_custom_call" | custom-call | flops 1207959552 | bytes 12000000 | tf_op jit(solution)/shard_map/pallas_call | solution.py:104
  118.9 5.9 %shard_map.104 = bf16[16,64,1152]{2,1,0:T(8,128)(2,1)} custom-call(bf16[4,256,512]{2,1,0:T(8,128)(2,1)} %fusion.1.pick, bf16[4,512,1152]{2,1,0:T(8,128)(2,1)} %bitcast.60), custom_call_target="tpu_custom_call" | custom-call | flops 1207959552 | bytes 8000000 | tf_op jit(solution)/shard_map/pallas_call | solution.py:104
  124.7 14.1 %all-to-all-start.2 = ((bf16[8,2,64,1152]{3,2,1,0:T(8,128)(2,1)}), bf16[8,2,64,1152]{3,2,1,0:T(8,128)(2,1)}, u32[]{:S(2)}, u32[]{:S(2)}) async-start(bf16[8,2,64,1152]{3,2,1,0:T(8,128)(2,1)} %bitcast.63), calls=%async_computation.3 | async-start | bytes 4718592 | tf_op jit(solution)/shard_map/all_to_all | solution.py:301
  138.8 2.5 copy.51
  141.3 4.4 %copy.52 = bf16[4,2,128,1152]{2,3,1,0:T(8,128)(2,1)} copy(bf16[4,2,128,1152]{3,2,1,0:T(8,128)(2,1)} %collective-permute-done.7) | data formatting | bytes 4718592 | tf_op jit(solution)/shard_map/ppermute | solution.py:22
  145.7 22.5 %all-to-all-done.2.rows = bf16[8,2,64,1152]{3,2,1,0:T(8,128)(2,1)} async-done(((bf16[8,2,64,1152]{3,2,1,0:T(8,128)(2,1)}), bf16[8,2,64,1152]{3,2,1,0:T(8,128)(2,1)}, u32[]{:S(2)}, u32[]{:S(2)}) %all-to-all-start.2) | async-done | bytes 2359328 | tf_op jit(solution)/shard_map/all_to_all | solution.py:301
  168.1 25.9 %reduce-scatter.2.cloned.1.call-done = bf16[128,1152]{1,0:T(8,128)(2,1)} async-done(((bf16[2048,1152]{1,0:T(8,128)(2,1)}), bf16[128,1152]{1,0:T(8,128)(2,1)}) %reduce-scatter.2.cloned.1.call-update) | async-done | bytes 294928 | tf_op jit(solution)/shard_map/reduce_scatter | solution.py:344
  195.9 13.9 %all-to-all-start.3 = ((bf16[8,2,64,128]{3,2,1,0:T(8,128)(2,1)}), bf16[8,2,64,128]{3,2,1,0:T(8,128)(2,1)S(1)}, u32[]{:S(2)}, u32[]{:S(2)}) async-start(bf16[8,2,64,128]{3,2,1,0:T(8,128)(2,1)} %bitcast.33), calls=%async_computation.4 | async-start | bytes 524288 | tf_op jit(solution)/shard_map/all_to_all | solution.py:301
  210.0 6.4 %all-to-all-done.3.values = bf16[8,2,64,128]{3,2,1,0:T(8,128)(2,1)S(1)} async-done(((bf16[8,2,64,128]{3,2,1,0:T(8,128)(2,1)}), bf16[8,2,64,128]{3,2,1,0:T(8,128)(2,1)S(1)}, u32[]{:S(2)}, u32[]{:S(2)}) %all-to-all-start.3) | async-done | bytes 262176 | tf_op jit(solution)/shard_map/all_to_all | solution.py:301
  216.4 59.9 %all-gather.5.cloned.1.call-done = bf16[2048,1152]{1,0:T(8,128)(2,1)} async-done(((bf16[128,1152]{1,0:T(8,128)(2,1)}), bf16[2048,1152]{1,0:T(8,128)(2,1)}) %all-gather.5.cloned.1.call-update) | async-done | bytes 4718608 | tf_op jit(solution)/shard_map/all_gather | solution.py:306
  276.3 7.9 %shard_map.105 = (bf16[1,16,64,128]{3,2,1,0:T(8,128)(2,1)}, bf16[16,64,1152]{2,1,0:T(8,128)(2,1)}) custom-call(s32[8]{0:T(128)} %compare_select_fusion.6.order, bf16[4,256,512]{2,1,0:T(8,128)(2,1)} %fusion.1.pick, bf16[4,512,1152]{2,1,0:T(8,128)(2,1)} %bitcast.66, bf16[8,1152,128]{2,1,0:T(8,128)(2,1)} %bitcast.61, bf16[8,1152,128]{2,1,0:T(8,128)(2,1)} %bitcast.62), custom_call_target="tpu_custom_call" | custom-call | flops 1207959552 | bytes 12000000 | tf_op jit(solution)/shard_map/pallas_call | solution.py:104
  284.2 12.8 %all-to-all-start.4 = ((bf16[8,2,64,1152]{3,2,1,0:T(8,128)(2,1)}), bf16[8,2,64,1152]{3,2,1,0:T(8,128)(2,1)S(1)}, u32[]{:S(2)}, u32[]{:S(2)}) async-start(bf16[8,2,64,1152]{3,2,1,0:T(8,128)(2,1)} %bitcast.69), calls=%async_computation.5 | async-start | bytes 4718592 | tf_op jit(solution)/shard_map/all_to_all | solution.py:301
  297.0 3.1 collective-permute-start.8
  300.0 4.4 %collective-permute-start.9 = (bf16[16,64,128]{2,1,0:T(8,128)(2,1)S(1)}, bf16[16,64,128]{2,1,0:T(8,128)(2,1)S(1)}, u32[]{:S(2)}, u32[]{:S(2)}) collective-permute-start(bf16[16,64,128]{2,1,0:T(8,128)(2,1)S(1)} %bitcast.55), channel_id=1, source_target_pairs={{0,2},{1,3},{2,0},{3,1},{4,6},{5,7},{6,4},{7,5},{8,10},{9,11},{10,... | collective-permute-start | bytes 786440 | tf_op jit(solution)/shard_map/ppermute | solution.py:181
  304.5 3.0 collective-permute-start.10
  308.0 6.6 %collective-permute-done.9.c = bf16[16,64,128]{2,1,0:T(8,128)(2,1)S(1)} collective-permute-done((bf16[16,64,128]{2,1,0:T(8,128)(2,1)S(1)}, bf16[16,64,128]{2,1,0:T(8,128)(2,1)S(1)}, u32[]{:S(2)}, u32[]{:S(2)}) %collective-permute-start.9) | collective-permute-done | bytes 262176 | tf_op jit(solution)/shard_map/ppermute | solution.py:181
  316.6 9.4 %all-to-all-done.4.rows = bf16[8,2,64,1152]{3,2,1,0:T(8,128)(2,1)S(1)} async-done(((bf16[8,2,64,1152]{3,2,1,0:T(8,128)(2,1)}), bf16[8,2,64,1152]{3,2,1,0:T(8,128)(2,1)S(1)}, u32[]{:S(2)}, u32[]{:S(2)}) %all-to-all-start.4) | async-done | bytes 2359328 | tf_op jit(solution)/shard_map/all_to_all | solution.py:301
  326.0 3.7 %all-to-all-start.5 = ((bf16[8,2,64,128]{3,2,1,0:T(8,128)(2,1)}), bf16[8,2,64,128]{3,2,1,0:T(8,128)(2,1)S(1)}, u32[]{:S(2)}, u32[]{:S(2)}) async-start(bf16[8,2,64,128]{3,2,1,0:T(8,128)(2,1)} %bitcast.37), calls=%async_computation.6 | async-start | bytes 524288 | tf_op jit(solution)/shard_map/all_to_all | solution.py:301
  329.7 3.8 %shard_map.108 = (bf16[2,128,1152]{2,1,0:T(8,128)(2,1)}, f32[2,128]{1,0:T(2,128)}) custom-call(bf16[8,2,64,128]{3,2,1,0:T(8,128)(2,1)} %copy-done.8, bf16[8,2,64,1152]{3,2,1,0:T(8,128)(2,1)} %copy-done.3), custom_call_target="tpu_custom_call" | custom-call | flops 301989888 | bytes 5000000 | tf_op jit(solution)/shard_map/pallas_call | solution.py:104
  333.5 2.7 all-to-all-done.5.values
  336.9 3.8 %shard_map.107 = (bf16[2,128,1152]{2,1,0:T(8,128)(2,1)}, f32[2,128]{1,0:T(2,128)}) custom-call(bf16[8,2,64,128]{3,2,1,0:T(8,128)(2,1)} %copy-done.9, bf16[8,2,64,1152]{3,2,1,0:T(8,128)(2,1)} %all-to-all-done.2.rows), custom_call_target="tpu_custom_call" | custom-call | flops 301989888 | bytes 5000000 | tf_op jit(solution)/shard_map/pallas_call | solution.py:104
  (85 shorter events, 33.6 us)
Async XLA Ops:
  7.2 11.8 %copy-start.5 = (bf16[2,128,1152]{2,1,0:T(8,128)(2,1)S(1)}, bf16[2,128,1152]{2,1,0:T(8,128)(2,1)}, u32[]{:S(2)}) copy-start(bf16[2,128,1152]{2,1,0:T(8,128)(2,1)} %param.12) | copy-start | bytes 1769476
  7.2 81.7 %all-gather.3.cloned.1.call-start = ((), (), s32[]{:S(2)}) async-start(), calls=%async_computation.7 | async-start | bytes 5013504 | tf_op jit(solution)/shard_map/all_gather | solution.py:306
  10.2 10.7 %collective-permute-start.3 = (bf16[2,1168,128]{2,1,0:T(8,128)(2,1)S(1)}, bf16[2,1168,128]{2,1,0:T(8,128)(2,1)S(1)}, u32[]{:S(2)}, u32[]{:S(2)}) collective-permute-start(bf16[2,1168,128]{2,1,0:T(8,128)(2,1)S(1)} %get-tuple-element.61), channel_id=1, source_target_pairs={{0,256},{256,0},{1,257},{257,1},{2,258},{258,2},{3,259},{259,3},{4... | collective-permute-start | bytes 1794056 | tf_op jit(solution)/shard_map/ppermute | solution.py:22
  19.0 5.0 %collective-permute-start = (bf16[2,128,1152]{2,1,0:T(8,128)(2,1)S(1)}, bf16[2,128,1152]{2,1,0:T(8,128)(2,1)S(1)}, u32[]{:S(2)}, u32[]{:S(2)}) collective-permute-start(bf16[2,128,1152]{2,1,0:T(8,128)(2,1)S(1)} %copy-done.5), channel_id=1, source_target_pairs={{0,256},{256,0},{1,257},{257,1},{2,258},{258,2},{3,259},{259,3},{4... | collective-permute-start | bytes 1769480 | tf_op jit(solution)/shard_map/ppermute | solution.py:22
  20.9 6.3 %copy-start.13 = (s32[128]{0:T(128)S(1)}, s32[128]{0:T(128)}, u32[]{:S(2)}) copy-start(s32[128]{0:T(128)} %param.8) | copy-start | bytes 1540
  20.9 6.3 %copy-start.12 = (s32[128,4]{0,1:T(4,128)S(1)}, s32[128,4]{0,1:T(4,128)}, u32[]{:S(2)}) copy-start(s32[128,4]{0,1:T(4,128)} %param.9) | copy-start | bytes 6148
  22.1 30.4 %collective-permute-start.4 = (bf16[2,2,1168,128]{3,2,1,0:T(8,128)(2,1)}, bf16[2,2,1168,128]{3,2,1,0:T(8,128)(2,1)S(1)}, u32[]{:S(2)}, u32[]{:S(2)}) collective-permute-start(bf16[2,2,1168,128]{3,2,1,0:T(8,128)(2,1)} %pad_maximum_fusion.2), channel_id=1, source_target_pairs={{0,64},{64,128},{128,192},{192,0},{256,448},{320,256},{384,320},{4... | collective-permute-start | bytes 3588104 | tf_op jit(solution)/shard_map/ppermute | solution.py:28
  25.2 27.2 %collective-permute-start.1 = (bf16[2,2,128,1152]{3,2,1,0:T(8,128)(2,1)}, bf16[2,2,128,1152]{3,2,1,0:T(8,128)(2,1)S(1)}, u32[]{:S(2)}, u32[]{:S(2)}) collective-permute-start(bf16[2,2,128,1152]{3,2,1,0:T(8,128)(2,1)} %pad_maximum_fusion.3), channel_id=1, source_target_pairs={{0,64},{64,128},{128,192},{192,0},{256,448},{320,256},{384,320},{4... | collective-permute-start | bytes 3538952 | tf_op jit(solution)/shard_map/ppermute | solution.py:28
  27.8 24.4 %all-to-all-start = ((s32[16,4,128]{2,1,0:T(4,128)}), s32[16,4,128]{2,1,0:T(4,128)S(1)}, u32[]{:S(2)}, u32[]{:S(2)}) async-start(s32[16,4,128]{2,1,0:T(4,128)} %broadcast_in_dim.48), calls=%async_computation | async-start | bytes 65536 | tf_op jit(solution)/shard_map/all_to_all | solution.py:312
  52.5 11.1 %collective-permute-start.5 = (bf16[2,1168,128]{2,1,0:T(8,128)(2,1)S(1)}, bf16[2,1168,128]{2,1,0:T(8,128)(2,1)S(1)}, u32[]{:S(2)}, u32[]{:S(2)}) collective-permute-start(bf16[2,1168,128]{2,1,0:T(8,128)(2,1)S(1)} %slice_bitcast_fusion), channel_id=1, source_target_pairs={{0,64},{64,128},{128,192},{192,0},{256,448},{320,256},{384,320},{4... | collective-permute-start | bytes 1794056 | tf_op jit(solution)/shard_map/ppermute | solution.py:28
  56.5 21.9 %collective-permute-start.2 = (bf16[2,128,1152]{2,1,0:T(8,128)(2,1)}, bf16[2,128,1152]{2,1,0:T(8,128)(2,1)}, u32[]{:S(2)}, u32[]{:S(2)}) collective-permute-start(bf16[2,128,1152]{2,1,0:T(8,128)(2,1)} %slice_bitcast_fusion.1), channel_id=1, source_target_pairs={{0,64},{64,128},{128,192},{192,0},{256,448},{320,256},{384,320},{4... | collective-permute-start | bytes 1769480 | tf_op jit(solution)/shard_map/ppermute | solution.py:28
  65.4 17.1 %collective-permute-start.6 = (bf16[4,2,1168,128]{3,2,1,0:T(8,128)(2,1)}, bf16[4,2,1168,128]{3,2,1,0:T(8,128)(2,1)}, u32[]{:S(2)}, u32[]{:S(2)}) collective-permute-start(bf16[4,2,1168,128]{3,2,1,0:T(8,128)(2,1)} %pad_maximum_fusion), channel_id=1, source_target_pairs={{0,256},{256,0},{1,257},{257,1},{2,258},{258,2},{3,259},{259,3},{4... | collective-permute-start | bytes 7176200 | tf_op jit(solution)/shard_map/ppermute | solution.py:22
  77.2 1.2 copy-start.6
  79.8 16.4 %copy-start.1 = (bf16[4,2,128,1152]{3,2,1,0:T(8,128)(2,1)}, bf16[4,2,128,1152]{3,2,1,0:T(8,128)(2,1)S(1)}, u32[]{:S(2)}) copy-start(bf16[4,2,128,1152]{3,2,1,0:T(8,128)(2,1)S(1)} %pad_maximum_fusion.1) | copy-start | bytes 7077892
  79.8 20.4 %collective-permute-start.7 = (bf16[4,2,128,1152]{3,2,1,0:T(8,128)(2,1)S(1)}, bf16[4,2,128,1152]{3,2,1,0:T(8,128)(2,1)}, u32[]{:S(2)}, u32[]{:S(2)}) collective-permute-start(bf16[4,2,128,1152]{3,2,1,0:T(8,128)(2,1)S(1)} %pad_maximum_fusion.1), channel_id=1, source_target_pairs={{0,256},{256,0},{1,257},{257,1},{2,258},{258,2},{3,259},{259,3},{4... | collective-permute-start | bytes 7077896 | tf_op jit(solution)/shard_map/ppermute | solution.py:22
  96.2 13.7 %all-to-all-start.1 = ((bf16[4,16,64,128]{3,2,1,0:T(8,128)(2,1)}), bf16[4,16,64,128]{3,2,1,0:T(8,128)(2,1)S(1)}, u32[]{:S(2)}, u32[]{:S(2)}) async-start(bf16[4,16,64,128]{3,2,1,0:T(8,128)(2,1)} %shard_map.102), calls=%async_computation.1 | async-start | bytes 2097152 | tf_op jit(solution)/shard_map/all_to_all | solution.py:341
  100.2 93.8 %reduce-scatter.2.cloned.1.call-start = ((), (), s32[]{:S(2)}) async-start(), calls=%async_computation.8 | async-start | bytes 5013504 | tf_op jit(solution)/shard_map/reduce_scatter | solution.py:344
  124.7 14.1 %copy-start.2 = (bf16[4,2,128,1152]{3,2,1,0:T(8,128)(2,1)S(1)}, bf16[4,2,128,1152]{3,2,1,0:T(8,128)(2,1)}, u32[]{:S(2)}) copy-start(bf16[4,2,128,1152]{3,2,1,0:T(8,128)(2,1)} %copy-done.1) | copy-start | bytes 7077892
  124.7 43.4 %all-to-all-start.2 = ((bf16[8,2,64,1152]{3,2,1,0:T(8,128)(2,1)}), bf16[8,2,64,1152]{3,2,1,0:T(8,128)(2,1)}, u32[]{:S(2)}, u32[]{:S(2)}) async-start(bf16[8,2,64,1152]{3,2,1,0:T(8,128)(2,1)} %bitcast.63), calls=%async_computation.3 | async-start | bytes 4718592 | tf_op jit(solution)/shard_map/all_to_all | solution.py:301
  138.8 137.5 %all-gather.5.cloned.1.call-start = ((), (), s32[]{:S(2)}) async-start(), calls=%async_computation.9 | async-start | bytes 5013504 | tf_op jit(solution)/shard_map/all_gather | solution.py:306
  141.3 52.7 %copy-start.7 = (bf16[128,1152]{1,0:T(8,128)(2,1)S(1)}, bf16[128,1152]{1,0:T(8,128)(2,1)}, u32[]{:S(2)}) copy-start(bf16[128,1152]{1,0:T(8,128)(2,1)} %param.7) | copy-start | bytes 884740
  141.3 52.7 %copy-start.11 = (f32[1152]{0:T(1024)S(1)}, f32[1152]{0:T(1024)}, u32[]{:S(2)}) copy-start(f32[1152]{0:T(1024)} %param.13) | copy-start | bytes 13828
  145.7 64.1 %copy-start.10 = (f32[16,64,128]{2,1,0:T(8,128)S(1)}, f32[16,64,128]{2,1,0:T(8,128)}, u32[]{:S(2)}) copy-start(f32[16,64,128]{2,1,0:T(8,128)} %get-tuple-element.45) | copy-start | bytes 1572868
  195.9 20.4 %all-to-all-start.3 = ((bf16[8,2,64,128]{3,2,1,0:T(8,128)(2,1)}), bf16[8,2,64,128]{3,2,1,0:T(8,128)(2,1)S(1)}, u32[]{:S(2)}, u32[]{:S(2)}) async-start(bf16[8,2,64,128]{3,2,1,0:T(8,128)(2,1)} %bitcast.33), calls=%async_computation.4 | async-start | bytes 524288 | tf_op jit(solution)/shard_map/all_to_all | solution.py:301
  216.4 67.8 %copy-start.8 = (bf16[8,2,64,128]{3,2,1,0:T(8,128)(2,1)}, bf16[8,2,64,128]{3,2,1,0:T(8,128)(2,1)S(1)}, u32[]{:S(2)}) copy-start(bf16[8,2,64,128]{3,2,1,0:T(8,128)(2,1)S(1)} %all-to-all-done.3.values) | copy-start | bytes 786436
  284.2 12.8 %copy-start = (bf16[1,16,64,128]{3,2,1,0:T(8,128)(2,1)S(1)}, bf16[1,16,64,128]{3,2,1,0:T(8,128)(2,1)}, u32[]{:S(2)}) copy-start(bf16[1,16,64,128]{3,2,1,0:T(8,128)(2,1)} %get-tuple-element.50) | copy-start | bytes 786436
  284.2 41.8 %all-to-all-start.4 = ((bf16[8,2,64,1152]{3,2,1,0:T(8,128)(2,1)}), bf16[8,2,64,1152]{3,2,1,0:T(8,128)(2,1)S(1)}, u32[]{:S(2)}, u32[]{:S(2)}) async-start(bf16[8,2,64,1152]{3,2,1,0:T(8,128)(2,1)} %bitcast.69), calls=%async_computation.5 | async-start | bytes 4718592 | tf_op jit(solution)/shard_map/all_to_all | solution.py:301
  297.0 11.0 %collective-permute-start.8 = (bf16[16,64,128]{2,1,0:T(8,128)(2,1)S(1)}, bf16[16,64,128]{2,1,0:T(8,128)(2,1)S(1)}, u32[]{:S(2)}, u32[]{:S(2)}) collective-permute-start(bf16[16,64,128]{2,1,0:T(8,128)(2,1)S(1)} %bitcast.54), channel_id=1, source_target_pairs={{0,1},{1,2},{2,3},{3,0},{4,5},{5,6},{6,7},{7,4},{8,9},{9,10},{10,1... | collective-permute-start | bytes 786440 | tf_op jit(solution)/shard_map/ppermute | solution.py:181
  300.0 14.6 %collective-permute-start.9 = (bf16[16,64,128]{2,1,0:T(8,128)(2,1)S(1)}, bf16[16,64,128]{2,1,0:T(8,128)(2,1)S(1)}, u32[]{:S(2)}, u32[]{:S(2)}) collective-permute-start(bf16[16,64,128]{2,1,0:T(8,128)(2,1)S(1)} %bitcast.55), channel_id=1, source_target_pairs={{0,2},{1,3},{2,0},{3,1},{4,6},{5,7},{6,4},{7,5},{8,10},{9,11},{10,... | collective-permute-start | bytes 786440 | tf_op jit(solution)/shard_map/ppermute | solution.py:181
  304.5 11.3 %collective-permute-start.10 = (bf16[16,64,128]{2,1,0:T(8,128)(2,1)S(1)}, bf16[16,64,128]{2,1,0:T(8,128)(2,1)S(1)}, u32[]{:S(2)}, u32[]{:S(2)}) collective-permute-start(bf16[16,64,128]{2,1,0:T(8,128)(2,1)S(1)} %bitcast.56), channel_id=1, source_target_pairs={{0,3},{1,0},{2,1},{3,2},{4,7},{5,4},{6,5},{7,6},{8,11},{9,8},{10,9... | collective-permute-start | bytes 786440 | tf_op jit(solution)/shard_map/ppermute | solution.py:181
  326.0 3.7 %copy-start.3 = (bf16[8,2,64,1152]{3,2,1,0:T(8,128)(2,1)}, bf16[8,2,64,1152]{3,2,1,0:T(8,128)(2,1)S(1)}, u32[]{:S(2)}) copy-start(bf16[8,2,64,1152]{3,2,1,0:T(8,128)(2,1)S(1)} %all-to-all-done.4.rows) | copy-start | bytes 7077892
  326.0 10.3 %all-to-all-start.5 = ((bf16[8,2,64,128]{3,2,1,0:T(8,128)(2,1)}), bf16[8,2,64,128]{3,2,1,0:T(8,128)(2,1)S(1)}, u32[]{:S(2)}, u32[]{:S(2)}) async-start(bf16[8,2,64,128]{3,2,1,0:T(8,128)(2,1)} %bitcast.37), calls=%async_computation.6 | async-start | bytes 524288 | tf_op jit(solution)/shard_map/all_to_all | solution.py:301
  (2 other events, 1.7 us)
Sparse Core Ops, SparseCore 0:
  10.1 78.7 all-gather.2
  119.0 74.9 reduce-scatter.1
  196.7 79.5 all-gather.4

commit v6 on v5

--- a/solution.py
+++ b/solution.py
@@ -100,10 +100,10 @@
 ORDER = pl.BlockSpec(memory_space=pltpu.SMEM)
 
 
-def call(body, ins, in_specs, outs, out_specs, scratch, flops, moved):
+def call(steps, body, ins, in_specs, outs, out_specs, scratch, flops, moved):
     return pl.pallas_call(
         body,
-        grid=(TILES,),
+        grid=(steps,),
         in_specs=in_specs,
         out_specs=out_specs,
         out_shape=[jax.ShapeDtypeStruct(shape, kind) for shape, kind in outs],
@@ -118,6 +118,7 @@
     width = rows.shape[2]
     count = groups * wide // LOCAL
     return call(
+        TILES,
         take,
         (pick, rows),
         [whole(groups, wide, toks), columns(groups, toks, width // TILES)],
@@ -129,115 +130,155 @@
     )[0]
 
 
-def project_body(order, pick, rows, wa, wb, out, slots, total):
-    step = pl.program_id(0)
-
-    @pl.when(step == 0)
-    def _():
-        total[...] = jnp.zeros_like(total)
-
-    take(pick, rows, slots)
+def start(*pairs):
+    copies = [pltpu.make_async_copy(*pair) for pair in pairs]
+    for copy in copies:
+        copy.start()
+    return copies
+
+
+ANY = pl.BlockSpec(memory_space=pl.ANY)
+VMEM = pl.BlockSpec(memory_space=pltpu.VMEM)
+
+
+def staged(body, ins, in_specs, outs, out_specs, scratch, flops, moved):
+    return pl.pallas_call(
+        body,
+        in_specs=in_specs,
+        out_specs=out_specs,
+        out_shape=[jax.ShapeDtypeStruct(shape, kind) for shape, kind in outs],
+        scratch_shapes=scratch,
+        compiler_params=pltpu.CompilerParams(vmem_limit_bytes=58 * 1024 * 1024),
+        cost_estimate=pl.CostEstimate(flops=flops, bytes_accessed=moved, transcendentals=0),
+    )(*ins)
+
+
+def project_body(keep, order, pick, rows, wa, wb, out, *refs):
+    if keep:
+        kept, *refs = refs
+    held, moved, va, vb, slots, sems = refs
+    groups, wide, _ = pick.shape
+    each = wide // LOCAL
+    width = rows.shape[2]
+    parts = [
+        start((pick.at[q], held.at[q], sems.at[0, q]), (rows.at[q], moved.at[q], sems.at[1, q]))
+        for q in range(groups)
+    ]
+    weights = start(
+        (wa.at[:, pl.ds(0, width)], va, sems.at[2, 0]),
+        (wb.at[:, pl.ds(0, width)], vb, sems.at[2, 1]),
+    )
+    for q in range(groups):
+        for copy in parts[q]:
+            copy.wait()
+        taken = jnp.dot(held[q], moved[q], preferred_element_type=F32).astype(BF16)
+        slots[:, q * each : (q + 1) * each, :] = taken.reshape(LOCAL, each, width)
+    leaving = start((slots, kept, sems.at[2, 2])) if keep else []
+    for copy in weights:
+        copy.wait()
     for k in range(LOCAL):
-        w = placed(order, wa, wb, k, LOCAL // 8)
-        total[k] = total[k] + jnp.dot(slots[k], w, preferred_element_type=F32)
-
-    @pl.when(step == TILES - 1)
-    def _():
-        value = total[...].astype(BF16)
+        w = placed(order, va, vb, k, LOCAL // 8)
+        value = jnp.dot(slots[k], w, preferred_element_type=F32).astype(BF16)
         for c in range(out.shape[0]):
-            out[c] = value
+            out[c, k] = value
+    for copy in leaving:
+        copy.wait()
 
 
 def project(order, pick, rows, wa, wb, keep):
     groups, wide, toks = pick.shape
     half, _, latents = wa.shape
     width = rows.shape[2]
-    tile = width // TILES
     count = groups * wide // LOCAL
-    depth = pl.BlockSpec((half, tile, latents), lambda i: (0, i, 0))
-    copies = 1 if keep else 4
-    outs = [((copies, LOCAL, count, latents), BF16)]
-    out_specs = [whole(copies, LOCAL, count, latents)]
-    scratch = [pltpu.VMEM((LOCAL, count, latents), F32)]
+    outs = [((1 if keep else 4, LOCAL, count, latents), BF16)]
     if keep:
         outs.append(((LOCAL, count, width), BF16))
-        out_specs.append(columns(LOCAL, count, tile))
-    else:
-        scratch.insert(0, pltpu.VMEM((LOCAL, count, tile), BF16))
-    return call(
-        project_body,
+    return staged(
+        lambda *refs: project_body(keep, *refs),
         (order, pick, rows, wa, wb),
-        [ORDER, whole(groups, wide, toks), columns(groups, toks, tile), depth, depth],
+        [ORDER] + [ANY] * 4,
         outs,
-        out_specs,
-        scratch,
+        [VMEM, ANY][: len(outs)],
+        [
+            pltpu.VMEM((groups, wide, toks), BF16),
+            pltpu.VMEM((groups, toks, width), BF16),
+            pltpu.VMEM((half, width, latents), BF16),
+            pltpu.VMEM((half, width, latents), BF16),
+            pltpu.VMEM((LOCAL, count, width), BF16),
+            pltpu.SemaphoreType.DMA((3, 4)),
+        ],
         2 * groups * wide * toks * width,
         12_000_000,
     )
 
 
-def over_lat(part):
-    return [part] + [
-        lax.ppermute(part, "lat", [(i, (i + k) % 4) for i in range(4)]) for k in (1, 2, 3)
-    ]
-
-
-def sum_lat(a, b, c, d):
-    return (a.astype(F32) + c.astype(F32)) + (b.astype(F32) + d.astype(F32))
-
-
-def decode_body(order, copies, bias, turned, wa, wb, pre, act, home, part):
+def decode_body(order, copies, bias, turned, wa, wb, pre, act, home, got, held, va, vb, part, done, sems):
     groups, _, wide = turned.shape
     each = wide // LOCAL
-
-    @pl.when(pl.program_id(0) == 0)
-    def _():
-        for k in range(LOCAL):
-            owned = LOCAL // 8
-            at = order[k // owned] * owned + k % owned
-            value = sum_lat(*[copies[c, k] for c in range(4)]) + bias[at]
-            pre[k] = value
-            soft = jnp.maximum(value, 0.0) + jnp.log1p(jnp.exp(-jnp.abs(value)))
-            act[k] = soft.astype(BF16)
-
+    first = start((copies, got, sems.at[0, 0]))
+    weights = start((wa, va, sems.at[0, 1]), (wb, vb, sems.at[0, 2]))
+    tables = start((turned, held, sems.at[0, 3]))
+    for copy in first:
+        copy.wait()
+    owned = LOCAL // 8
     for k in range(LOCAL):
-        w = placed(order, wa, wb, k, LOCAL // 8)
+        at = order[k // owned] * owned + k % owned
+        value = sum_lat(*[got[c, k] for c in range(4)]) + bias[at]
+        pre[k] = value
+        soft = jnp.maximum(value, 0.0) + jnp.log1p(jnp.exp(-jnp.abs(value)))
+        act[k] = soft.astype(BF16)
+    for copy in weights:
+        copy.wait()
+    for k in range(LOCAL):
+        w = placed(order, va, vb, k, owned)
         part[k] = jnp.dot(act[k], w, preferred_element_type=F32).astype(BF16)
+    for copy in tables:
+        copy.wait()
+    leaving = []
     for q in range(groups):
         rows = part[:, q * each : (q + 1) * each, :].reshape(wide, part.shape[2])
-        home[q] = jnp.dot(turned[q], rows, preferred_element_type=F32).astype(BF16)
+        done[q] = jnp.dot(held[q], rows, preferred_element_type=F32).astype(BF16)
+        leaving += start((done.at[q], home.at[q], sems.at[1, q]))
+    for copy in leaving:
+        copy.wait()
 
 
 def decode(order, copies, bias, turned, wa, wb):
     groups, toks, wide = turned.shape
     half, latents, width = wa.shape
-    tile = width // TILES
     count = groups * wide // LOCAL
-    return call(
+    return staged(
         decode_body,
         (order, copies, bias, turned, wa, wb),
-        [
-            ORDER,
-            whole(4, LOCAL, count, latents),
-            whole(LOCAL, 1, latents),
-            whole(groups, toks, wide),
-            columns(half, latents, tile),
-            columns(half, latents, tile),
-        ],
+        [ORDER, ANY, VMEM, ANY, ANY, ANY],
         [
             ((LOCAL, count, latents), F32),
             ((LOCAL, count, latents), BF16),
             ((groups, toks, width), BF16),
         ],
+        [VMEM, VMEM, ANY],
         [
-            whole(LOCAL, count, latents),
-            whole(LOCAL, count, latents),
-            columns(groups, toks, tile),
+            pltpu.VMEM((4, LOCAL, count, latents), BF16),
+            pltpu.VMEM((groups, toks, wide), BF16),
+            pltpu.VMEM((half, latents, width), BF16),
+            pltpu.VMEM((half, latents, width), BF16),
+            pltpu.VMEM((LOCAL, count, width), BF16),
+            pltpu.VMEM((groups, toks, width), BF16),
+            pltpu.SemaphoreType.DMA((2, 4)),
         ],
-        [pltpu.VMEM((LOCAL, count, tile), BF16)],
         2 * groups * wide * toks * width,
         12_000_000,
     )
+
+
+def over_lat(part):
+    return [part] + [
+        lax.ppermute(part, "lat", [(i, (i + k) % 4) for i in range(4)]) for k in (1, 2, 3)
+    ]
+
+
+def sum_lat(a, b, c, d):
+    return (a.astype(F32) + c.astype(F32)) + (b.astype(F32) + d.astype(F32))
 
 
 def slope_body(a, b, c, d, sig, out):
@@ -274,13 +315,13 @@
 def outer(values, rows):
     peers, owned, count, width = rows.shape
     latents = values.shape[3]
-    tile = width // TILES
     return call(
+        1,
         outer_body,
         (values, rows),
-        [whole(peers, owned, count, latents), columns(peers, owned, count, tile)],
+        [whole(peers, owned, count, latents), columns(peers, owned, count, width)],
         [((owned, latents, width), BF16), ((owned, latents), F32)],
-        [columns(owned, latents, tile), whole(owned, latents)],
+        [columns(owned, latents, width), whole(owned, latents)],
         [pltpu.VMEM((owned, latents, peers * count), BF16)],
         4 * peers * count * width * latents,
         5_000_000,

time: 349 us -> 347 us (level)
  no operation moved by 1% of the time
where the time goes in v6:
time: 347 us; the launch traced here: 345 us
  waiting for transfers between devices  167 us (48%)
  starting transfers between devices  99.9 us (29%)
  Pallas kernels  34.9 us (10%)
  local copies, waits for them, and re-layouts  16.9 us (5%)
  between operations  14.1 us (4%)
  other arithmetic  12.4 us (4%)
    all_gather x2, waiting for transfers between devices, over_z(): v = lax.all_gather(v, 'z', axis=0, tiled=True)  64.8 us
    all_to_all x4, starting transfers between devices, to_owners(): lax.all_to_all(v.reshape(8, owned, *v.shape[1:]), ('sect', 'y'), 0, 0, ti...  44.8 us
    all_to_all x4, waiting for transfers between devices, to_owners(): lax.all_to_all(v.reshape(8, owned, *v.shape[1:]), ('sect', 'y'), 0, 0, ti...  41.5 us
    reduce_scatter x1, waiting for transfers between devices, shards(): lax.psum_scatter(home.reshape(NZ * tok_count, width), 'z', scatter_dimens...  25.4 us
    pallas_call x3, Pallas kernels, staged(): pl.pallas_call(body, in_specs=in_specs, out_specs=out_specs, out_shape=[j...  21.8 us
    ppermute x4, starting transfers between devices, swap_cores(): return lax.ppermute(v, 'sect', [(0, 1), (1, 0)])  18.9 us
    all_to_all x1, starting transfers between devices, shards(): lax.all_to_all(jnp.broadcast_to(global_block, (NZ, 4, tok_count)), 'z', 0...  12.7 us
    pallas_call x3, Pallas kernels, call(): pl.pallas_call(body, grid=(steps,), in_specs=in_specs, out_specs=out_spec...  12.1 us
  transfers between devices with their start and end apart: 20, of which 14 were waited for; matrix products, arithmetic and copies ran while one was open for 7% of the time, Pallas kernels for 5%

profile of v6, /device:TPU:1, one launch (start us, length us, event | category | flops | bytes accessed | tf_op | source)
XLA Modules:
  0.0 345.1 jit_solution(1771774210203912231)
XLA Ops:
  10.2 8.8 %collective-permute-start.3 = (bf16[2,1168,128]{2,1,0:T(8,128)(2,1)S(1)}, bf16[2,1168,128]{2,1,0:T(8,128)(2,1)S(1)}, u32[]{:S(2)}, u32[]{:S(2)}) collective-permute-start(bf16[2,1168,128]{2,1,0:T(8,128)(2,1)S(1)} %get-tuple-element.61), channel_id=1, source_target_pairs={{0,256},{256,0},{1,257},{257,1},{2,258},{258,2},{3,259},{259,3},{4... | collective-permute-start | bytes 1794056 | tf_op jit(solution)/shard_map/ppermute | solution.py:22
  27.8 12.7 %all-to-all-start = ((s32[16,4,128]{2,1,0:T(4,128)}), s32[16,4,128]{2,1,0:T(4,128)S(1)}, u32[]{:S(2)}, u32[]{:S(2)}) async-start(s32[16,4,128]{2,1,0:T(4,128)} %broadcast_in_dim.48), calls=%async_computation | async-start | bytes 65536 | tf_op jit(solution)/shard_map/all_to_all | solution.py:353
  41.2 11.1 %all-to-all-done = s32[16,4,128]{2,1,0:T(4,128)S(1)} async-done(((s32[16,4,128]{2,1,0:T(4,128)}), s32[16,4,128]{2,1,0:T(4,128)S(1)}, u32[]{:S(2)}, u32[]{:S(2)}) %all-to-all-start) | async-done | bytes 32800 | tf_op jit(solution)/shard_map/all_to_all | solution.py:353
  52.5 3.1 collective-permute-start.5
  58.4 5.2 %collective-permute-done.5 = bf16[2,1168,128]{2,1,0:T(8,128)(2,1)S(1)} collective-permute-done((bf16[2,1168,128]{2,1,0:T(8,128)(2,1)S(1)}, bf16[2,1168,128]{2,1,0:T(8,128)(2,1)S(1)}, u32[]{:S(2)}, u32[]{:S(2)}) %collective-permute-start.5) | collective-permute-done | bytes 598048 | tf_op jit(solution)/shard_map/ppermute | solution.py:28
  65.4 6.3 %collective-permute-start.6 = (bf16[4,2,1168,128]{3,2,1,0:T(8,128)(2,1)}, bf16[4,2,1168,128]{3,2,1,0:T(8,128)(2,1)}, u32[]{:S(2)}, u32[]{:S(2)}) collective-permute-start(bf16[4,2,1168,128]{3,2,1,0:T(8,128)(2,1)} %pad_maximum_fusion), channel_id=1, source_target_pairs={{0,256},{256,0},{1,257},{257,1},{2,258},{258,2},{3,259},{259,3},{4... | collective-permute-start | bytes 7176200 | tf_op jit(solution)/shard_map/ppermute | solution.py:22
  74.9 1.9 copy.47
  83.9 5.0 %all-gather.3.cloned.1.call-done = bf16[2048,1152]{1,0:T(8,128)(2,1)} async-done(((bf16[128,1152]{1,0:T(8,128)(2,1)}), bf16[2048,1152]{1,0:T(8,128)(2,1)}) %all-gather.3.cloned.1.call-update) | async-done | bytes 4718608 | tf_op jit(solution)/shard_map/all_gather | solution.py:347
  88.9 7.1 %shard_map.102 = bf16[4,16,64,128]{3,2,1,0:T(8,128)(2,1)} custom-call(s32[8]{0:T(128)} %compare_select_fusion.6.refs_0_.order, bf16[4,256,512]{2,1,0:T(8,128)(2,1)} %fusion.1.refs_1_.pick, bf16[4,512,1152]{2,1,0:T(8,128)(2,1)} %bitcast.59, bf16[8,1168,128]{2,1,0:T(8,128)(2,1)} %bitcast.19.refs_3_, bf16[8,1168,128]{2,1,0:T(8,128)(2,1)} %bitcast.20.refs_4_), custom_call_target="tpu_custom_call" | custom-call | flops 1207959552 | bytes 12000000 | tf_op jit(solution)/shard_map/pallas_call | solution.py:145
  96.0 4.0 %all-to-all-start.1 = ((bf16[4,16,64,128]{3,2,1,0:T(8,128)(2,1)}), bf16[4,16,64,128]{3,2,1,0:T(8,128)(2,1)S(1)}, u32[]{:S(2)}, u32[]{:S(2)}) async-start(bf16[4,16,64,128]{3,2,1,0:T(8,128)(2,1)} %shard_map.102), calls=%async_computation.1 | async-start | bytes 2097152 | tf_op jit(solution)/shard_map/all_to_all | solution.py:382
  100.0 9.7 %all-to-all-done.1.copies = bf16[4,16,64,128]{3,2,1,0:T(8,128)(2,1)S(1)} async-done(((bf16[4,16,64,128]{3,2,1,0:T(8,128)(2,1)}), bf16[4,16,64,128]{3,2,1,0:T(8,128)(2,1)S(1)}, u32[]{:S(2)}, u32[]{:S(2)}) %all-to-all-start.1) | async-done | bytes 1048608 | tf_op jit(solution)/shard_map/all_to_all | solution.py:382
  110.7 7.9 %shard_map.103 = (f32[16,64,128]{2,1,0:T(8,128)}, bf16[16,64,128]{2,1,0:T(8,128)(2,1)}, bf16[4,512,1152]{2,1,0:T(8,128)(2,1)}) custom-call(s32[8]{0:T(128)} %compare_select_fusion.6.refs_0_.order, bf16[4,16,64,128]{3,2,1,0:T(8,128)(2,1)} %copy-done.4, f32[16,1,128]{2,1,0:T(1,128)} %bitcast.79, bf16[4,512,256]{2,1,0:T(8,128)(2,1)} %compare_convert_fusion.turned, ...), custom_call_target="tpu_custom_call" | custom-call | flops 1207959552 | bytes 12000000 | tf_op jit(solution)/shard_map/pallas_call | solution.py:145
  118.7 5.9 %shard_map.104 = bf16[16,64,1152]{2,1,0:T(8,128)(2,1)} custom-call(bf16[4,256,512]{2,1,0:T(8,128)(2,1)} %fusion.1.refs_1_.pick, bf16[4,512,1152]{2,1,0:T(8,128)(2,1)} %bitcast.60), custom_call_target="tpu_custom_call" | custom-call | flops 1207959552 | bytes 8000000 | tf_op jit(solution)/shard_map/pallas_call | solution.py:104
  124.6 14.1 %all-to-all-start.2 = ((bf16[8,2,64,1152]{3,2,1,0:T(8,128)(2,1)}), bf16[8,2,64,1152]{3,2,1,0:T(8,128)(2,1)}, u32[]{:S(2)}, u32[]{:S(2)}) async-start(bf16[8,2,64,1152]{3,2,1,0:T(8,128)(2,1)} %bitcast.63), calls=%async_computation.3 | async-start | bytes 4718592 | tf_op jit(solution)/shard_map/all_to_all | solution.py:342
  138.7 2.5 copy.51
  141.2 4.4 %copy.52 = bf16[4,2,128,1152]{2,3,1,0:T(8,128)(2,1)} copy(bf16[4,2,128,1152]{3,2,1,0:T(8,128)(2,1)} %collective-permute-done.7) | data formatting | bytes 4718592 | tf_op jit(solution)/shard_map/ppermute | solution.py:22
  145.5 22.4 %all-to-all-done.2.rows = bf16[8,2,64,1152]{3,2,1,0:T(8,128)(2,1)} async-done(((bf16[8,2,64,1152]{3,2,1,0:T(8,128)(2,1)}), bf16[8,2,64,1152]{3,2,1,0:T(8,128)(2,1)}, u32[]{:S(2)}, u32[]{:S(2)}) %all-to-all-start.2) | async-done | bytes 2359328 | tf_op jit(solution)/shard_map/all_to_all | solution.py:342
  168.0 25.4 %reduce-scatter.2.cloned.1.call-done = bf16[128,1152]{1,0:T(8,128)(2,1)} async-done(((bf16[2048,1152]{1,0:T(8,128)(2,1)}), bf16[128,1152]{1,0:T(8,128)(2,1)}) %reduce-scatter.2.cloned.1.call-update) | async-done | bytes 294928 | tf_op jit(solution)/shard_map/reduce_scatter | solution.py:385
  195.3 14.2 %all-to-all-start.3 = ((bf16[8,2,64,128]{3,2,1,0:T(8,128)(2,1)}), bf16[8,2,64,128]{3,2,1,0:T(8,128)(2,1)S(1)}, u32[]{:S(2)}, u32[]{:S(2)}) async-start(bf16[8,2,64,128]{3,2,1,0:T(8,128)(2,1)} %bitcast.33), calls=%async_computation.4 | async-start | bytes 524288 | tf_op jit(solution)/shard_map/all_to_all | solution.py:342
  209.7 6.4 %all-to-all-done.3.values = bf16[8,2,64,128]{3,2,1,0:T(8,128)(2,1)S(1)} async-done(((bf16[8,2,64,128]{3,2,1,0:T(8,128)(2,1)}), bf16[8,2,64,128]{3,2,1,0:T(8,128)(2,1)S(1)}, u32[]{:S(2)}, u32[]{:S(2)}) %all-to-all-start.3) | async-done | bytes 262176 | tf_op jit(solution)/shard_map/all_to_all | solution.py:342
  216.0 59.8 %all-gather.5.cloned.1.call-done = bf16[2048,1152]{1,0:T(8,128)(2,1)} async-done(((bf16[128,1152]{1,0:T(8,128)(2,1)}), bf16[2048,1152]{1,0:T(8,128)(2,1)}) %all-gather.5.cloned.1.call-update) | async-done | bytes 4718608 | tf_op jit(solution)/shard_map/all_gather | solution.py:347
  275.8 6.8 %shard_map.105 = (bf16[1,16,64,128]{3,2,1,0:T(8,128)(2,1)}, bf16[16,64,1152]{2,1,0:T(8,128)(2,1)}) custom-call(s32[8]{0:T(128)} %compare_select_fusion.6.refs_0_.order, bf16[4,256,512]{2,1,0:T(8,128)(2,1)} %fusion.1.refs_1_.pick, bf16[4,512,1152]{2,1,0:T(8,128)(2,1)} %bitcast.66, bf16[8,1152,128]{2,1,0:T(8,128)(2,1)} %bitcast.61, bf16[8,1152,128]{2,1,0:T(8,128)(2,1)} %bitcast.62), custom_call_target="tpu_custom_call" | custom-call | flops 1207959552 | bytes 12000000 | tf_op jit(solution)/shard_map/pallas_call | solution.py:145
  282.7 12.8 %all-to-all-start.4 = ((bf16[8,2,64,1152]{3,2,1,0:T(8,128)(2,1)}), bf16[8,2,64,1152]{3,2,1,0:T(8,128)(2,1)S(1)}, u32[]{:S(2)}, u32[]{:S(2)}) async-start(bf16[8,2,64,1152]{3,2,1,0:T(8,128)(2,1)} %bitcast.69), calls=%async_computation.5 | async-start | bytes 4718592 | tf_op jit(solution)/shard_map/all_to_all | solution.py:342
  295.4 3.1 collective-permute-start.8
  298.5 4.4 %collective-permute-start.9 = (bf16[16,64,128]{2,1,0:T(8,128)(2,1)S(1)}, bf16[16,64,128]{2,1,0:T(8,128)(2,1)S(1)}, u32[]{:S(2)}, u32[]{:S(2)}) collective-permute-start(bf16[16,64,128]{2,1,0:T(8,128)(2,1)S(1)} %bitcast.55), channel_id=1, source_target_pairs={{0,2},{1,3},{2,0},{3,1},{4,6},{5,7},{6,4},{7,5},{8,10},{9,11},{10,... | collective-permute-start | bytes 786440 | tf_op jit(solution)/shard_map/ppermute | solution.py:276
  302.9 3.0 collective-permute-start.10
  306.4 6.6 %collective-permute-done.9.c = bf16[16,64,128]{2,1,0:T(8,128)(2,1)S(1)} collective-permute-done((bf16[16,64,128]{2,1,0:T(8,128)(2,1)S(1)}, bf16[16,64,128]{2,1,0:T(8,128)(2,1)S(1)}, u32[]{:S(2)}, u32[]{:S(2)}) %collective-permute-start.9) | collective-permute-done | bytes 262176 | tf_op jit(solution)/shard_map/ppermute | solution.py:276
  315.1 9.4 %all-to-all-done.4.rows = bf16[8,2,64,1152]{3,2,1,0:T(8,128)(2,1)S(1)} async-done(((bf16[8,2,64,1152]{3,2,1,0:T(8,128)(2,1)}), bf16[8,2,64,1152]{3,2,1,0:T(8,128)(2,1)S(1)}, u32[]{:S(2)}, u32[]{:S(2)}) %all-to-all-start.4) | async-done | bytes 2359328 | tf_op jit(solution)/shard_map/all_to_all | solution.py:342
  324.5 3.7 %all-to-all-start.5 = ((bf16[8,2,64,128]{3,2,1,0:T(8,128)(2,1)}), bf16[8,2,64,128]{3,2,1,0:T(8,128)(2,1)S(1)}, u32[]{:S(2)}, u32[]{:S(2)}) async-start(bf16[8,2,64,128]{3,2,1,0:T(8,128)(2,1)} %bitcast.37), calls=%async_computation.6 | async-start | bytes 524288 | tf_op jit(solution)/shard_map/all_to_all | solution.py:342
  328.2 3.1 shard_map.108
  331.3 3.4 all-to-all-done.5.values
  335.4 3.1 shard_map.107
  (85 shorter events, 33.6 us)
Async XLA Ops:
  7.2 11.8 %copy-start.5 = (bf16[2,128,1152]{2,1,0:T(8,128)(2,1)S(1)}, bf16[2,128,1152]{2,1,0:T(8,128)(2,1)}, u32[]{:S(2)}) copy-start(bf16[2,128,1152]{2,1,0:T(8,128)(2,1)} %param.12) | copy-start | bytes 1769476
  7.2 81.7 %all-gather.3.cloned.1.call-start = ((), (), s32[]{:S(2)}) async-start(), calls=%async_computation.7 | async-start | bytes 5013504 | tf_op jit(solution)/shard_map/all_gather | solution.py:347
  10.2 10.7 %collective-permute-start.3 = (bf16[2,1168,128]{2,1,0:T(8,128)(2,1)S(1)}, bf16[2,1168,128]{2,1,0:T(8,128)(2,1)S(1)}, u32[]{:S(2)}, u32[]{:S(2)}) collective-permute-start(bf16[2,1168,128]{2,1,0:T(8,128)(2,1)S(1)} %get-tuple-element.61), channel_id=1, source_target_pairs={{0,256},{256,0},{1,257},{257,1},{2,258},{258,2},{3,259},{259,3},{4... | collective-permute-start | bytes 1794056 | tf_op jit(solution)/shard_map/ppermute | solution.py:22
  19.0 5.0 %collective-permute-start = (bf16[2,128,1152]{2,1,0:T(8,128)(2,1)S(1)}, bf16[2,128,1152]{2,1,0:T(8,128)(2,1)S(1)}, u32[]{:S(2)}, u32[]{:S(2)}) collective-permute-start(bf16[2,128,1152]{2,1,0:T(8,128)(2,1)S(1)} %copy-done.5), channel_id=1, source_target_pairs={{0,256},{256,0},{1,257},{257,1},{2,258},{258,2},{3,259},{259,3},{4... | collective-permute-start | bytes 1769480 | tf_op jit(solution)/shard_map/ppermute | solution.py:22
  20.9 6.3 %copy-start.13 = (s32[128]{0:T(128)S(1)}, s32[128]{0:T(128)}, u32[]{:S(2)}) copy-start(s32[128]{0:T(128)} %param.8) | copy-start | bytes 1540
  20.9 6.3 %copy-start.12 = (s32[128,4]{0,1:T(4,128)S(1)}, s32[128,4]{0,1:T(4,128)}, u32[]{:S(2)}) copy-start(s32[128,4]{0,1:T(4,128)} %param.9) | copy-start | bytes 6148
  22.1 30.4 %collective-permute-start.4 = (bf16[2,2,1168,128]{3,2,1,0:T(8,128)(2,1)}, bf16[2,2,1168,128]{3,2,1,0:T(8,128)(2,1)S(1)}, u32[]{:S(2)}, u32[]{:S(2)}) collective-permute-start(bf16[2,2,1168,128]{3,2,1,0:T(8,128)(2,1)} %pad_maximum_fusion.2), channel_id=1, source_target_pairs={{0,64},{64,128},{128,192},{192,0},{256,448},{320,256},{384,320},{4... | collective-permute-start | bytes 3588104 | tf_op jit(solution)/shard_map/ppermute | solution.py:28
  25.2 27.2 %collective-permute-start.1 = (bf16[2,2,128,1152]{3,2,1,0:T(8,128)(2,1)}, bf16[2,2,128,1152]{3,2,1,0:T(8,128)(2,1)S(1)}, u32[]{:S(2)}, u32[]{:S(2)}) collective-permute-start(bf16[2,2,128,1152]{3,2,1,0:T(8,128)(2,1)} %pad_maximum_fusion.3), channel_id=1, source_target_pairs={{0,64},{64,128},{128,192},{192,0},{256,448},{320,256},{384,320},{4... | collective-permute-start | bytes 3538952 | tf_op jit(solution)/shard_map/ppermute | solution.py:28
  27.8 24.4 %all-to-all-start = ((s32[16,4,128]{2,1,0:T(4,128)}), s32[16,4,128]{2,1,0:T(4,128)S(1)}, u32[]{:S(2)}, u32[]{:S(2)}) async-start(s32[16,4,128]{2,1,0:T(4,128)} %broadcast_in_dim.48), calls=%async_computation | async-start | bytes 65536 | tf_op jit(solution)/shard_map/all_to_all | solution.py:353
  52.5 11.1 %collective-permute-start.5 = (bf16[2,1168,128]{2,1,0:T(8,128)(2,1)S(1)}, bf16[2,1168,128]{2,1,0:T(8,128)(2,1)S(1)}, u32[]{:S(2)}, u32[]{:S(2)}) collective-permute-start(bf16[2,1168,128]{2,1,0:T(8,128)(2,1)S(1)} %slice_bitcast_fusion), channel_id=1, source_target_pairs={{0,64},{64,128},{128,192},{192,0},{256,448},{320,256},{384,320},{4... | collective-permute-start | bytes 1794056 | tf_op jit(solution)/shard_map/ppermute | solution.py:28
  56.5 21.9 %collective-permute-start.2 = (bf16[2,128,1152]{2,1,0:T(8,128)(2,1)}, bf16[2,128,1152]{2,1,0:T(8,128)(2,1)}, u32[]{:S(2)}, u32[]{:S(2)}) collective-permute-start(bf16[2,128,1152]{2,1,0:T(8,128)(2,1)} %slice_bitcast_fusion.1), channel_id=1, source_target_pairs={{0,64},{64,128},{128,192},{192,0},{256,448},{320,256},{384,320},{4... | collective-permute-start | bytes 1769480 | tf_op jit(solution)/shard_map/ppermute | solution.py:28
  65.4 17.1 %collective-permute-start.6 = (bf16[4,2,1168,128]{3,2,1,0:T(8,128)(2,1)}, bf16[4,2,1168,128]{3,2,1,0:T(8,128)(2,1)}, u32[]{:S(2)}, u32[]{:S(2)}) collective-permute-start(bf16[4,2,1168,128]{3,2,1,0:T(8,128)(2,1)} %pad_maximum_fusion), channel_id=1, source_target_pairs={{0,256},{256,0},{1,257},{257,1},{2,258},{258,2},{3,259},{259,3},{4... | collective-permute-start | bytes 7176200 | tf_op jit(solution)/shard_map/ppermute | solution.py:22
  77.2 1.2 copy-start.6
  79.8 16.2 %copy-start.1 = (bf16[4,2,128,1152]{3,2,1,0:T(8,128)(2,1)}, bf16[4,2,128,1152]{3,2,1,0:T(8,128)(2,1)S(1)}, u32[]{:S(2)}) copy-start(bf16[4,2,128,1152]{3,2,1,0:T(8,128)(2,1)S(1)} %pad_maximum_fusion.1) | copy-start | bytes 7077892
  79.8 20.2 %collective-permute-start.7 = (bf16[4,2,128,1152]{3,2,1,0:T(8,128)(2,1)S(1)}, bf16[4,2,128,1152]{3,2,1,0:T(8,128)(2,1)}, u32[]{:S(2)}, u32[]{:S(2)}) collective-permute-start(bf16[4,2,128,1152]{3,2,1,0:T(8,128)(2,1)S(1)} %pad_maximum_fusion.1), channel_id=1, source_target_pairs={{0,256},{256,0},{1,257},{257,1},{2,258},{258,2},{3,259},{259,3},{4... | collective-permute-start | bytes 7077896 | tf_op jit(solution)/shard_map/ppermute | solution.py:22
  96.0 13.7 %all-to-all-start.1 = ((bf16[4,16,64,128]{3,2,1,0:T(8,128)(2,1)}), bf16[4,16,64,128]{3,2,1,0:T(8,128)(2,1)S(1)}, u32[]{:S(2)}, u32[]{:S(2)}) async-start(bf16[4,16,64,128]{3,2,1,0:T(8,128)(2,1)} %shard_map.102), calls=%async_computation.1 | async-start | bytes 2097152 | tf_op jit(solution)/shard_map/all_to_all | solution.py:382
  100.0 93.4 %reduce-scatter.2.cloned.1.call-start = ((), (), s32[]{:S(2)}) async-start(), calls=%async_computation.8 | async-start | bytes 5013504 | tf_op jit(solution)/shard_map/reduce_scatter | solution.py:385
  124.6 14.1 %copy-start.2 = (bf16[4,2,128,1152]{3,2,1,0:T(8,128)(2,1)S(1)}, bf16[4,2,128,1152]{3,2,1,0:T(8,128)(2,1)}, u32[]{:S(2)}) copy-start(bf16[4,2,128,1152]{3,2,1,0:T(8,128)(2,1)} %copy-done.1) | copy-start | bytes 7077892
  124.6 43.4 %all-to-all-start.2 = ((bf16[8,2,64,1152]{3,2,1,0:T(8,128)(2,1)}), bf16[8,2,64,1152]{3,2,1,0:T(8,128)(2,1)}, u32[]{:S(2)}, u32[]{:S(2)}) async-start(bf16[8,2,64,1152]{3,2,1,0:T(8,128)(2,1)} %bitcast.63), calls=%async_computation.3 | async-start | bytes 4718592 | tf_op jit(solution)/shard_map/all_to_all | solution.py:342
  138.7 137.2 %all-gather.5.cloned.1.call-start = ((), (), s32[]{:S(2)}) async-start(), calls=%async_computation.9 | async-start | bytes 5013504 | tf_op jit(solution)/shard_map/all_gather | solution.py:347
  141.2 52.2 %copy-start.7 = (bf16[128,1152]{1,0:T(8,128)(2,1)S(1)}, bf16[128,1152]{1,0:T(8,128)(2,1)}, u32[]{:S(2)}) copy-start(bf16[128,1152]{1,0:T(8,128)(2,1)} %param.7) | copy-start | bytes 884740
  141.2 52.2 %copy-start.11 = (f32[1152]{0:T(1024)S(1)}, f32[1152]{0:T(1024)}, u32[]{:S(2)}) copy-start(f32[1152]{0:T(1024)} %param.13) | copy-start | bytes 13828
  145.5 63.9 %copy-start.10 = (f32[16,64,128]{2,1,0:T(8,128)S(1)}, f32[16,64,128]{2,1,0:T(8,128)}, u32[]{:S(2)}) copy-start(f32[16,64,128]{2,1,0:T(8,128)} %get-tuple-element.45) | copy-start | bytes 1572868
  195.3 20.8 %all-to-all-start.3 = ((bf16[8,2,64,128]{3,2,1,0:T(8,128)(2,1)}), bf16[8,2,64,128]{3,2,1,0:T(8,128)(2,1)S(1)}, u32[]{:S(2)}, u32[]{:S(2)}) async-start(bf16[8,2,64,128]{3,2,1,0:T(8,128)(2,1)} %bitcast.33), calls=%async_computation.4 | async-start | bytes 524288 | tf_op jit(solution)/shard_map/all_to_all | solution.py:342
  216.0 66.6 %copy-start.8 = (bf16[8,2,64,128]{3,2,1,0:T(8,128)(2,1)}, bf16[8,2,64,128]{3,2,1,0:T(8,128)(2,1)S(1)}, u32[]{:S(2)}) copy-start(bf16[8,2,64,128]{3,2,1,0:T(8,128)(2,1)S(1)} %all-to-all-done.3.values) | copy-start | bytes 786436
  282.6 12.8 %copy-start = (bf16[1,16,64,128]{3,2,1,0:T(8,128)(2,1)S(1)}, bf16[1,16,64,128]{3,2,1,0:T(8,128)(2,1)}, u32[]{:S(2)}) copy-start(bf16[1,16,64,128]{3,2,1,0:T(8,128)(2,1)} %get-tuple-element.50) | copy-start | bytes 786436
  282.7 41.8 %all-to-all-start.4 = ((bf16[8,2,64,1152]{3,2,1,0:T(8,128)(2,1)}), bf16[8,2,64,1152]{3,2,1,0:T(8,128)(2,1)S(1)}, u32[]{:S(2)}, u32[]{:S(2)}) async-start(bf16[8,2,64,1152]{3,2,1,0:T(8,128)(2,1)} %bitcast.69), calls=%async_computation.5 | async-start | bytes 4718592 | tf_op jit(solution)/shard_map/all_to_all | solution.py:342
  295.4 11.0 %collective-permute-start.8 = (bf16[16,64,128]{2,1,0:T(8,128)(2,1)S(1)}, bf16[16,64,128]{2,1,0:T(8,128)(2,1)S(1)}, u32[]{:S(2)}, u32[]{:S(2)}) collective-permute-start(bf16[16,64,128]{2,1,0:T(8,128)(2,1)S(1)} %bitcast.54), channel_id=1, source_target_pairs={{0,1},{1,2},{2,3},{3,0},{4,5},{5,6},{6,7},{7,4},{8,9},{9,10},{10,1... | collective-permute-start | bytes 786440 | tf_op jit(solution)/shard_map/ppermute | solution.py:276
  298.5 14.5 %collective-permute-start.9 = (bf16[16,64,128]{2,1,0:T(8,128)(2,1)S(1)}, bf16[16,64,128]{2,1,0:T(8,128)(2,1)S(1)}, u32[]{:S(2)}, u32[]{:S(2)}) collective-permute-start(bf16[16,64,128]{2,1,0:T(8,128)(2,1)S(1)} %bitcast.55), channel_id=1, source_target_pairs={{0,2},{1,3},{2,0},{3,1},{4,6},{5,7},{6,4},{7,5},{8,10},{9,11},{10,... | collective-permute-start | bytes 786440 | tf_op jit(solution)/shard_map/ppermute | solution.py:276
  302.9 11.3 %collective-permute-start.10 = (bf16[16,64,128]{2,1,0:T(8,128)(2,1)S(1)}, bf16[16,64,128]{2,1,0:T(8,128)(2,1)S(1)}, u32[]{:S(2)}, u32[]{:S(2)}) collective-permute-start(bf16[16,64,128]{2,1,0:T(8,128)(2,1)S(1)} %bitcast.56), channel_id=1, source_target_pairs={{0,3},{1,0},{2,1},{3,2},{4,7},{5,4},{6,5},{7,6},{8,11},{9,8},{10,9... | collective-permute-start | bytes 786440 | tf_op jit(solution)/shard_map/ppermute | solution.py:276
  324.5 3.7 %copy-start.3 = (bf16[8,2,64,1152]{3,2,1,0:T(8,128)(2,1)}, bf16[8,2,64,1152]{3,2,1,0:T(8,128)(2,1)S(1)}, u32[]{:S(2)}) copy-start(bf16[8,2,64,1152]{3,2,1,0:T(8,128)(2,1)S(1)} %all-to-all-done.4.rows) | copy-start | bytes 7077892
  324.5 10.3 %all-to-all-start.5 = ((bf16[8,2,64,128]{3,2,1,0:T(8,128)(2,1)}), bf16[8,2,64,128]{3,2,1,0:T(8,128)(2,1)S(1)}, u32[]{:S(2)}, u32[]{:S(2)}) async-start(bf16[8,2,64,128]{3,2,1,0:T(8,128)(2,1)} %bitcast.37), calls=%async_computation.6 | async-start | bytes 524288 | tf_op jit(solution)/shard_map/all_to_all | solution.py:342
  (2 other events, 1.7 us)
Sparse Core Ops, SparseCore 0:
  10.1 78.7 all-gather.2
  118.8 74.5 reduce-scatter.1
  196.0 79.7 all-gather.4

commit v7 on v6

--- a/solution.py
+++ b/solution.py
@@ -271,6 +271,68 @@
     )
 
 
+def pick_body(pick, rows, out, held, moved, sems):
+    groups, wide, _ = pick.shape
+    each = wide // LOCAL
+    parts = [
+        start((pick.at[q], held.at[q], sems.at[0, q]), (rows.at[q], moved.at[q], sems.at[1, q]))
+        for q in range(groups)
+    ]
+    for q in range(groups):
+        for copy in parts[q]:
+            copy.wait()
+        taken = jnp.dot(held[q], moved[q], preferred_element_type=F32).astype(BF16)
+        out[:, q * each : (q + 1) * each, :] = taken.reshape(LOCAL, each, rows.shape[2])
+
+
+def pick_slots(pick, rows):
+    groups, wide, toks = pick.shape
+    width = rows.shape[2]
+    return staged(
+        pick_body,
+        (pick, rows),
+        [ANY, ANY],
+        [((LOCAL, groups * wide // LOCAL, width), BF16)],
+        [VMEM],
+        [
+            pltpu.VMEM((groups, wide, toks), BF16),
+            pltpu.VMEM((groups, toks, width), BF16),
+            pltpu.SemaphoreType.DMA((2, 4)),
+        ],
+        2 * groups * wide * toks * width,
+        8_000_000,
+    )[0]
+
+
+def inward_body(order, slots, wa, wb, out, held, va, vb, sems):
+    copies = start((slots, held, sems.at[0]), (wa, va, sems.at[1]), (wb, vb, sems.at[2]))
+    for copy in copies:
+        copy.wait()
+    for k in range(LOCAL):
+        w = placed(order, va, vb, k, LOCAL // 8)
+        out[k] = jnp.dot(held[k], w, preferred_element_type=F32).astype(BF16)
+
+
+def inward(order, slots, wa, wb):
+    _, count, width = slots.shape
+    half, _, latents = wa.shape
+    return staged(
+        inward_body,
+        (order, slots, wa, wb),
+        [ORDER, ANY, ANY, ANY],
+        [((LOCAL, count, latents), BF16)],
+        [VMEM],
+        [
+            pltpu.VMEM((LOCAL, count, width), BF16),
+            pltpu.VMEM((half, width, latents), BF16),
+            pltpu.VMEM((half, width, latents), BF16),
+            pltpu.SemaphoreType.DMA((3,)),
+        ],
+        2 * LOCAL * count * width * latents,
+        8_000_000,
+    )[0]
+
+
 def over_lat(part):
     return [part] + [
         lax.ppermute(part, "lat", [(i, (i + k) % 4) for i in range(4)]) for k in (1, 2, 3)
@@ -398,9 +460,10 @@
     sig = jax.nn.sigmoid(pre) * present
     errors, owner_act, sig = tie(errors, owner_act, sig)
 
-    dact, error_slots = project(order, pick, errors, *turned_dec, True)
+    error_slots = pick_slots(pick, errors)
+    dact = inward(order, error_slots, *turned_dec)
     owner_errors = to_owners(error_slots)
-    slope, owner_errors = tie(slopes(dact[0], sig), owner_errors)
+    slope, owner_errors = tie(slopes(dact, sig), owner_errors)
     owner_slope = to_owners(slope)
     enc_grad, enc_bias_grad = outer(owner_slope, owner_rows)
     dec_grad, _ = outer(owner_act, owner_errors)

time: 347 us -> 344 us (level)
  waiting for transfers between devices: 167 us -> 161 us
  Pallas kernels: 34.9 us -> 38.7 us
    all_to_all x4, waiting for transfers between devices: 41.5 us -> 34.4 us  [to_owners(): lax.all_to_all(v.reshape(8, owned, *v.shape[1:]), ('sect', 'y'), 0, 0, ti...]
    pallas_call x3 -> x4, Pallas kernels: 21.8 us -> 25.7 us  [staged(): pl.pallas_call(body, in_specs=in_specs, out_specs=out_specs, out_shape=[j...]
  transfers between devices with their start and end apart: 20 -> 20, of which waited for: 14 -> 14; matrix products, arithmetic and copies ran while one was open for 7% -> 8% of each run, Pallas kernels for 5% -> 7%
where the time goes in v7:
time: 344 us; the launch traced here: 343 us
  waiting for transfers between devices  161 us (47%)
  starting transfers between devices  98.6 us (29%)
  Pallas kernels  38.7 us (11%)
  local copies, waits for them, and re-layouts  17.9 us (5%)
  between operations  14.1 us (4%)
  other arithmetic  12.4 us (4%)
    all_gather x2, waiting for transfers between devices, over_z(): v = lax.all_gather(v, 'z', axis=0, tiled=True)  65.3 us
    all_to_all x4, starting transfers between devices, to_owners(): lax.all_to_all(v.reshape(8, owned, *v.shape[1:]), ('sect', 'y'), 0, 0, ti...  43.5 us
    all_to_all x4, waiting for transfers between devices, to_owners(): lax.all_to_all(v.reshape(8, owned, *v.shape[1:]), ('sect', 'y'), 0, 0, ti...  34.4 us
    reduce_scatter x1, waiting for transfers between devices, shards(): lax.psum_scatter(home.reshape(NZ * tok_count, width), 'z', scatter_dimens...  26.1 us
    pallas_call x4, Pallas kernels, staged(): pl.pallas_call(body, in_specs=in_specs, out_specs=out_specs, out_shape=[j...  25.7 us
    ppermute x4, starting transfers between devices, swap_cores(): return lax.ppermute(v, 'sect', [(0, 1), (1, 0)])  18.9 us
    all_to_all x1, starting transfers between devices, shards(): lax.all_to_all(jnp.broadcast_to(global_block, (NZ, 4, tok_count)), 'z', 0...  12.7 us
    pallas_call x3, Pallas kernels, call(): pl.pallas_call(body, grid=(steps,), in_specs=in_specs, out_specs=out_spec...  12.2 us
  transfers between devices with their start and end apart: 20, of which 14 were waited for; matrix products, arithmetic and copies ran while one was open for 8% of the time, Pallas kernels for 7%

profile of v7, /device:TPU:1, one launch (start us, length us, event | category | flops | bytes accessed | tf_op | source)
XLA Modules:
  0.0 343.0 jit_solution(9709628728257691608)
XLA Ops:
  10.2 8.8 %collective-permute-start.3 = (bf16[2,1168,128]{2,1,0:T(8,128)(2,1)S(1)}, bf16[2,1168,128]{2,1,0:T(8,128)(2,1)S(1)}, u32[]{:S(2)}, u32[]{:S(2)}) collective-permute-start(bf16[2,1168,128]{2,1,0:T(8,128)(2,1)S(1)} %get-tuple-element.57), channel_id=1, source_target_pairs={{0,256},{256,0},{1,257},{257,1},{2,258},{258,2},{3,259},{259,3},{4... | collective-permute-start | bytes 1794056 | tf_op jit(solution)/shard_map/ppermute | solution.py:22
  27.8 12.7 %all-to-all-start = ((s32[16,4,128]{2,1,0:T(4,128)}), s32[16,4,128]{2,1,0:T(4,128)S(1)}, u32[]{:S(2)}, u32[]{:S(2)}) async-start(s32[16,4,128]{2,1,0:T(4,128)} %broadcast_in_dim.48), calls=%async_computation | async-start | bytes 65536 | tf_op jit(solution)/shard_map/all_to_all | solution.py:415
  41.2 11.0 %all-to-all-done = s32[16,4,128]{2,1,0:T(4,128)S(1)} async-done(((s32[16,4,128]{2,1,0:T(4,128)}), s32[16,4,128]{2,1,0:T(4,128)S(1)}, u32[]{:S(2)}, u32[]{:S(2)}) %all-to-all-start) | async-done | bytes 32800 | tf_op jit(solution)/shard_map/all_to_all | solution.py:415
  52.5 3.1 collective-permute-start.5
  58.4 5.2 %collective-permute-done.5 = bf16[2,1168,128]{2,1,0:T(8,128)(2,1)S(1)} collective-permute-done((bf16[2,1168,128]{2,1,0:T(8,128)(2,1)S(1)}, bf16[2,1168,128]{2,1,0:T(8,128)(2,1)S(1)}, u32[]{:S(2)}, u32[]{:S(2)}) %collective-permute-start.5) | collective-permute-done | bytes 598048 | tf_op jit(solution)/shard_map/ppermute | solution.py:28
  65.4 6.3 %collective-permute-start.6 = (bf16[4,2,1168,128]{3,2,1,0:T(8,128)(2,1)}, bf16[4,2,1168,128]{3,2,1,0:T(8,128)(2,1)}, u32[]{:S(2)}, u32[]{:S(2)}) collective-permute-start(bf16[4,2,1168,128]{3,2,1,0:T(8,128)(2,1)} %pad_maximum_fusion), channel_id=1, source_target_pairs={{0,256},{256,0},{1,257},{257,1},{2,258},{258,2},{3,259},{259,3},{4... | collective-permute-start | bytes 7176200 | tf_op jit(solution)/shard_map/ppermute | solution.py:22
  83.9 5.6 %all-gather.3.cloned.1.call-done = bf16[2048,1152]{1,0:T(8,128)(2,1)} async-done(((bf16[128,1152]{1,0:T(8,128)(2,1)}), bf16[2048,1152]{1,0:T(8,128)(2,1)}) %all-gather.3.cloned.1.call-update) | async-done | bytes 4718608 | tf_op jit(solution)/shard_map/all_gather | solution.py:409
  89.5 7.1 %shard_map.102 = bf16[4,16,64,128]{3,2,1,0:T(8,128)(2,1)} custom-call(s32[8]{0:T(128)} %compare_select_fusion.6.refs_0_.order, bf16[4,256,512]{2,1,0:T(8,128)(2,1)} %fusion.1.refs_1_.pick, bf16[4,512,1152]{2,1,0:T(8,128)(2,1)} %bitcast.55, bf16[8,1168,128]{2,1,0:T(8,128)(2,1)} %bitcast.19.refs_3_, bf16[8,1168,128]{2,1,0:T(8,128)(2,1)} %bitcast.20.refs_4_), custom_call_target="tpu_custom_call" | custom-call | flops 1207959552 | bytes 12000000 | tf_op jit(solution)/shard_map/pallas_call | solution.py:145
  96.6 4.1 %all-to-all-start.1 = ((bf16[4,16,64,128]{3,2,1,0:T(8,128)(2,1)}), bf16[4,16,64,128]{3,2,1,0:T(8,128)(2,1)S(1)}, u32[]{:S(2)}, u32[]{:S(2)}) async-start(bf16[4,16,64,128]{3,2,1,0:T(8,128)(2,1)} %shard_map.102), calls=%async_computation.1 | async-start | bytes 2097152 | tf_op jit(solution)/shard_map/all_to_all | solution.py:444
  100.7 9.7 %all-to-all-done.1.copies = bf16[4,16,64,128]{3,2,1,0:T(8,128)(2,1)S(1)} async-done(((bf16[4,16,64,128]{3,2,1,0:T(8,128)(2,1)}), bf16[4,16,64,128]{3,2,1,0:T(8,128)(2,1)S(1)}, u32[]{:S(2)}, u32[]{:S(2)}) %all-to-all-start.1) | async-done | bytes 1048608 | tf_op jit(solution)/shard_map/all_to_all | solution.py:444
  111.4 8.0 %shard_map.103 = (f32[16,64,128]{2,1,0:T(8,128)}, bf16[16,64,128]{2,1,0:T(8,128)(2,1)}, bf16[4,512,1152]{2,1,0:T(8,128)(2,1)}) custom-call(s32[8]{0:T(128)} %compare_select_fusion.6.refs_0_.order, bf16[4,16,64,128]{3,2,1,0:T(8,128)(2,1)} %copy-done.4, f32[16,1,128]{2,1,0:T(1,128)} %bitcast.74, bf16[4,512,256]{2,1,0:T(8,128)(2,1)} %compare_convert_fusion.turned, ...), custom_call_target="tpu_custom_call" | custom-call | flops 1207959552 | bytes 12000000 | tf_op jit(solution)/shard_map/pallas_call | solution.py:145
  119.4 5.9 %shard_map.104 = bf16[16,64,1152]{2,1,0:T(8,128)(2,1)} custom-call(bf16[4,256,512]{2,1,0:T(8,128)(2,1)} %fusion.1.refs_1_.pick, bf16[4,512,1152]{2,1,0:T(8,128)(2,1)} %bitcast.56), custom_call_target="tpu_custom_call" | custom-call | flops 1207959552 | bytes 8000000 | tf_op jit(solution)/shard_map/pallas_call | solution.py:104
  125.3 13.5 %all-to-all-start.2 = ((bf16[8,2,64,1152]{3,2,1,0:T(8,128)(2,1)}), bf16[8,2,64,1152]{3,2,1,0:T(8,128)(2,1)}, u32[]{:S(2)}, u32[]{:S(2)}) async-start(bf16[8,2,64,1152]{3,2,1,0:T(8,128)(2,1)} %bitcast.59), calls=%async_computation.3 | async-start | bytes 4718592 | tf_op jit(solution)/shard_map/all_to_all | solution.py:404
  138.7 2.6 copy.51
  141.3 4.3 %copy.52 = bf16[4,2,128,1152]{2,3,1,0:T(8,128)(2,1)} copy(bf16[4,2,128,1152]{3,2,1,0:T(8,128)(2,1)} %collective-permute-done.7) | data formatting | bytes 4718592 | tf_op jit(solution)/shard_map/ppermute | solution.py:22
  145.7 22.2 %all-to-all-done.2.rows = bf16[8,2,64,1152]{3,2,1,0:T(8,128)(2,1)} async-done(((bf16[8,2,64,1152]{3,2,1,0:T(8,128)(2,1)}), bf16[8,2,64,1152]{3,2,1,0:T(8,128)(2,1)}, u32[]{:S(2)}, u32[]{:S(2)}) %all-to-all-start.2) | async-done | bytes 2359328 | tf_op jit(solution)/shard_map/all_to_all | solution.py:404
  167.9 26.1 %reduce-scatter.2.cloned.1.call-done = bf16[128,1152]{1,0:T(8,128)(2,1)} async-done(((bf16[2048,1152]{1,0:T(8,128)(2,1)}), bf16[128,1152]{1,0:T(8,128)(2,1)}) %reduce-scatter.2.cloned.1.call-update) | async-done | bytes 294928 | tf_op jit(solution)/shard_map/reduce_scatter | solution.py:447
  195.8 13.6 %all-to-all-start.3 = ((bf16[8,2,64,128]{3,2,1,0:T(8,128)(2,1)}), bf16[8,2,64,128]{3,2,1,0:T(8,128)(2,1)S(1)}, u32[]{:S(2)}, u32[]{:S(2)}) async-start(bf16[8,2,64,128]{3,2,1,0:T(8,128)(2,1)} %bitcast.33), calls=%async_computation.4 | async-start | bytes 524288 | tf_op jit(solution)/shard_map/all_to_all | solution.py:404
  209.7 6.4 %all-to-all-done.3.values = bf16[8,2,64,128]{3,2,1,0:T(8,128)(2,1)S(1)} async-done(((bf16[8,2,64,128]{3,2,1,0:T(8,128)(2,1)}), bf16[8,2,64,128]{3,2,1,0:T(8,128)(2,1)S(1)}, u32[]{:S(2)}, u32[]{:S(2)}) %all-to-all-start.3) | async-done | bytes 262176 | tf_op jit(solution)/shard_map/all_to_all | solution.py:404
  216.0 59.7 %all-gather.5.cloned.1.call-done = bf16[2048,1152]{1,0:T(8,128)(2,1)} async-done(((bf16[128,1152]{1,0:T(8,128)(2,1)}), bf16[2048,1152]{1,0:T(8,128)(2,1)}) %all-gather.5.cloned.1.call-update) | async-done | bytes 4718608 | tf_op jit(solution)/shard_map/all_gather | solution.py:409
  275.8 4.9 %shard_map.105.slots = bf16[16,64,1152]{2,1,0:T(8,128)(2,1)} custom-call(bf16[4,256,512]{2,1,0:T(8,128)(2,1)} %fusion.1.refs_1_.pick, bf16[4,512,1152]{2,1,0:T(8,128)(2,1)} %bitcast.62), custom_call_target="tpu_custom_call" | custom-call | flops 1207959552 | bytes 8000000 | tf_op jit(solution)/shard_map/pallas_call | solution.py:145
  280.7 12.6 %all-to-all-start.4 = ((bf16[8,2,64,1152]{3,2,1,0:T(8,128)(2,1)}), bf16[8,2,64,1152]{3,2,1,0:T(8,128)(2,1)S(1)}, u32[]{:S(2)}, u32[]{:S(2)}) async-start(bf16[8,2,64,1152]{3,2,1,0:T(8,128)(2,1)} %bitcast.54), calls=%async_computation.5 | async-start | bytes 4718592 | tf_op jit(solution)/shard_map/all_to_all | solution.py:404
  293.3 5.7 %shard_map.106.a = bf16[16,64,128]{2,1,0:T(8,128)(2,1)} custom-call(s32[8]{0:T(128)} %compare_select_fusion.6.refs_0_.order, bf16[16,64,1152]{2,1,0:T(8,128)(2,1)} %shard_map.105.slots, bf16[8,1152,128]{2,1,0:T(8,128)(2,1)} %bitcast.57, bf16[8,1152,128]{2,1,0:T(8,128)(2,1)} %bitcast.58), custom_call_target="tpu_custom_call" | custom-call | flops 301989888 | bytes 8000000 | tf_op jit(solution)/shard_map/pallas_call | solution.py:145
  299.1 3.1 collective-permute-start.8
  302.2 4.4 %collective-permute-start.9 = (bf16[16,64,128]{2,1,0:T(8,128)(2,1)}, bf16[16,64,128]{2,1,0:T(8,128)(2,1)S(1)}, u32[]{:S(2)}, u32[]{:S(2)}) collective-permute-start(bf16[16,64,128]{2,1,0:T(8,128)(2,1)} %shard_map.106.a), channel_id=1, source_target_pairs={{0,2},{1,3},{2,0},{3,1},{4,6},{5,7},{6,4},{7,5},{8,10},{9,11},{10,... | collective-permute-start | bytes 786440 | tf_op jit(solution)/shard_map/ppermute | solution.py:338
  306.6 3.0 collective-permute-start.10
  310.3 6.6 %collective-permute-done.9.c = bf16[16,64,128]{2,1,0:T(8,128)(2,1)S(1)} collective-permute-done((bf16[16,64,128]{2,1,0:T(8,128)(2,1)}, bf16[16,64,128]{2,1,0:T(8,128)(2,1)S(1)}, u32[]{:S(2)}, u32[]{:S(2)}) %collective-permute-start.9) | collective-permute-done | bytes 262176 | tf_op jit(solution)/shard_map/ppermute | solution.py:338
  319.9 2.4 all-to-all-done.4.rows
  322.4 3.7 %all-to-all-start.5 = ((bf16[8,2,64,128]{3,2,1,0:T(8,128)(2,1)}), bf16[8,2,64,128]{3,2,1,0:T(8,128)(2,1)S(1)}, u32[]{:S(2)}, u32[]{:S(2)}) async-start(bf16[8,2,64,128]{3,2,1,0:T(8,128)(2,1)} %bitcast.36), calls=%async_computation.6 | async-start | bytes 524288 | tf_op jit(solution)/shard_map/all_to_all | solution.py:404
  326.1 3.1 shard_map.109
  329.2 3.4 all-to-all-done.5.values
  333.3 3.1 shard_map.108
  (86 shorter events, 36.8 us)
Async XLA Ops:
  7.2 11.8 %copy-start.5 = (bf16[2,128,1152]{2,1,0:T(8,128)(2,1)S(1)}, bf16[2,128,1152]{2,1,0:T(8,128)(2,1)}, u32[]{:S(2)}) copy-start(bf16[2,128,1152]{2,1,0:T(8,128)(2,1)} %param.12) | copy-start | bytes 1769476
  7.2 82.3 %all-gather.3.cloned.1.call-start = ((), (), s32[]{:S(2)}) async-start(), calls=%async_computation.7 | async-start | bytes 5013504 | tf_op jit(solution)/shard_map/all_gather | solution.py:409
  10.2 10.7 %collective-permute-start.3 = (bf16[2,1168,128]{2,1,0:T(8,128)(2,1)S(1)}, bf16[2,1168,128]{2,1,0:T(8,128)(2,1)S(1)}, u32[]{:S(2)}, u32[]{:S(2)}) collective-permute-start(bf16[2,1168,128]{2,1,0:T(8,128)(2,1)S(1)} %get-tuple-element.57), channel_id=1, source_target_pairs={{0,256},{256,0},{1,257},{257,1},{2,258},{258,2},{3,259},{259,3},{4... | collective-permute-start | bytes 1794056 | tf_op jit(solution)/shard_map/ppermute | solution.py:22
  19.0 5.0 %collective-permute-start = (bf16[2,128,1152]{2,1,0:T(8,128)(2,1)S(1)}, bf16[2,128,1152]{2,1,0:T(8,128)(2,1)S(1)}, u32[]{:S(2)}, u32[]{:S(2)}) collective-permute-start(bf16[2,128,1152]{2,1,0:T(8,128)(2,1)S(1)} %copy-done.5), channel_id=1, source_target_pairs={{0,256},{256,0},{1,257},{257,1},{2,258},{258,2},{3,259},{259,3},{4... | collective-permute-start | bytes 1769480 | tf_op jit(solution)/shard_map/ppermute | solution.py:22
  20.9 6.3 %copy-start.13 = (s32[128]{0:T(128)S(1)}, s32[128]{0:T(128)}, u32[]{:S(2)}) copy-start(s32[128]{0:T(128)} %param.8) | copy-start | bytes 1540
  20.9 6.3 %copy-start.12 = (s32[128,4]{0,1:T(4,128)S(1)}, s32[128,4]{0,1:T(4,128)}, u32[]{:S(2)}) copy-start(s32[128,4]{0,1:T(4,128)} %param.9) | copy-start | bytes 6148
  22.1 30.4 %collective-permute-start.4 = (bf16[2,2,1168,128]{3,2,1,0:T(8,128)(2,1)}, bf16[2,2,1168,128]{3,2,1,0:T(8,128)(2,1)S(1)}, u32[]{:S(2)}, u32[]{:S(2)}) collective-permute-start(bf16[2,2,1168,128]{3,2,1,0:T(8,128)(2,1)} %pad_maximum_fusion.2), channel_id=1, source_target_pairs={{0,64},{64,128},{128,192},{192,0},{256,448},{320,256},{384,320},{4... | collective-permute-start | bytes 3588104 | tf_op jit(solution)/shard_map/ppermute | solution.py:28
  25.2 27.2 %collective-permute-start.1 = (bf16[2,2,128,1152]{3,2,1,0:T(8,128)(2,1)}, bf16[2,2,128,1152]{3,2,1,0:T(8,128)(2,1)S(1)}, u32[]{:S(2)}, u32[]{:S(2)}) collective-permute-start(bf16[2,2,128,1152]{3,2,1,0:T(8,128)(2,1)} %pad_maximum_fusion.3), channel_id=1, source_target_pairs={{0,64},{64,128},{128,192},{192,0},{256,448},{320,256},{384,320},{4... | collective-permute-start | bytes 3538952 | tf_op jit(solution)/shard_map/ppermute | solution.py:28
  27.8 24.4 %all-to-all-start = ((s32[16,4,128]{2,1,0:T(4,128)}), s32[16,4,128]{2,1,0:T(4,128)S(1)}, u32[]{:S(2)}, u32[]{:S(2)}) async-start(s32[16,4,128]{2,1,0:T(4,128)} %broadcast_in_dim.48), calls=%async_computation | async-start | bytes 65536 | tf_op jit(solution)/shard_map/all_to_all | solution.py:415
  52.5 11.1 %collective-permute-start.5 = (bf16[2,1168,128]{2,1,0:T(8,128)(2,1)S(1)}, bf16[2,1168,128]{2,1,0:T(8,128)(2,1)S(1)}, u32[]{:S(2)}, u32[]{:S(2)}) collective-permute-start(bf16[2,1168,128]{2,1,0:T(8,128)(2,1)S(1)} %slice_bitcast_fusion), channel_id=1, source_target_pairs={{0,64},{64,128},{128,192},{192,0},{256,448},{320,256},{384,320},{4... | collective-permute-start | bytes 1794056 | tf_op jit(solution)/shard_map/ppermute | solution.py:28
  56.5 21.9 %collective-permute-start.2 = (bf16[2,128,1152]{2,1,0:T(8,128)(2,1)}, bf16[2,128,1152]{2,1,0:T(8,128)(2,1)}, u32[]{:S(2)}, u32[]{:S(2)}) collective-permute-start(bf16[2,128,1152]{2,1,0:T(8,128)(2,1)} %slice_bitcast_fusion.1), channel_id=1, source_target_pairs={{0,64},{64,128},{128,192},{192,0},{256,448},{320,256},{384,320},{4... | collective-permute-start | bytes 1769480 | tf_op jit(solution)/shard_map/ppermute | solution.py:28
  65.4 17.1 %collective-permute-start.6 = (bf16[4,2,1168,128]{3,2,1,0:T(8,128)(2,1)}, bf16[4,2,1168,128]{3,2,1,0:T(8,128)(2,1)}, u32[]{:S(2)}, u32[]{:S(2)}) collective-permute-start(bf16[4,2,1168,128]{3,2,1,0:T(8,128)(2,1)} %pad_maximum_fusion), channel_id=1, source_target_pairs={{0,256},{256,0},{1,257},{257,1},{2,258},{258,2},{3,259},{259,3},{4... | collective-permute-start | bytes 7176200 | tf_op jit(solution)/shard_map/ppermute | solution.py:22
  77.2 1.2 copy-start.6
  79.8 16.8 %copy-start.1 = (bf16[4,2,128,1152]{3,2,1,0:T(8,128)(2,1)}, bf16[4,2,128,1152]{3,2,1,0:T(8,128)(2,1)S(1)}, u32[]{:S(2)}) copy-start(bf16[4,2,128,1152]{3,2,1,0:T(8,128)(2,1)S(1)} %pad_maximum_fusion.1) | copy-start | bytes 7077892
  79.8 20.8 %collective-permute-start.7 = (bf16[4,2,128,1152]{3,2,1,0:T(8,128)(2,1)S(1)}, bf16[4,2,128,1152]{3,2,1,0:T(8,128)(2,1)}, u32[]{:S(2)}, u32[]{:S(2)}) collective-permute-start(bf16[4,2,128,1152]{3,2,1,0:T(8,128)(2,1)S(1)} %pad_maximum_fusion.1), channel_id=1, source_target_pairs={{0,256},{256,0},{1,257},{257,1},{2,258},{258,2},{3,259},{259,3},{4... | collective-permute-start | bytes 7077896 | tf_op jit(solution)/shard_map/ppermute | solution.py:22
  96.6 13.8 %all-to-all-start.1 = ((bf16[4,16,64,128]{3,2,1,0:T(8,128)(2,1)}), bf16[4,16,64,128]{3,2,1,0:T(8,128)(2,1)S(1)}, u32[]{:S(2)}, u32[]{:S(2)}) async-start(bf16[4,16,64,128]{3,2,1,0:T(8,128)(2,1)} %shard_map.102), calls=%async_computation.1 | async-start | bytes 2097152 | tf_op jit(solution)/shard_map/all_to_all | solution.py:444
  100.6 93.3 %reduce-scatter.2.cloned.1.call-start = ((), (), s32[]{:S(2)}) async-start(), calls=%async_computation.8 | async-start | bytes 5013504 | tf_op jit(solution)/shard_map/reduce_scatter | solution.py:447
  110.4 1.0 copy-start.4
  125.2 13.5 %copy-start.2 = (bf16[4,2,128,1152]{3,2,1,0:T(8,128)(2,1)S(1)}, bf16[4,2,128,1152]{3,2,1,0:T(8,128)(2,1)}, u32[]{:S(2)}) copy-start(bf16[4,2,128,1152]{3,2,1,0:T(8,128)(2,1)} %copy-done.1) | copy-start | bytes 7077892
  125.3 42.6 %all-to-all-start.2 = ((bf16[8,2,64,1152]{3,2,1,0:T(8,128)(2,1)}), bf16[8,2,64,1152]{3,2,1,0:T(8,128)(2,1)}, u32[]{:S(2)}, u32[]{:S(2)}) async-start(bf16[8,2,64,1152]{3,2,1,0:T(8,128)(2,1)} %bitcast.59), calls=%async_computation.3 | async-start | bytes 4718592 | tf_op jit(solution)/shard_map/all_to_all | solution.py:404
  138.7 137.1 %all-gather.5.cloned.1.call-start = ((), (), s32[]{:S(2)}) async-start(), calls=%async_computation.9 | async-start | bytes 5013504 | tf_op jit(solution)/shard_map/all_gather | solution.py:409
  141.3 52.6 %copy-start.7 = (bf16[128,1152]{1,0:T(8,128)(2,1)S(1)}, bf16[128,1152]{1,0:T(8,128)(2,1)}, u32[]{:S(2)}) copy-start(bf16[128,1152]{1,0:T(8,128)(2,1)} %param.7) | copy-start | bytes 884740
  141.3 52.6 %copy-start.11 = (f32[1152]{0:T(1024)S(1)}, f32[1152]{0:T(1024)}, u32[]{:S(2)}) copy-start(f32[1152]{0:T(1024)} %param.13) | copy-start | bytes 13828
  145.7 63.8 %copy-start.10 = (f32[16,64,128]{2,1,0:T(8,128)S(1)}, f32[16,64,128]{2,1,0:T(8,128)}, u32[]{:S(2)}) copy-start(f32[16,64,128]{2,1,0:T(8,128)} %get-tuple-element.43) | copy-start | bytes 1572868
  195.8 20.2 %all-to-all-start.3 = ((bf16[8,2,64,128]{3,2,1,0:T(8,128)(2,1)}), bf16[8,2,64,128]{3,2,1,0:T(8,128)(2,1)S(1)}, u32[]{:S(2)}, u32[]{:S(2)}) async-start(bf16[8,2,64,128]{3,2,1,0:T(8,128)(2,1)} %bitcast.33), calls=%async_computation.4 | async-start | bytes 524288 | tf_op jit(solution)/shard_map/all_to_all | solution.py:404
  216.0 64.6 %copy-start.8 = (bf16[8,2,64,128]{3,2,1,0:T(8,128)(2,1)}, bf16[8,2,64,128]{3,2,1,0:T(8,128)(2,1)S(1)}, u32[]{:S(2)}) copy-start(bf16[8,2,64,128]{3,2,1,0:T(8,128)(2,1)S(1)} %all-to-all-done.3.values) | copy-start | bytes 786436
  280.7 41.7 %all-to-all-start.4 = ((bf16[8,2,64,1152]{3,2,1,0:T(8,128)(2,1)}), bf16[8,2,64,1152]{3,2,1,0:T(8,128)(2,1)S(1)}, u32[]{:S(2)}, u32[]{:S(2)}) async-start(bf16[8,2,64,1152]{3,2,1,0:T(8,128)(2,1)} %bitcast.54), calls=%async_computation.5 | async-start | bytes 4718592 | tf_op jit(solution)/shard_map/all_to_all | solution.py:404
  299.1 11.2 %collective-permute-start.8 = (bf16[16,64,128]{2,1,0:T(8,128)(2,1)}, bf16[16,64,128]{2,1,0:T(8,128)(2,1)S(1)}, u32[]{:S(2)}, u32[]{:S(2)}) collective-permute-start(bf16[16,64,128]{2,1,0:T(8,128)(2,1)} %shard_map.106.a), channel_id=1, source_target_pairs={{0,1},{1,2},{2,3},{3,0},{4,5},{5,6},{6,7},{7,4},{8,9},{9,10},{10,1... | collective-permute-start | bytes 786440 | tf_op jit(solution)/shard_map/ppermute | solution.py:338
  302.2 14.8 %collective-permute-start.9 = (bf16[16,64,128]{2,1,0:T(8,128)(2,1)}, bf16[16,64,128]{2,1,0:T(8,128)(2,1)S(1)}, u32[]{:S(2)}, u32[]{:S(2)}) collective-permute-start(bf16[16,64,128]{2,1,0:T(8,128)(2,1)} %shard_map.106.a), channel_id=1, source_target_pairs={{0,2},{1,3},{2,0},{3,1},{4,6},{5,7},{6,4},{7,5},{8,10},{9,11},{10,... | collective-permute-start | bytes 786440 | tf_op jit(solution)/shard_map/ppermute | solution.py:338
  306.6 11.5 %collective-permute-start.10 = (bf16[16,64,128]{2,1,0:T(8,128)(2,1)}, bf16[16,64,128]{2,1,0:T(8,128)(2,1)S(1)}, u32[]{:S(2)}, u32[]{:S(2)}) collective-permute-start(bf16[16,64,128]{2,1,0:T(8,128)(2,1)} %shard_map.106.a), channel_id=1, source_target_pairs={{0,3},{1,0},{2,1},{3,2},{4,7},{5,4},{6,5},{7,6},{8,11},{9,8},{10,9... | collective-permute-start | bytes 786440 | tf_op jit(solution)/shard_map/ppermute | solution.py:338
  322.4 3.7 %copy-start.3 = (bf16[8,2,64,1152]{3,2,1,0:T(8,128)(2,1)}, bf16[8,2,64,1152]{3,2,1,0:T(8,128)(2,1)S(1)}, u32[]{:S(2)}) copy-start(bf16[8,2,64,1152]{3,2,1,0:T(8,128)(2,1)S(1)} %all-to-all-done.4.rows) | copy-start | bytes 7077892
  322.4 10.3 %all-to-all-start.5 = ((bf16[8,2,64,128]{3,2,1,0:T(8,128)(2,1)}), bf16[8,2,64,128]{3,2,1,0:T(8,128)(2,1)S(1)}, u32[]{:S(2)}, u32[]{:S(2)}) async-start(bf16[8,2,64,128]{3,2,1,0:T(8,128)(2,1)} %bitcast.36), calls=%async_computation.6 | async-start | bytes 524288 | tf_op jit(solution)/shard_map/all_to_all | solution.py:404
  (2 other events, 1.7 us)
Sparse Core Ops, SparseCore 0:
  10.1 79.3 all-gather.2
  119.5 74.3 reduce-scatter.1
  196.6 79.1 all-gather.4
